TPU v7x, 32 devices: a whole 2x2x4 slice. The times are simulated.
32 devices in a mesh: fsdp: 8 (over z, y), tensor: 4 (over x, core).
Axes of the slice: x: 2, y: 2, z: 4, core: 2. Of those that a mesh axis runs over, the one named last changes fastest.
Arguments:
- layer_in: bfloat16 [16384, 1152], P(('fsdp', 'tensor')), may hold values from -6 to 6
- teacher: bfloat16 [16384, 1152], P(('fsdp', 'tensor')), may hold values from -8 to 8
- query_proj: bfloat16 [1152, 1024], P('fsdp', 'tensor'), may hold values from -0.1875 to 0.1875
- key_proj: bfloat16 [1152, 256], P(('fsdp', 'tensor')), may hold values from -0.1875 to 0.1875
- value_proj: bfloat16 [1152, 256], P(('fsdp', 'tensor')), may hold values from -0.1875 to 0.1875
- out_proj: bfloat16 [1024, 1152], P('tensor', 'fsdp'), may hold values from -0.1875 to 0.1875
- gate_proj: bfloat16 [1152, 6912], P('fsdp', 'tensor'), may hold values from -0.1875 to 0.1875
- up_proj: bfloat16 [1152, 6912], P('fsdp', 'tensor'), may hold values from -0.1875 to 0.1875
- down_proj: bfloat16 [6912, 1152], P('tensor', 'fsdp'), may hold values from -0.078125 to 0.078125
- attn_norm: bfloat16 [1152], P(('fsdp', 'tensor')), may hold values from -0.3984375 to 0.59765625
- attn_post: bfloat16 [1152], P(('fsdp', 'tensor')), may hold values from -0.3984375 to 0.59765625
- ffw_norm: bfloat16 [1152], P(('fsdp', 'tensor')), may hold values from -0.3984375 to 0.59765625
- ffw_post: bfloat16 [1152], P(('fsdp', 'tensor')), may hold values from -0.3984375 to 0.59765625
- query_norm: bfloat16 [256], P(('fsdp', 'tensor')), may hold values from -0.3984375 to 0.59765625
- key_norm: bfloat16 [256], P(('fsdp', 'tensor')), may hold values from -0.3984375 to 0.59765625
- cont_prompt: int32 [32], P('fsdp'), may hold values from 0 to 3
- cont_length: int32 [32], P('fsdp'), may hold values from 128 to 256, as said below
- token_count: int32 [], replicated, may hold values from 8192 to 16384
- loss_scale: float32 [], replicated, may hold values from 4096 to 16384
Outputs:
- layer_out: bfloat16 [16384, 1152], P(('fsdp', 'tensor'))
- loss: float32 [], replicated
- grad_in: bfloat16 [16384, 1152], P(('fsdp', 'tensor'))
- grad_query: float32 [1152, 1024], P('fsdp', 'tensor')
- grad_key: float32 [1152, 256], P(('fsdp', 'tensor'))
- grad_value: float32 [1152, 256], P(('fsdp', 'tensor'))
- grad_out: float32 [1024, 1152], P('tensor', 'fsdp')
- grad_gate: float32 [1152, 6912], P('fsdp', 'tensor')
- grad_up: float32 [1152, 6912], P('fsdp', 'tensor')
- grad_down: float32 [6912, 1152], P('tensor', 'fsdp')
- grad_attn_norm: float32 [1152], P(('fsdp', 'tensor'))
- grad_attn_post: float32 [1152], P(('fsdp', 'tensor'))
- grad_ffw_norm: float32 [1152], P(('fsdp', 'tensor'))
- grad_ffw_post: float32 [1152], P(('fsdp', 'tensor'))
- grad_query_norm: float32 [256], P(('fsdp', 'tensor'))
- grad_key_norm: float32 [256], P(('fsdp', 'tensor'))
Inputs may be any that keep to these rules, and one draw needn't show every extreme that they name: `cont_prompt`: each continuation follows one of the 4 prompts of its own group of 8 fsdp indices. `cont_length`: rows of a continuation from this length on are padding.
All inputs are finite; a program needn't handle non-finite values.
Results may differ from a plain program's by a relative error of at most 0.025.
Values may be sent and summed in bfloat16 or wider, within the bound.
No kernel may reach another device: no remote copies, remote signals or barrier semaphores. Data moves between devices by JAX's collectives and lax.ppermute only.
A program may use at most 256 MiB of HBM per device.

v0:
```python
import math

import jax
import jax.numpy as jnp
from jax import lax
from jax.sharding import PartitionSpec as P

HEAD = 256
PROMPT = 2048
CONT = 256
GROUP = 8
GROUPS_DEV = 4
PSLICE = 256
ROWS_F = 2048


eps_norm = 1e-06
rope_base = 1000000.0
masked_score = -1e30


def partner_2(value, axis, stride):
    mask = 2**stride
    pairs = [(source, source ^ mask) for source in range(lax.axis_size(axis))]
    return lax.ppermute(value, axis, pairs)


def rms_scale(tensor_in, gain_vec):
    return (
        tensor_in
        * lax.rsqrt(jnp.mean(tensor_in * tensor_in, axis=-1, keepdims=True) + eps_norm)
        * (1.0 + gain_vec)
    )


def rotate(tensor_in, angles):
    half_dim = tensor_in.shape[-1] // 2
    first_half = tensor_in[..., :half_dim]
    second_half = tensor_in[..., half_dim:]
    cosine = jnp.cos(angles)
    sine_part = jnp.sin(angles)
    return jnp.concatenate(
        [
            first_half * cosine - second_half * sine_part,
            second_half * cosine + first_half * sine_part,
        ],
        axis=-1,
    )


def inverse_freq():
    return jnp.exp(-math.log(rope_base) * 2.0 * jnp.arange(HEAD // 2, dtype=jnp.float32) / HEAD)


def head_prep(raw_in, gain_vec, angles):
    return rotate(rms_scale(raw_in, gain_vec), angles)


def contract_rows(left_side, right_side):
    return lax.dot_general(
        left_side, right_side, (((0,), (0,)), ((), ())), preferred_element_type=jnp.float32
    )


def contract_cols(left_side, right_side):
    return lax.dot_general(
        left_side, right_side, (((1,), (1,)), ((), ())), preferred_element_type=jnp.float32
    )


def prompt_mask(slice_pos):
    shape_qk = (PSLICE, PROMPT)
    query_ids = lax.broadcasted_iota(jnp.int32, shape_qk, 0)
    key_ids = lax.broadcasted_iota(jnp.int32, shape_qk, 1)
    return key_ids <= slice_pos * PSLICE + query_ids


def cont_mask(length):
    shape_qk = (CONT, PROMPT + CONT)
    query_ids = lax.broadcasted_iota(jnp.int32, shape_qk, 0)
    key_ids = lax.broadcasted_iota(jnp.int32, shape_qk, 1)
    cont_key = key_ids - PROMPT
    return (key_ids < PROMPT) | (cont_key >= 0) & (cont_key <= query_ids) & (cont_key < length)


def attend_block(query_blk, keys_blk, values_blk, key_mask, score_scale):
    scores = jnp.where(key_mask, contract_cols(query_blk, keys_blk) * score_scale, masked_score)
    row_max = jnp.max(scores, axis=-1, keepdims=True)
    shifted = jnp.exp(scores - row_max)
    row_sum = jnp.sum(shifted, axis=-1, keepdims=True)
    row_probs = shifted / row_sum
    output = jnp.dot(row_probs.astype(jnp.bfloat16), values_blk, preferred_element_type=jnp.float32)
    return (output, row_max + jnp.log(row_sum))


def attend_back(query_blk, keys_blk, values_blk, key_mask, log_sum, grad_blk, score_scale):
    scores = jnp.where(key_mask, contract_cols(query_blk, keys_blk) * score_scale, masked_score)
    row_probs = jnp.exp(scores - log_sum)
    grad_probs = contract_cols(grad_blk, values_blk)
    row_dot = jnp.sum(row_probs * grad_probs, axis=-1, keepdims=True)
    grad_scores = (row_probs * (grad_probs - row_dot)).astype(jnp.bfloat16)
    grad_query_blk = (
        jnp.dot(grad_scores, keys_blk, preferred_element_type=jnp.float32) * score_scale
    )
    grad_keys_blk = contract_rows(grad_scores, query_blk) * score_scale
    grad_values_blk = contract_rows(row_probs.astype(jnp.bfloat16), grad_blk)
    return (grad_query_blk, jnp.concatenate([grad_keys_blk, grad_values_blk], 1))


def spread_rows(tensor_in):
    return lax.all_gather(tensor_in, "tensor", axis=0, tiled=True)


def collect_rows(tensor_in):
    return lax.psum_scatter(
        tensor_in.astype(jnp.bfloat16), "tensor", scatter_dimension=0, tiled=True
    ).astype(jnp.float32)


def spread_grads(tensor_in):
    return lax.all_gather(tensor_in, "tensor", axis=0, tiled=True)


def collect_grads(tensor_in):
    return lax.psum_scatter(
        tensor_in.astype(jnp.bfloat16), "tensor", scatter_dimension=0, tiled=True
    ).astype(jnp.float32)


def local(
    layer_in,
    teacher,
    query_proj,
    key_proj,
    value_proj,
    out_proj,
    gate_proj,
    up_proj,
    down_proj,
    attn_norm,
    attn_post,
    ffw_norm,
    ffw_post,
    query_norm,
    key_norm,
    cont_prompt,
    cont_length,
    token_count,
    loss_scale,
):
    fsdp_pos = lax.axis_index("fsdp")
    tensor_pos = lax.axis_index("tensor")
    local_rows = layer_in.shape[0]
    prompt_part = GROUPS_DEV * PSLICE
    score_scale = 1.0 / math.sqrt(HEAD)
    small_full = (
        lax.all_gather(key_proj, ("fsdp", "tensor"), axis=0, tiled=True),
        lax.all_gather(value_proj, ("fsdp", "tensor"), axis=0, tiled=True),
        lax.all_gather(attn_norm, ("fsdp", "tensor"), axis=0, tiled=True),
        lax.all_gather(attn_post, ("fsdp", "tensor"), axis=0, tiled=True),
        lax.all_gather(ffw_norm, ("fsdp", "tensor"), axis=0, tiled=True),
        lax.all_gather(ffw_post, ("fsdp", "tensor"), axis=0, tiled=True),
        lax.all_gather(query_norm, ("fsdp", "tensor"), axis=0, tiled=True),
        lax.all_gather(key_norm, ("fsdp", "tensor"), axis=0, tiled=True),
    )
    key_full = small_full[0]
    value_full = small_full[1]
    attn_gain = small_full[2].astype(jnp.float32)
    attn_post_gain = small_full[3].astype(jnp.float32)
    ffw_gain = small_full[4].astype(jnp.float32)
    ffw_post_gain = small_full[5].astype(jnp.float32)
    query_gain = small_full[6].astype(jnp.float32)
    key_gain = small_full[7].astype(jnp.float32)
    query_full, out_full = (
        lax.all_gather(query_proj, "fsdp", axis=0, tiled=True),
        lax.all_gather(out_proj, "fsdp", axis=1, tiled=True),
    )
    row_ids = jnp.arange(ROWS_F, dtype=jnp.int32)
    group_slot = fsdp_pos % GROUP
    positions = jnp.where(
        row_ids < prompt_part,
        group_slot * PSLICE + row_ids % PSLICE,
        PROMPT + (row_ids - prompt_part) % CONT,
    )
    angles = positions.astype(jnp.float32)[:, None] * inverse_freq()[None, :]
    input_f = layer_in.astype(jnp.float32)
    normed_in = rms_scale(input_f, attn_gain).astype(jnp.bfloat16)
    normed_all = spread_rows(normed_in)
    query_raw = jnp.dot(normed_all, query_full, preferred_element_type=jnp.float32)
    key_raw = jnp.dot(normed_all, key_full, preferred_element_type=jnp.float32)
    value_raw = jnp.dot(normed_all, value_full, preferred_element_type=jnp.float32)
    query_rot = head_prep(query_raw, query_gain, angles).astype(jnp.bfloat16)
    key_rot = head_prep(key_raw, key_gain, angles).astype(jnp.bfloat16)
    pair_rows = jnp.concatenate([key_rot, value_raw.astype(jnp.bfloat16)], axis=1)
    prompt_pairs = pair_rows[:prompt_part].reshape(GROUPS_DEV, PSLICE, 2 * HEAD).transpose(1, 0, 2)
    level_count = GROUP.bit_length() - 1
    held_rows = prompt_pairs
    for bit_level in range(level_count):
        partner = partner_2(held_rows, "fsdp", bit_level)
        upper_half = fsdp_pos // 2**bit_level % 2 == 1
        held_rows = jnp.where(
            upper_half,
            jnp.concatenate([partner, held_rows], 0),
            jnp.concatenate([held_rows, partner], 0),
        )
    cont_pairs = pair_rows[prompt_part:]
    the_prompt_mask = prompt_mask(group_slot)
    kept_cont_keys = []
    kept_prompt_sums = []
    kept_cont_sums = []
    prompt_outs = []
    cont_outs = []
    for slot_number in range(GROUPS_DEV):
        query_prompt = query_rot[slot_number * PSLICE : (slot_number + 1) * PSLICE]
        query_cont = query_rot[
            prompt_part + slot_number * CONT : prompt_part + (slot_number + 1) * CONT
        ]
        own_pairs = held_rows[:, slot_number]
        mapped_pairs = lax.dynamic_index_in_dim(
            held_rows, cont_prompt[slot_number], 1, keepdims=False
        )
        cont_keys = jnp.concatenate(
            [mapped_pairs, cont_pairs[slot_number * CONT : (slot_number + 1) * CONT]], 0
        )
        prompt_out, prompt_sum = attend_block(
            query_prompt, own_pairs[:, :HEAD], own_pairs[:, HEAD:], the_prompt_mask, score_scale
        )
        cont_out, cont_sum = attend_block(
            query_cont,
            cont_keys[:, :HEAD],
            cont_keys[:, HEAD:],
            cont_mask(cont_length[slot_number]),
            score_scale,
        )
        kept_cont_keys.append(cont_keys)
        kept_prompt_sums.append(prompt_sum)
        kept_cont_sums.append(cont_sum)
        prompt_outs.append(prompt_out)
        cont_outs.append(cont_out)
    attn_low = jnp.concatenate(prompt_outs + cont_outs, 0).astype(jnp.bfloat16)
    attn_sum = collect_rows(jnp.dot(attn_low, out_full, preferred_element_type=jnp.float32))
    mixed = input_f + rms_scale(attn_sum, attn_post_gain)
    gate_full, up_full, down_full = (
        lax.all_gather(gate_proj, "fsdp", axis=0, tiled=True),
        lax.all_gather(up_proj, "fsdp", axis=0, tiled=True),
        lax.all_gather(down_proj, "fsdp", axis=1, tiled=True),
    )
    normed_mid = rms_scale(mixed, ffw_gain).astype(jnp.bfloat16)
    mid_all = spread_rows(normed_mid)
    gate_raw = jnp.dot(mid_all, gate_full, preferred_element_type=jnp.float32)
    up_raw = jnp.dot(mid_all, up_full, preferred_element_type=jnp.float32)
    act_low = (jax.nn.gelu(gate_raw, approximate=True) * up_raw).astype(jnp.bfloat16)
    ffw_sum = collect_rows(jnp.dot(act_low, down_full, preferred_element_type=jnp.float32))
    result = mixed + rms_scale(ffw_sum, ffw_post_gain)
    local_ids = tensor_pos * local_rows + jnp.arange(local_rows, dtype=jnp.int32)
    cont_offset = local_ids - prompt_part
    slot_of_row = jnp.clip(cont_offset // CONT, 0, GROUPS_DEV - 1)
    row_length = jnp.sum(
        jnp.where(
            slot_of_row[:, None] == jnp.arange(GROUPS_DEV, dtype=jnp.int32)[None, :],
            cont_length[None, :],
            0,
        ),
        axis=1,
    )
    live_rows = jnp.where(
        (local_ids < prompt_part) | (cont_offset % CONT < row_length), 1.0, 0.0
    ).astype(jnp.float32)
    diff = result - teacher.astype(jnp.float32)
    loss_sum = lax.psum(jnp.sum(live_rows[:, None] * diff * diff), ("fsdp", "tensor"))
    count_f = token_count.astype(jnp.float32)
    loss = loss_sum / count_f
    grad_result = loss_scale / count_f * 2.0 * live_rows[:, None] * diff
    ffw_check, ffw_pull = jax.vjp(rms_scale, ffw_sum, ffw_post_gain)
    grad_ffw_sum, grad_ffw_post_gain = ffw_pull(grad_result)
    grad_ffw_all = spread_grads(grad_ffw_sum.astype(jnp.bfloat16))
    grad_down_w = contract_rows(act_low, grad_ffw_all)
    grad_act = contract_cols(grad_ffw_all, down_full)
    act_check, act_pull = jax.vjp(
        lambda gate_in, up_in: jax.nn.gelu(gate_in, approximate=True) * up_in, gate_raw, up_raw
    )
    grad_gate_raw, grad_up_raw = act_pull(grad_act)
    grad_gate_low = grad_gate_raw.astype(jnp.bfloat16)
    grad_up_low = grad_up_raw.astype(jnp.bfloat16)
    grad_gate_w = contract_rows(mid_all, grad_gate_low)
    grad_up_w = contract_rows(mid_all, grad_up_low)
    grad_mid = collect_grads(
        contract_cols(grad_gate_low, gate_full) + contract_cols(grad_up_low, up_full)
    )
    mid_check, mid_pull = jax.vjp(rms_scale, mixed, ffw_gain)
    grad_mixed_part, grad_ffw_gain = mid_pull(grad_mid)
    grad_mixed = grad_result + grad_mixed_part
    post_check, post_pull = jax.vjp(rms_scale, attn_sum, attn_post_gain)
    grad_attn_sum, grad_attn_post_gain = post_pull(grad_mixed)
    grad_attn_all = spread_grads(grad_attn_sum.astype(jnp.bfloat16))
    grad_out_w = contract_rows(attn_low, grad_attn_all)
    grad_attn_rows = contract_cols(grad_attn_all, out_full).astype(jnp.bfloat16)
    grad_shared = jnp.zeros((PROMPT, GROUPS_DEV, 2 * HEAD), jnp.float32)
    grad_query_prompt = []
    grad_query_cont = []
    grad_cont_pairs = []
    for slot_number in range(GROUPS_DEV):
        query_prompt = query_rot[slot_number * PSLICE : (slot_number + 1) * PSLICE]
        query_cont = query_rot[
            prompt_part + slot_number * CONT : prompt_part + (slot_number + 1) * CONT
        ]
        grad_prompt_blk = grad_attn_rows[slot_number * PSLICE : (slot_number + 1) * PSLICE]
        grad_cont_blk = grad_attn_rows[
            prompt_part + slot_number * CONT : prompt_part + (slot_number + 1) * CONT
        ]
        own_pairs = held_rows[:, slot_number]
        cont_keys = kept_cont_keys[slot_number]
        grad_query_p, grad_pairs_p = attend_back(
            query_prompt,
            own_pairs[:, :HEAD],
            own_pairs[:, HEAD:],
            the_prompt_mask,
            kept_prompt_sums[slot_number],
            grad_prompt_blk,
            score_scale,
        )
        grad_query_c, grad_pairs_c = attend_back(
            query_cont,
            cont_keys[:, :HEAD],
            cont_keys[:, HEAD:],
            cont_mask(cont_length[slot_number]),
            kept_cont_sums[slot_number],
            grad_cont_blk,
            score_scale,
        )
        grad_shared = grad_shared.at[:, slot_number].add(grad_pairs_p)
        mapped = cont_prompt[slot_number]
        current = lax.dynamic_index_in_dim(grad_shared, mapped, 1, keepdims=False)
        grad_shared = lax.dynamic_update_index_in_dim(
            grad_shared, current + grad_pairs_c[:PROMPT], mapped, 1
        )
        grad_cont_pairs.append(grad_pairs_c[PROMPT:])
        grad_query_prompt.append(grad_query_p)
        grad_query_cont.append(grad_query_c)
    held_grads = grad_shared
    for bit_level in reversed(range(level_count)):
        half_rows = held_grads.shape[0] // 2
        upper_half = fsdp_pos // 2**bit_level % 2 == 1
        keep_part = jnp.where(upper_half, held_grads[half_rows:], held_grads[:half_rows])
        give_part = jnp.where(upper_half, held_grads[:half_rows], held_grads[half_rows:])
        held_grads = keep_part + partner_2(
            give_part.astype(jnp.bfloat16), "fsdp", bit_level
        ).astype(give_part.dtype)
    own_flat = held_grads.transpose(1, 0, 2).reshape(prompt_part, 2 * HEAD)
    grad_pair_rows = jnp.concatenate([own_flat] + grad_cont_pairs, 0)
    grad_query_rot = jnp.concatenate(grad_query_prompt + grad_query_cont, 0)
    query_check, query_pull = jax.vjp(
        lambda raw_in, gain_vec: head_prep(raw_in, gain_vec, angles), query_raw, query_gain
    )
    grad_query_raw, grad_query_gain = query_pull(grad_query_rot)
    key_check, key_pull = jax.vjp(
        lambda raw_in, gain_vec: head_prep(raw_in, gain_vec, angles), key_raw, key_gain
    )
    grad_key_raw, grad_key_gain = key_pull(grad_pair_rows[:, :HEAD])
    grad_query_low = grad_query_raw.astype(jnp.bfloat16)
    grad_key_low = grad_key_raw.astype(jnp.bfloat16)
    grad_value_low = grad_pair_rows[:, HEAD:].astype(jnp.bfloat16)
    grad_query_w = contract_rows(normed_all, grad_query_low)
    grad_key_w = contract_rows(normed_all, grad_key_low)
    grad_value_w = contract_rows(normed_all, grad_value_low)
    grad_normed = collect_grads(
        contract_cols(grad_query_low, query_full)
        + contract_cols(grad_key_low, key_full)
        + contract_cols(grad_value_low, value_full)
    )
    input_check, input_pull = jax.vjp(rms_scale, input_f, attn_gain)
    grad_input_part, grad_attn_gain = input_pull(grad_normed)
    grad_input = grad_mixed + grad_input_part
    summed_big = (
        lax.psum_scatter(
            grad_query_w.astype(jnp.bfloat16), "fsdp", scatter_dimension=0, tiled=True
        ).astype(jnp.float32),
        lax.psum_scatter(
            grad_out_w.astype(jnp.bfloat16), "fsdp", scatter_dimension=1, tiled=True
        ).astype(jnp.float32),
        lax.psum_scatter(
            grad_gate_w.astype(jnp.bfloat16), "fsdp", scatter_dimension=0, tiled=True
        ).astype(jnp.float32),
        lax.psum_scatter(
            grad_up_w.astype(jnp.bfloat16), "fsdp", scatter_dimension=0, tiled=True
        ).astype(jnp.float32),
        lax.psum_scatter(
            grad_down_w.astype(jnp.bfloat16), "fsdp", scatter_dimension=1, tiled=True
        ).astype(jnp.float32),
    )
    summed_small = (
        lax.psum_scatter(grad_key_w, ("fsdp", "tensor"), scatter_dimension=0, tiled=True),
        lax.psum_scatter(grad_value_w, ("fsdp", "tensor"), scatter_dimension=0, tiled=True),
        lax.psum_scatter(grad_attn_gain, ("fsdp", "tensor"), scatter_dimension=0, tiled=True),
        lax.psum_scatter(grad_attn_post_gain, ("fsdp", "tensor"), scatter_dimension=0, tiled=True),
        lax.psum_scatter(grad_ffw_gain, ("fsdp", "tensor"), scatter_dimension=0, tiled=True),
        lax.psum_scatter(grad_ffw_post_gain, ("fsdp", "tensor"), scatter_dimension=0, tiled=True),
        lax.psum_scatter(grad_query_gain, ("fsdp", "tensor"), scatter_dimension=0, tiled=True),
        lax.psum_scatter(grad_key_gain, ("fsdp", "tensor"), scatter_dimension=0, tiled=True),
    )
    return (
        result.astype(jnp.bfloat16),
        loss,
        grad_input.astype(jnp.bfloat16),
        summed_big[0],
        summed_small[0],
        summed_small[1],
        summed_big[1],
        summed_big[2],
        summed_big[3],
        summed_big[4],
        summed_small[2],
        summed_small[3],
        summed_small[4],
        summed_small[5],
        summed_small[6],
        summed_small[7],
    )


def solution(mesh):
    placed = (
        P(("fsdp", "tensor"), None),
        P(("fsdp", "tensor"), None),
        P("fsdp", "tensor"),
        P(("fsdp", "tensor"), None),
        P(("fsdp", "tensor"), None),
        P("tensor", "fsdp"),
        P("fsdp", "tensor"),
        P("fsdp", "tensor"),
        P("tensor", "fsdp"),
        P(("fsdp", "tensor")),
        P(("fsdp", "tensor")),
        P(("fsdp", "tensor")),
        P(("fsdp", "tensor")),
        P(("fsdp", "tensor")),
        P(("fsdp", "tensor")),
        P("fsdp"),
        P("fsdp"),
        P(),
        P(),
    )
    return jax.shard_map(
        local,
        mesh=mesh,
        in_specs=placed,
        out_specs=(
            P(("fsdp", "tensor"), None),
            P(),
            P(("fsdp", "tensor"), None),
            P("fsdp", "tensor"),
            P(("fsdp", "tensor"), None),
            P(("fsdp", "tensor"), None),
            P("tensor", "fsdp"),
            P("fsdp", "tensor"),
            P("fsdp", "tensor"),
            P("tensor", "fsdp"),
            P(("fsdp", "tensor")),
            P(("fsdp", "tensor")),
            P(("fsdp", "tensor")),
            P(("fsdp", "tensor")),
            P(("fsdp", "tensor")),
            P(("fsdp", "tensor")),
        ),
        check_vma=False,
    )
```

profile of v0, /device:TPU:0, one launch (start us, length us, event | category | flops | bytes accessed | tf_op | source)
XLA Modules:
  0.0 1725.8 jit_solution(11473363546042569464)
XLA Ops:
  14.8 42.3 %all-reduce.22 = (bf16[1152]{0:T(1024)(128)(2,1)S(1)}, bf16[1152]{0:T(1024)(128)(2,1)S(1)}, bf16[1152]{0:T(1024)(128)(2,1)S(1)}, bf16[256]{0:T(256)(128)(2,1)S(1...) all-reduce(bf16[1152]{0:T(1024)(128)(2,1)S(1)} %dynamic-update-slic, ...), channel_id=1, replica_groups=mesh['fsdp'=8,'tensor'=4] {'fsdp','tensor'}, use_global_device_ids=true, to_apply=%add.9 | all-reduce | flops 5120 | bytes 20480
  60.5 43.2 %all-gather = bf16[32,36,256]{2,1,0:T(8,128)(2,1)S(1)} all-gather(bf16[1,36,256]{2,1,0:T(8,128)(2,1)S(1)} %bitcast.134), channel_id=1, replica_groups=mesh['fsdp'=8,'tensor'=4] {'fsdp','tensor'}, dimensions={0}, use_global_device_ids=true | all-gather | bytes 608256 | tf_op jit(solution)/shard_map/all_gather | solution.py:157
  103.8 38.4 %all-gather.1 = bf16[32,36,256]{2,1,0:T(8,128)(2,1)S(1)} all-gather(bf16[1,36,256]{2,1,0:T(8,128)(2,1)S(1)} %bitcast.135), channel_id=1, replica_groups=mesh['fsdp'=8,'tensor'=4] {'fsdp','tensor'}, dimensions={0}, use_global_device_ids=true | all-gather | bytes 608256 | tf_op jit(solution)/shard_map/all_gather | solution.py:158
  142.4 31.6 %all_gather.53 = bf16[1152,256]{1,0:T(8,128)(2,1)S(1)} all-gather(bf16[144,256]{1,0:T(8,128)(2,1)S(1)} %copy-done.139), channel_id=1, replica_groups=mesh['fsdp'=8,'tensor'=4] {'fsdp'}, dimensions={0}, use_global_device_ids=true | all-gather | bytes 663552 | tf_op jit(solution)/shard_map/all_gather | solution.py:175
  190.3 18.2 %collective-permute-done = bf16[256,4,512]{2,0,1:T(8,128)(2,1)} collective-permute-done((bf16[256,4,512]{2,0,1:T(8,128)(2,1)S(1)}, bf16[256,4,512]{2,0,1:T(8,128)(2,1)}, u32[]{:S(2)}, u32[]{:S(2)}) %collective-permute-start) | collective-permute-done | bytes 1048608 | tf_op jit(solution)/shard_map/ppermute | solution.py:25
  211.5 40.5 %collective-permute-done.1 = bf16[512,4,512]{2,0,1:T(8,128)(2,1)} collective-permute-done((bf16[512,4,512]{2,0,1:T(8,128)(2,1)S(1)}, bf16[512,4,512]{2,0,1:T(8,128)(2,1)}, u32[]{:S(2)}, u32[]{:S(2)}) %collective-permute-start.1) | collective-permute-done | bytes 2097184 | tf_op jit(solution)/shard_map/ppermute | solution.py:25
  268.5 187.9 %all_gather.58 = bf16[256,1152]{0,1:T(8,128)(2,1)} all-gather(bf16[256,144]{0,1:T(8,128)(2,1)S(1)} %copy-done.140), channel_id=1, replica_groups=mesh['fsdp'=8,'tensor'=4] {'fsdp'}, dimensions={1}, use_global_device_ids=true | all-gather | bytes 663552 | tf_op jit(solution)/shard_map/all_gather | solution.py:176
  502.1 47.5 %reduce-scatter.14.cloned.1.call-done = bf16[512,1152]{1,0:T(8,128)(2,1)} async-done(((bf16[2048,1152]{1,0:T(8,128)(2,1)}), bf16[512,1152]{1,0:T(8,128)(2,1)}) %reduce-scatter.14.cloned.1.call-update) | async-done | bytes 1179664 | tf_op jit(solution)/shard_map/reduce_scatter | solution.py:115
  557.0 19.7 %all-gather.14.cloned.1.call-done = bf16[1152,1728]{1,0:T(8,128)(2,1)} async-done(((bf16[144,1728]{1,0:T(8,128)(2,1)}), bf16[1152,1728]{1,0:T(8,128)(2,1)}) %all-gather.14.cloned.1.call-update) | async-done | bytes 3981328 | tf_op jit(solution)/shard_map/all_gather | solution.py:244
  576.6 37.9 %all-gather.12.cloned.1.call-done = bf16[2048,1152]{1,0:T(8,128)(2,1)} async-done(((bf16[512,1152]{1,0:T(8,128)(2,1)}), bf16[2048,1152]{1,0:T(8,128)(2,1)}) %all-gather.12.cloned.1.call-update) | async-done | bytes 4718608 | tf_op jit(solution)/shard_map/all_gather | solution.py:111
  614.5 15.3 fusion.299
  629.8 59.2 %all-gather.16.cloned.1.call-done = bf16[1152,1728]{1,0:T(8,128)(2,1)} async-done(((bf16[144,1728]{1,0:T(8,128)(2,1)}), bf16[1152,1728]{1,0:T(8,128)(2,1)}) %all-gather.16.cloned.1.call-update) | async-done | bytes 3981328 | tf_op jit(solution)/shard_map/all_gather | solution.py:245
  688.9 22.0 %multiply_convert_fusion.1 = (bf16[2048,1728]{0,1:T(8,128)(2,1)}, f32[2048,1728]{0,1:T(8,128)}) fusion(f32[2048,1728]{0,1:T(8,128)} %fusion.299, bf16[2048,1152]{1,0:T(8,128)(2,1)} %all-gather.12.cloned.1.call-done, bf16[1152,1728]{1,0:T(8,128)(2,1)} %all-gather.16.cloned.1.call-done), kind=kOutput, calls=%fused_computation.10 | convolution fusion | flops 8189116416 | bytes 44089344 | tf_op jit(solution)/shard_map/dot_general | solution.py:251
  710.9 51.1 %all-gather.18.cloned.1.call-done = bf16[1728,1152]{0,1:T(8,128)(2,1)} async-done(((bf16[1728,144]{0,1:T(8,128)(2,1)}), bf16[1728,1152]{0,1:T(8,128)(2,1)}) %all-gather.18.cloned.1.call-update) | async-done | bytes 3981328 | tf_op jit(solution)/shard_map/all_gather | solution.py:246
  762.0 14.9 convolution_convert_fusion
  781.0 42.3 %reduce-scatter.16.cloned.1.call-done = bf16[512,1152]{1,0:T(8,128)(2,1)} async-done(((bf16[2048,1152]{1,0:T(8,128)(2,1)}), bf16[512,1152]{1,0:T(8,128)(2,1)}) %reduce-scatter.16.cloned.1.call-update) | async-done | bytes 1179664 | tf_op jit(solution)/shard_map/reduce_scatter | solution.py:115
  833.3 37.6 %all-gather.20.cloned.1.call-done = bf16[2048,1152]{1,0:T(8,128)(2,1)} async-done(((bf16[512,1152]{1,0:T(8,128)(2,1)}), bf16[2048,1152]{1,0:T(8,128)(2,1)}) %all-gather.20.cloned.1.call-update) | async-done | bytes 4718608 | tf_op jit(solution)/shard_map/all_gather | solution.py:121
  870.9 28.0 %multiply_convert_fusion = (bf16[2048,1728]{0,1:T(8,128)(2,1)}, bf16[2048,1728]{0,1:T(8,128)(2,1)}) fusion(f32[2048,1728]{0,1:T(8,128)} %fusion.299, f32[2048,1728]{0,1:T(8,128)} %get-tuple-element.154, bf16[2048,1152]{1,0:T(8,128)(2,1)} %all-gather.20.cloned.1.call-done, bf16[1728,1152]{0,1:T(8,128)(2,1)} %all-gather.18.cloned.1.call-done), kind=kOutput, calls=%fused_computation.9 | convolution fusion | flops 8238661632 | bytes 51167232 | tf_op jit(solution)/shard_map/dot_general | solution.py:66
  913.3 15.1 add_convert_fusion
  928.4 47.8 %reduce-scatter.18.cloned.1.call-done = bf16[512,1152]{1,0:T(8,128)(2,1)} async-done(((bf16[2048,1152]{1,0:T(8,128)(2,1)}), bf16[512,1152]{1,0:T(8,128)(2,1)}) %reduce-scatter.18.cloned.1.call-update) | async-done | bytes 1179664 | tf_op jit(solution)/shard_map/reduce_scatter | solution.py:125
  1150.5 217.4 %collective-permute-done.3 = bf16[1024,4,512]{0,2,1:T(8,128)(2,1)} collective-permute-done((bf16[1024,4,512]{0,2,1:T(8,128)(2,1)}, bf16[1024,4,512]{0,2,1:T(8,128)(2,1)}, u32[]{:S(2)}, u32[]{:S(2)}) %collective-permute-start.3) | collective-permute-done | bytes 4194336 | tf_op jit(solution)/shard_map/ppermute | solution.py:25
  1391.6 54.3 %collective-permute-done.4 = bf16[512,4,512]{0,2,1:T(8,128)(2,1)} collective-permute-done((bf16[512,4,512]{0,2,1:T(8,128)(2,1)}, bf16[512,4,512]{0,2,1:T(8,128)(2,1)}, u32[]{:S(2)}, u32[]{:S(2)}) %collective-permute-start.4) | collective-permute-done | bytes 2097184 | tf_op jit(solution)/shard_map/ppermute | solution.py:25
  1532.6 81.0 %fusion.286 = (f32[40,256]{1,0:T(8,128)}, f32[40,256]{1,0:T(8,128)}) fusion(f32[1152,256]{1,0:T(8,128)S(1)} %fusion.302, f32[1152,256]{1,0:T(8,128)S(1)} %fusion.197), kind=kCustom, calls=%all-reduce-scatter.2 | all-reduce-scatter fusion | flops 655361 | bytes 2441216
  1660.8 45.8 %all-reduce.21 = (f32[]{:T(128)}, f32[1152]{0:T(1024)}, f32[1152]{0:T(1024)}, f32[1152]{0:T(1024)}, f32[1152]{0:T(1024)}, /*index=5*/f32[256]{0:T(256)}, f32[256]{0:T(256)S(1)}) all-reduce(f32[]{:T(128)} %get-tuple-element.74, f32[1152]{0:T(1024)} %get-tuple-element.75, ...), channel_id=1, replica_groups=mesh['fsdp'=8,'tensor'=4] {'fsdp','tensor'}, use_global_device_ids=true, to_apply=%region_26.27 | all-reduce | flops 5121 | bytes 40968 | tf_op jit(solution)/shard_map/psum | solution.py:270
  (680 shorter events, 457.6 us)
Async XLA Ops:
  8.0 166.0 %all-gather.10.cloned.1.call-start = ((), (), s32[]{:S(2)}) async-start(), calls=%async_computation.9 | async-start | bytes 5898240 | tf_op jit(solution)/shard_map/all_gather | solution.py:111
  60.4 489.2 %reduce-scatter.14.cloned.1.call-start = ((), (), s32[]{:S(2)}) async-start(), calls=%async_computation.10 | async-start | bytes 5898240 | tf_op jit(solution)/shard_map/reduce_scatter | solution.py:115
  211.3 40.7 %collective-permute-start.1 = (bf16[512,4,512]{2,0,1:T(8,128)(2,1)S(1)}, bf16[512,4,512]{2,0,1:T(8,128)(2,1)}, u32[]{:S(2)}, u32[]{:S(2)}) collective-permute-start(bf16[512,4,512]{2,0,1:T(8,128)(2,1)S(1)} %maximum_select_fusion.2), channel_id=1, source_target_pairs={{0,8},{4,12},{8,0},{12,4},{16,24},{20,28},{24,16},{28,20},{1,9},{5... | collective-permute-start | bytes 6291464 | tf_op jit(solution)/shard_map/ppermute | solution.py:25
  256.8 203.6 %collective-permute-start.2 = (bf16[1024,4,512]{2,0,1:T(8,128)(2,1)}, bf16[1024,4,512]{2,0,1:T(8,128)(2,1)}, u32[]{:S(2)}, u32[]{:S(2)}) collective-permute-start(bf16[1024,4,512]{2,0,1:T(8,128)(2,1)} %maximum_select_fusion.1), channel_id=1, source_target_pairs={{0,16},{4,20},{8,24},{12,28},{16,0},{20,4},{24,8},{28,12},{1,17},{... | collective-permute-start | bytes 12582920 | tf_op jit(solution)/shard_map/ppermute | solution.py:25
  501.5 75.1 %all-gather.14.cloned.1.call-start = ((), (), s32[]{:S(2)}) async-start(), calls=%async_computation.12 | async-start | bytes 4644864 | tf_op jit(solution)/shard_map/all_gather | solution.py:244
  502.1 112.4 %all-gather.12.cloned.1.call-start = ((), (), s32[]{:S(2)}) async-start(), calls=%async_computation.11 | async-start | bytes 5898240 | tf_op jit(solution)/shard_map/all_gather | solution.py:111
  555.6 133.3 %all-gather.16.cloned.1.call-start = ((), (), s32[]{:S(2)}) async-start(), calls=%async_computation.13 | async-start | bytes 4644864 | tf_op jit(solution)/shard_map/all_gather | solution.py:245
  556.2 205.8 %all-gather.18.cloned.1.call-start = ((), (), s32[]{:S(2)}) async-start(), calls=%async_computation.14 | async-start | bytes 4644864 | tf_op jit(solution)/shard_map/all_gather | solution.py:246
  556.9 266.4 %reduce-scatter.16.cloned.1.call-start = ((), (), s32[]{:S(2)}) async-start(), calls=%async_computation.15 | async-start | bytes 5898240 | tf_op jit(solution)/shard_map/reduce_scatter | solution.py:115
  776.9 94.0 %all-gather.20.cloned.1.call-start = ((), (), s32[]{:S(2)}) async-start(), calls=%async_computation.16 | async-start | bytes 5898240 | tf_op jit(solution)/shard_map/all_gather | solution.py:121
  833.2 143.0 %reduce-scatter.18.cloned.1.call-start = ((), (), s32[]{:S(2)}) async-start(), calls=%async_computation.17 | async-start | bytes 5898240 | tf_op jit(solution)/shard_map/reduce_scatter | solution.py:125
  928.4 94.6 %all-gather.22.cloned.1.call-start = ((), (), s32[]{:S(2)}) async-start(), calls=%async_computation.18 | async-start | bytes 5898240 | tf_op jit(solution)/shard_map/all_gather | solution.py:121
  985.4 645.5 %reduce-scatter.30.cloned.1.call-start = ((), (), s32[]{:S(2)}) async-start(), calls=%async_computation.24 | async-start | bytes 4644864 | tf_op jit(solution)/shard_map/reduce_scatter | solution.py:387
  999.6 633.3 %reduce-scatter.28.cloned.1.call-start = ((), (), s32[]{:S(2)}) async-start(), calls=%async_computation.23 | async-start | bytes 4644864 | tf_op jit(solution)/shard_map/reduce_scatter | solution.py:384
  1014.2 620.9 %reduce-scatter.26.cloned.1.call-start = ((), (), s32[]{:S(2)}) async-start(), calls=%async_computation.22 | async-start | bytes 4644864 | tf_op jit(solution)/shard_map/reduce_scatter | solution.py:381
  1133.7 234.2 %collective-permute-start.3 = (bf16[1024,4,512]{0,2,1:T(8,128)(2,1)}, bf16[1024,4,512]{0,2,1:T(8,128)(2,1)}, u32[]{:S(2)}, u32[]{:S(2)}) collective-permute-start(bf16[1024,4,512]{0,2,1:T(8,128)(2,1)} %select_convert_fusion), channel_id=1, source_target_pairs={{0,16},{4,20},{8,24},{12,28},{16,0},{20,4},{24,8},{28,12},{1,17},{... | collective-permute-start | bytes 12582920 | tf_op jit(solution)/shard_map/ppermute | solution.py:25
  1150.2 487.1 %reduce-scatter.24.cloned.1.call-start = ((), (), s32[]{:S(2)}) async-start(), calls=%async_computation.21 | async-start | bytes 663552 | tf_op jit(solution)/shard_map/reduce_scatter | solution.py:378
  1381.7 64.2 %collective-permute-start.4 = (bf16[512,4,512]{0,2,1:T(8,128)(2,1)}, bf16[512,4,512]{0,2,1:T(8,128)(2,1)}, u32[]{:S(2)}, u32[]{:S(2)}) collective-permute-start(bf16[512,4,512]{0,2,1:T(8,128)(2,1)} %select_convert_fusion.1), channel_id=1, source_target_pairs={{0,8},{4,12},{8,0},{12,4},{16,24},{20,28},{24,16},{28,20},{1,9},{5... | collective-permute-start | bytes 6291464 | tf_op jit(solution)/shard_map/ppermute | solution.py:25
  1454.3 25.5 %collective-permute-start.5 = (bf16[256,4,512]{0,2,1:T(8,128)(2,1)}, bf16[256,4,512]{0,2,1:T(8,128)(2,1)}, u32[]{:S(2)}, u32[]{:S(2)}) collective-permute-start(bf16[256,4,512]{0,2,1:T(8,128)(2,1)} %select_convert_fusion.2), channel_id=1, source_target_pairs={{0,4},{4,0},{8,12},{12,8},{16,20},{20,16},{24,28},{28,24},{1,5},{5... | collective-permute-start | bytes 3145736 | tf_op jit(solution)/shard_map/ppermute | solution.py:25
  1457.2 198.5 %reduce-scatter.22.cloned.1.call-start = ((), (), s32[]{:S(2)}) async-start(), calls=%async_computation.20 | async-start | bytes 663552 | tf_op jit(solution)/shard_map/reduce_scatter | solution.py:375
  1513.5 143.8 %reduce-scatter.20.cloned.1.call-start = ((), (), s32[]{:S(2)}) async-start(), calls=%async_computation.19 | async-start | bytes 5898240 | tf_op jit(solution)/shard_map/reduce_scatter | solution.py:125
  1621.9 24.0 %collective-permute-start.12 = (f32[40,256]{1,0:T(8,128)}, f32[40,256]{1,0:T(8,128)}, u32[]{:S(2)}, u32[]{:S(2)}) collective-permute-start(f32[40,256]{1,0:T(8,128)} %get-tuple-element.93), channel_id=1, source_target_pairs={{0,3},{1,4},{2,5},{3,6},{4,7},{5,8},{6,9},{7,10},{8,11},{9,12},{10... | collective-permute-start | bytes 122888
  1623.8 22.1 %collective-permute-start.11 = (f32[40,256]{1,0:T(8,128)}, f32[40,256]{1,0:T(8,128)}, u32[]{:S(2)}, u32[]{:S(2)}) collective-permute-start(f32[40,256]{1,0:T(8,128)} %get-tuple-element.93), channel_id=1, source_target_pairs={{0,2},{1,3},{2,4},{3,5},{4,6},{5,7},{6,8},{7,9},{8,10},{9,11},{10,... | collective-permute-start | bytes 122888
  1625.7 20.2 %collective-permute-start.10 = (f32[40,256]{1,0:T(8,128)}, f32[40,256]{1,0:T(8,128)}, u32[]{:S(2)}, u32[]{:S(2)}) collective-permute-start(f32[40,256]{1,0:T(8,128)} %get-tuple-element.93), channel_id=1, source_target_pairs={{0,1},{1,2},{2,3},{3,4},{4,5},{5,6},{6,7},{7,8},{8,9},{9,10},{10,1... | collective-permute-start | bytes 122888
  (210 other events, 2692.9 us)
Sparse Core Ops, SparseCore 0:
  60.5 42.7 all-gather.9
  501.6 47.9 reduce-scatter.13
  777.0 46.2 reduce-scatter.15
  833.3 37.4 all-gather.19
  985.5 37.4 all-gather.21
Sparse Core Ops, SparseCore 1:
  504.4 72.2 all-gather.13
  578.7 35.7 all-gather.11
  616.8 72.1 all-gather.15
  691.4 70.5 all-gather.17
  928.5 47.7 reduce-scatter.17
  999.7 87.4 reduce-scatter.29
  1090.6 164.4 reduce-scatter.27
  1259.0 165.4 reduce-scatter.25
  1457.2 62.5 reduce-scatter.23
  1523.4 61.9 reduce-scatter.21
  1587.8 50.2 reduce-scatter.19
where the time goes:
time: 1730 us
  waiting for transfers between devices  697 us (40%)
  blocking collectives  470 us (27%)
  matrix products  255 us (15%)
  other arithmetic  139 us (8%)
  local copies, waits for them, and re-layouts  113 us (7%)
  between operations  29.3 us (2%)
  starting transfers between devices  22.2 us (1%)
    ppermute x6, waiting for transfers between devices, partner_2(): return lax.ppermute(value, axis, pairs)  344 us
    all_gather x1, blocking collectives, local(): lax.all_gather(out_proj, 'fsdp', axis=1, tiled=True)  188 us
    unnamed x2, blocking collectives  123 us
    dot_general x23, matrix products, contract_cols(): lax.dot_general(left_side, right_side, (((1,), (1,)), ((), ())), preferre...  92.4 us
    reduce_scatter x2, waiting for transfers between devices, collect_rows(): lax.psum_scatter(tensor_in.astype(jnp.bfloat16), 'tensor', scatter_dimens...  89.8 us
    unnamed x435, local copies, waits for them, and re-layouts  86.2 us
    dot_general x23, matrix products, contract_rows(): lax.dot_general(left_side, right_side, (((0,), (0,)), ((), ())), preferre...  82.2 us
    all_gather x1, waiting for transfers between devices, local(): lax.all_gather(up_proj, 'fsdp', axis=0, tiled=True)  59.2 us
  transfers between devices with their start and end apart: 30, of which 14 were waited for; matrix products, arithmetic and copies ran while one was open for 21% of the time, Pallas kernels for 0%

commit v1 on v0

v1 whole, which is shorter than its diff:
```python
import math

import jax
import jax.numpy as jnp
from jax import lax
from jax.sharding import PartitionSpec as P

HEAD = 256
HEADS = 4
PROMPT = 2048
CONT = 256
GROUP = 8
GROUPS_DEV = 4
PSLICE = 256
UNITS = 2
TENSOR = 4

RING = (0, 2, 4, 6, 7, 5, 3, 1)
PLACE = tuple(RING.index(member) for member in range(GROUP))

eps_norm = 1e-06
rope_base = 1000000.0
masked_score = -1e30
score_scale = 1.0 / math.sqrt(HEAD)
bf = jnp.bfloat16
f32 = jnp.float32


def swap_core(value):
    return lax.ppermute(value, "tensor", [(t, t ^ 1) for t in range(TENSOR)])


def swap_x(value):
    return lax.ppermute(value, "tensor", [(t, t ^ 2) for t in range(TENSOR)])


def swap_bit(value, bit):
    size = lax.axis_size("fsdp")
    return lax.ppermute(value, "fsdp", [(f, f ^ bit) for f in range(size)])


def shift_z(value, step):
    pairs = [(z * 2 + y, (z + step) % 4 * 2 + y) for z in range(4) for y in range(2)]
    return lax.ppermute(value, "fsdp", pairs)


def ring_step(value, way):
    size = lax.axis_size("fsdp")
    pairs = []
    for base in range(0, size, GROUP):
        for at in range(GROUP):
            pairs.append((base + RING[at], base + RING[(at + way) % GROUP]))
    return lax.ppermute(value, "fsdp", pairs)


def spread_tensor(own):
    far = swap_x(own)
    near = swap_core(own)
    return own, near, far, swap_core(far)


def collect_tensor(part_0, part_1, part_2, part_3):
    far = (part_2.astype(f32) + swap_core(part_3.astype(bf)).astype(f32)).astype(bf)
    far = swap_x(far)
    near = part_0.astype(f32) + swap_core(part_1.astype(bf)).astype(f32)
    return near + far.astype(f32)


def pick(stack, index, axis=0):
    return lax.dynamic_index_in_dim(stack, index, axis, keepdims=False)


def spread_fsdp(own, fsdp_pos):
    if lax.axis_size("fsdp") != GROUP:
        return lax.all_gather(own, "fsdp", axis=0)
    z, y = fsdp_pos // 2, fsdp_pos % 2
    column = jnp.stack([own] + [shift_z(own, step) for step in (1, 2, 3)])
    both = jnp.concatenate([column, swap_bit(column, 1)])
    return jnp.stack(
        [
            pick(both, (z - zz) % 4 + 4 * jnp.where(y == yy, 0, 1))
            for zz in range(4)
            for yy in range(2)
        ]
    )


def collect_fsdp(parts, fsdp_pos):
    if lax.axis_size("fsdp") != GROUP:
        return lax.psum_scatter(parts.astype(bf), "fsdp", scatter_dimension=0).astype(f32)
    z, y = fsdp_pos // 2, fsdp_pos % 2
    paired = parts.reshape((4, 2) + parts.shape[1:])
    give = pick(paired, 1 - y, 1).astype(bf)
    column = pick(paired, y, 1).astype(f32) + swap_bit(give, 1).astype(f32)
    total = pick(column, z)
    for step in (1, 2, 3):
        total = total + shift_z(pick(column, (z + step) % 4).astype(bf), step).astype(f32)
    return total


def order_tensor(blocks, tensor_pos):
    odd = tensor_pos % 2 == 1
    high = tensor_pos // 2 == 1
    a, b, c, d = blocks
    a, b = jnp.where(odd, b, a), jnp.where(odd, a, b)
    c, d = jnp.where(odd, d, c), jnp.where(odd, c, d)
    return (
        jnp.where(high, c, a),
        jnp.where(high, d, b),
        jnp.where(high, a, c),
        jnp.where(high, b, d),
    )


def sum_all(value):
    value = value + swap_core(value)
    value = value + swap_x(value)
    bit = 1
    while bit < lax.axis_size("fsdp"):
        value = value + swap_bit(value, bit)
        bit *= 2
    return value


def ring_spread(first, second):
    firsts, seconds = [first], [second]
    for _ in range(GROUP - 1):
        firsts.append(ring_step(firsts[-1], 1))
        seconds.append(ring_step(seconds[-1], -1))
    return firsts, seconds


def ring_collect(take_first, take_second):
    first, second = take_first(GROUP - 1), take_second(GROUP - 1)
    for s in reversed(range(GROUP - 1)):
        moved_first = ring_step(first.astype(bf), -1)
        moved_second = ring_step(second.astype(bf), 1)
        first = moved_first.astype(f32) + take_first(s)
        second = moved_second.astype(f32) + take_second(s)
    return first, second


def rms_scale(tensor_in, gain_vec):
    return (
        tensor_in
        * lax.rsqrt(jnp.mean(tensor_in * tensor_in, axis=-1, keepdims=True) + eps_norm)
        * (1.0 + gain_vec)
    )


def rotate(tensor_in, cosine, sine_part):
    half_dim = tensor_in.shape[-1] // 2
    first_half = tensor_in[..., :half_dim]
    second_half = tensor_in[..., half_dim:]
    return jnp.concatenate(
        [
            first_half * cosine - second_half * sine_part,
            second_half * cosine + first_half * sine_part,
        ],
        axis=-1,
    )


def head_prep(raw_in, gain_vec, cosine, sine_part):
    return rotate(rms_scale(raw_in, gain_vec), cosine, sine_part)


def dot_nn(left, right):
    return jnp.dot(left, right, preferred_element_type=f32)


def dot_tn(left, right):
    return lax.dot_general(left, right, (((0,), (0,)), ((), ())), preferred_element_type=f32)


def dot_nt(left, right):
    return lax.dot_general(left, right, (((1,), (1,)), ((), ())), preferred_element_type=f32)


def masked_scores(query, keys, mask):
    scores = dot_nt(query, keys) * score_scale
    return jnp.where(mask, scores.reshape(HEADS, PSLICE, -1), masked_score)


def attend(query, pairs, mask):
    scores = masked_scores(query, pairs[:, :HEAD], mask)
    row_max = jnp.max(scores, axis=-1, keepdims=True)
    shifted = jnp.exp(scores - row_max)
    row_sum = jnp.sum(shifted, axis=-1, keepdims=True)
    probs = (shifted / row_sum).reshape(HEADS * PSLICE, -1)
    return dot_nn(probs.astype(bf), pairs[:, HEAD:]), row_max + jnp.log(row_sum)


def attend_back(query, pairs, mask, log_sum, grad_out):
    scores = masked_scores(query, pairs[:, :HEAD], mask)
    probs = jnp.exp(scores - log_sum).reshape(HEADS * PSLICE, -1)
    grad_probs = dot_nt(grad_out, pairs[:, HEAD:])
    row_dot = jnp.sum(probs * grad_probs, axis=-1, keepdims=True)
    grad_scores = (probs * (grad_probs - row_dot)).astype(bf)
    grad_query = dot_nn(grad_scores, pairs[:, :HEAD]) * score_scale
    grad_keys = dot_tn(grad_scores, query) * score_scale
    grad_values = dot_tn(probs.astype(bf), grad_out)
    return grad_query, jnp.concatenate([grad_keys, grad_values], 1)


def local(
    layer_in,
    teacher,
    query_proj,
    key_proj,
    value_proj,
    out_proj,
    gate_proj,
    up_proj,
    down_proj,
    attn_norm,
    attn_post,
    ffw_norm,
    ffw_post,
    query_norm,
    key_norm,
    cont_prompt,
    cont_length,
    token_count,
    loss_scale,
):
    members = lax.axis_size("fsdp")
    fsdp_pos = lax.axis_index("fsdp")
    tensor_pos = lax.axis_index("tensor")
    core, side = tensor_pos % 2, tensor_pos // 2
    is_cont = side == 1
    group_slot = fsdp_pos % GROUP
    place = jnp.array(PLACE, jnp.int32)[group_slot]
    ring_of = jnp.array(RING, jnp.int32)
    dim = layer_in.shape[1]
    hidden = gate_proj.shape[1]
    whole_ring = members == GROUP

    shard_kv = key_proj.shape[0]
    shard_gain, shard_head = attn_norm.shape[0], query_norm.shape[0]
    gains_own = jnp.concatenate([attn_norm, attn_post, ffw_norm, ffw_post, query_norm, key_norm])
    gains_own = jnp.pad(gains_own, (0, 2 * HEAD - gains_own.shape[0]))
    packed = jnp.concatenate([jnp.concatenate([key_proj, value_proj], 1), gains_own[None]], 0)
    packed = jnp.pad(packed, ((0, -packed.shape[0] % 8), (0, 0)))
    packed_all = jnp.stack(
        order_tensor(spread_tensor(spread_fsdp(packed, fsdp_pos)), tensor_pos), 1
    )
    kv_full = packed_all[:, :, :shard_kv].reshape(dim, 2 * HEAD)
    gains_all = packed_all[:, :, shard_kv].astype(f32)

    def gain_of(number):
        start = number * shard_gain
        return gains_all[:, :, start : start + shard_gain].reshape(dim)

    def head_gain_of(number):
        start = 4 * shard_gain + number * shard_head
        return gains_all[:, :, start : start + shard_head].reshape(HEAD)

    attn_gain, attn_post_gain, ffw_gain, ffw_post_gain = (gain_of(k) for k in range(4))
    query_gain, key_gain = head_gain_of(0), head_gain_of(1)

    qo_own = jnp.concatenate([query_proj, out_proj.T], 1)
    qo_column = spread_fsdp(qo_own, fsdp_pos).reshape(dim, 2 * HEAD)
    qo_blocks = spread_tensor(qo_column)
    query_full = jnp.concatenate([block[:, :HEAD] for block in qo_blocks], 1)
    out_full = jnp.concatenate([block[:, HEAD:] for block in qo_blocks], 1)

    down_own = down_proj.T
    if whole_ring:
        rows = gate_proj.shape[0]
        cut = 80
        firsts, seconds = ring_spread(
            jnp.concatenate([gate_proj, down_own[:cut]], 0),
            jnp.concatenate([up_proj, down_own[cut:]], 0),
        )
        gate_full = jnp.zeros((dim, hidden), bf)
        up_full = jnp.zeros((dim, hidden), bf)
        down_full = jnp.zeros((dim, hidden), bf)
        for s in range(GROUP):
            at_first = ring_of[(place - s) % GROUP] * rows
            at_second = ring_of[(place + s) % GROUP] * rows
            gate_full = lax.dynamic_update_slice(gate_full, firsts[s][:rows], (at_first, 0))
            down_full = lax.dynamic_update_slice(down_full, firsts[s][rows:], (at_first, 0))
            up_full = lax.dynamic_update_slice(up_full, seconds[s][:rows], (at_second, 0))
            down_full = lax.dynamic_update_slice(
                down_full, seconds[s][rows:], (at_second + cut, 0)
            )
    else:
        gate_full = lax.all_gather(gate_proj, "fsdp", axis=0, tiled=True)
        up_full = lax.all_gather(up_proj, "fsdp", axis=0, tiled=True)
        down_full = lax.all_gather(down_own, "fsdp", axis=0, tiled=True)

    local_rows = layer_in.shape[0]
    unit_ids = jnp.arange(local_rows, dtype=jnp.int32) % PSLICE
    positions = unit_ids + jnp.where(is_cont, PROMPT, group_slot * PSLICE)
    inverse_freq = jnp.exp(
        -math.log(rope_base) * 2.0 * jnp.arange(HEAD // 2, dtype=f32) / HEAD
    )
    angles = positions.astype(f32)[:, None] * inverse_freq[None, :]
    cosine, sine_part = jnp.cos(angles), jnp.sin(angles)
    input_f = layer_in.astype(f32)
    normed_in = rms_scale(input_f, attn_gain).astype(bf)

    kv_raw = dot_nn(normed_in, kv_full)
    key_raw = kv_raw[:, :HEAD]
    key_rot = head_prep(key_raw, key_gain, cosine, sine_part).astype(bf)
    own_pairs = jnp.concatenate([key_rot, kv_raw[:, HEAD:].astype(bf)], 1)
    across = lax.ppermute(own_pairs, "tensor", [(0, 2), (1, 3)])
    prompt_pairs = jnp.where(is_cont, across, own_pairs)
    pair_firsts, pair_seconds = ring_spread(prompt_pairs[:PSLICE], prompt_pairs[PSLICE:])
    held = jnp.stack([jnp.concatenate(pair_firsts), jnp.concatenate(pair_seconds)])
    held = jnp.concatenate([held, lax.ppermute(held, "tensor", [(2, 3), (3, 2)])])

    query_raw = dot_nn(normed_in, query_full)
    query_heads = [
        head_prep(query_raw[:, h * HEAD : (h + 1) * HEAD], query_gain, cosine, sine_part).astype(bf)
        for h in range(HEADS)
    ]

    row_of = lax.broadcasted_iota(jnp.int32, (PSLICE, PSLICE), 0)
    key_of = lax.broadcasted_iota(jnp.int32, (PSLICE, PSLICE), 1)
    steps = jnp.arange(GROUP, dtype=jnp.int32)
    units = []
    outs = []
    for unit in range(UNITS):
        way = 1 if unit == 0 else -1
        source = ring_of[(place - way * steps) % GROUP]
        length = cont_length[core * UNITS + unit]
        mapped = cont_prompt[core * UNITS + unit]
        index = jnp.where(
            is_cont, jnp.where(mapped // UNITS == core, 0, UNITS) + mapped % UNITS, unit
        )
        triangle = key_of <= row_of
        mask = jnp.concatenate(
            [
                is_cont
                | (source[s] < group_slot)
                | ((source[s] == group_slot) & triangle)
                for s in range(GROUP)
            ]
            + [is_cont & triangle & (key_of < length)],
            1,
        )
        at = slice(unit * PSLICE, (unit + 1) * PSLICE)
        query = jnp.concatenate([head[at] for head in query_heads], 0)
        pairs = jnp.concatenate([pick(held, index), own_pairs[at]], 0)
        out, log_sum = attend(query, pairs, mask)
        units.append((query, pairs, mask, log_sum, index))
        out = out.astype(bf)
        outs.append(
            jnp.concatenate([out[h * PSLICE : (h + 1) * PSLICE] for h in range(HEADS)], 1)
        )
    attn_low = jnp.concatenate(outs, 0)
    attn_sum = dot_nt(attn_low, out_full)
    mixed = input_f + rms_scale(attn_sum, attn_post_gain)
    normed_mid = rms_scale(mixed, ffw_gain).astype(bf)

    mid_blocks = spread_tensor(normed_mid)
    mid_halves = [jnp.concatenate(mid_blocks[:2], 0), jnp.concatenate(mid_blocks[2:], 0)]
    gates, ups, acts, downs = [], [], [], []
    for mid in mid_halves:
        gate_raw, up_raw = dot_nn(mid, gate_full), dot_nn(mid, up_full)
        act = (jax.nn.gelu(gate_raw, approximate=True) * up_raw).astype(bf)
        down = dot_nt(act, down_full).astype(bf)
        gates.append(gate_raw)
        ups.append(up_raw)
        acts.append(act)
        downs += [down[:local_rows], down[local_rows:]]
    ffw_sum = collect_tensor(*downs)
    result = mixed + rms_scale(ffw_sum, ffw_post_gain)

    row_length = jnp.where(
        jnp.arange(local_rows) < PSLICE,
        cont_length[core * UNITS],
        cont_length[core * UNITS + 1],
    )
    live_rows = jnp.where(is_cont & (unit_ids >= row_length), 0.0, 1.0).astype(f32)
    diff = result - teacher.astype(f32)
    loss_part = jnp.sum(live_rows[:, None] * diff * diff)
    count_f = token_count.astype(f32)
    grad_result = loss_scale / count_f * 2.0 * live_rows[:, None] * diff

    _, ffw_pull = jax.vjp(rms_scale, ffw_sum, ffw_post_gain)
    grad_ffw_sum, grad_ffw_post_gain = ffw_pull(grad_result)
    grad_blocks = spread_tensor(grad_ffw_sum.astype(bf))
    grad_halves = [jnp.concatenate(grad_blocks[:2], 0), jnp.concatenate(grad_blocks[2:], 0)]
    gate_lows, up_lows, mids = [], [], []
    for half in range(2):
        grad_act = dot_nn(grad_halves[half], down_full)
        _, act_pull = jax.vjp(
            lambda g, u: jax.nn.gelu(g, approximate=True) * u, gates[half], ups[half]
        )
        grad_gate, grad_up = act_pull(grad_act)
        gate_low, up_low = grad_gate.astype(bf), grad_up.astype(bf)
        mid = (dot_nt(gate_low, gate_full) + dot_nt(up_low, up_full)).astype(bf)
        gate_lows.append(gate_low)
        up_lows.append(up_low)
        mids += [mid[:local_rows], mid[local_rows:]]
    grad_mid = collect_tensor(*mids)
    mid_all = jnp.concatenate(mid_halves, 0)
    grad_down_w = dot_tn(jnp.concatenate(grad_halves, 0), jnp.concatenate(acts, 0)).astype(bf)
    grad_gate_w = dot_tn(mid_all, jnp.concatenate(gate_lows, 0)).astype(bf)
    grad_up_w = dot_tn(mid_all, jnp.concatenate(up_lows, 0)).astype(bf)
    if whole_ring:

        def take(wide, narrow, low, high, way):
            def term(s):
                start = ring_of[(place - way * s) % GROUP] * rows
                return jnp.concatenate(
                    [
                        lax.dynamic_slice(wide, (start, 0), (rows, hidden)),
                        lax.dynamic_slice(narrow, (start + low, 0), (high - low, hidden)),
                    ],
                    0,
                ).astype(f32)

            return term

        sum_first, sum_second = ring_collect(
            take(grad_gate_w, grad_down_w, 0, cut, 1),
            take(grad_up_w, grad_down_w, cut, rows, -1),
        )
        out_gate, out_up = sum_first[:rows], sum_second[:rows]
        out_down = jnp.concatenate([sum_first[rows:], sum_second[rows:]], 0).T
    else:
        out_gate, out_up, out_down = (
            lax.psum_scatter(part, "fsdp", scatter_dimension=0, tiled=True).astype(f32)
            for part in (grad_gate_w, grad_up_w, grad_down_w)
        )
        out_down = out_down.T

    _, mid_pull = jax.vjp(rms_scale, mixed, ffw_gain)
    grad_mixed_part, grad_ffw_gain = mid_pull(grad_mid)
    grad_mixed = grad_result + grad_mixed_part
    _, post_pull = jax.vjp(rms_scale, attn_sum, attn_post_gain)
    grad_attn_sum, grad_attn_post_gain = post_pull(grad_mixed)
    grad_attn_low = grad_attn_sum.astype(bf)
    grad_out_w = dot_tn(grad_attn_low, attn_low)
    grad_attn_rows = dot_nn(grad_attn_low, out_full).astype(bf)
    grad_query_units, grad_held, grad_own = [], [], []
    for unit in range(UNITS):
        query, pairs, mask, log_sum, index = units[unit]
        at = slice(unit * PSLICE, (unit + 1) * PSLICE)
        grad_rows = jnp.concatenate(
            [grad_attn_rows[at, h * HEAD : (h + 1) * HEAD] for h in range(HEADS)], 0
        )
        grad_query, grad_pairs = attend_back(query, pairs, mask, log_sum, grad_rows)
        grad_query_units.append(grad_query)
        grad_held.append(grad_pairs[:PROMPT])
        grad_own.append(grad_pairs[PROMPT:])

    def slot_grad(slot):
        total = 0.0
        for unit in range(UNITS):
            total = total + jnp.where(units[unit][4] == slot, grad_held[unit], 0.0)
        return total

    given = jnp.stack([slot_grad(2), slot_grad(3)]).astype(bf)
    given = lax.ppermute(given, "tensor", [(2, 3), (3, 2)])
    kept = [slot_grad(0) + given[0].astype(f32), slot_grad(1) + given[1].astype(f32)]
    ring_firsts, ring_seconds = ring_collect(
        lambda s: kept[0][s * PSLICE : (s + 1) * PSLICE],
        lambda s: kept[1][s * PSLICE : (s + 1) * PSLICE],
    )
    summed = jnp.concatenate([ring_firsts, ring_seconds], 0)
    back = lax.ppermute(summed.astype(bf), "tensor", [(2, 0), (3, 1)]).astype(f32)
    grad_pairs = jnp.where(is_cont, jnp.concatenate(grad_own, 0), summed + back)

    _, query_pull = jax.vjp(
        lambda raw, gain: tuple(
            head_prep(raw[:, h * HEAD : (h + 1) * HEAD], gain, cosine, sine_part)
            for h in range(HEADS)
        ),
        query_raw,
        query_gain,
    )
    grad_query_raw, grad_query_gain = query_pull(
        tuple(
            jnp.concatenate([g[h * PSLICE : (h + 1) * PSLICE] for g in grad_query_units], 0)
            for h in range(HEADS)
        )
    )
    _, key_pull = jax.vjp(
        lambda raw, gain: head_prep(raw, gain, cosine, sine_part), key_raw, key_gain
    )
    grad_key_raw, grad_key_gain = key_pull(grad_pairs[:, :HEAD])
    grad_query_low = grad_query_raw.astype(bf)
    grad_kv_low = jnp.concatenate([grad_key_raw, grad_pairs[:, HEAD:]], 1).astype(bf)
    grad_query_w = dot_tn(normed_in, grad_query_low)
    grad_kv_w = dot_tn(normed_in, grad_kv_low)
    grad_normed = dot_nt(grad_query_low, query_full) + dot_nt(grad_kv_low, kv_full)
    _, input_pull = jax.vjp(rms_scale, input_f, attn_gain)
    grad_input_part, grad_attn_gain = input_pull(grad_normed)
    grad_input = grad_mixed + grad_input_part

    def collect_heads(grad_w):
        column = collect_tensor(*(grad_w[:, h * HEAD : (h + 1) * HEAD] for h in range(HEADS)))
        return collect_fsdp(column.reshape(members, dim // members, HEAD), fsdp_pos)

    out_out = collect_heads(grad_out_w).T
    out_query = collect_heads(grad_query_w)
    kv_blocks = grad_kv_w.reshape(members, TENSOR, shard_kv, 2 * HEAD)
    kv_column = collect_tensor(
        *order_tensor([kv_blocks[:, t] for t in range(TENSOR)], tensor_pos)
    )
    out_kv = collect_fsdp(kv_column, fsdp_pos)

    small = jnp.concatenate(
        [
            grad_attn_gain,
            grad_attn_post_gain,
            grad_ffw_gain,
            grad_ffw_post_gain,
            grad_query_gain,
            grad_key_gain,
            loss_part[None],
        ]
    )
    length = small.shape[0]
    small = jnp.pad(small, (0, -length % 1024)).reshape(-1, 128)
    small = sum_all(small).reshape(-1)
    device = fsdp_pos * TENSOR + tensor_pos
    wide = [
        lax.dynamic_slice(small, (k * dim + device * shard_gain,), (shard_gain,)) for k in range(4)
    ]
    narrow = [
        lax.dynamic_slice(small, (4 * dim + k * HEAD + device * shard_head,), (shard_head,))
        for k in range(2)
    ]
    loss = small[length - 1] / count_f
    return (
        result.astype(bf),
        loss,
        grad_input.astype(bf),
        out_query,
        out_kv[:, :HEAD],
        out_kv[:, HEAD:],
        out_out,
        out_gate,
        out_up,
        out_down,
        *wide,
        *narrow,
    )


def solution(mesh):
    rows = P(("fsdp", "tensor"), None)
    split = P(("fsdp", "tensor"))
    inward, outward = P("fsdp", "tensor"), P("tensor", "fsdp")
    return jax.shard_map(
        local,
        mesh=mesh,
        in_specs=(
            rows,
            rows,
            inward,
            rows,
            rows,
            outward,
            inward,
            inward,
            outward,
            *(split,) * 6,
            P("fsdp"),
            P("fsdp"),
            P(),
            P(),
        ),
        out_specs=(
            rows,
            P(),
            rows,
            inward,
            rows,
            rows,
            outward,
            inward,
            inward,
            outward,
            *(split,) * 6,
        ),
        check_vma=False,
    )
```

time: 1730 us -> 978 us (0.57)
  blocking collectives: 470 us -> 0 us
  waiting for transfers between devices: 697 us -> 329 us
  starting transfers between devices: 22.2 us -> 122 us
  other arithmetic: 139 us -> 103 us
  matrix products: 255 us -> 225 us
  between operations: 29.3 us -> 55.2 us
  local copies, waits for them, and re-layouts: 113 us -> 132 us
    all_gather x4 -> x0, blocking collectives: 301 us -> none  [the longest x1 188 us: local(): lax.all_gather(out_proj, 'fsdp', axis=1, tiled=True)]
    all_gather x7 -> x0, waiting for transfers between devices: 214 us -> none  [the longest x1 59.2 us: local(): lax.all_gather(up_proj, 'fsdp', axis=0, tiled=True)]
    reduce_scatter x9 -> x0, waiting for transfers between devices: 138 us -> none  [the longest x2 89.8 us: collect_rows(): lax.psum_scatter(tensor_in.astype(jnp.bfloat16), 'tensor', scatter_dimens...]
    unnamed x2 -> x0, blocking collectives: 123 us -> none
    ppermute x6 -> x112, starting transfers between devices: 5.11 us -> 122 us  [the longest x56 58.5 us: ring_step(): return lax.ppermute(value, 'fsdp', pairs)]
    unnamed x435 -> x502, local copies, waits for them, and re-layouts: 86.2 us -> 34.4 us
    psum x1 -> x0, blocking collectives: 45.8 us -> none  [local(): lax.psum(jnp.sum(live_rows[:, None] * diff * diff), ('fsdp', 'tensor'))]
    dynamic_update_slice x0 -> x32, local copies, waits for them, and re-layouts: none -> 40.1 us  [the longest x8 10.9 us: local(): lax.dynamic_update_slice(up_full, seconds[s][:rows], (at_second, 0))]
  transfers between devices with their start and end apart: 30 -> 112, of which waited for: 14 -> 48; matrix products, arithmetic and copies ran while one was open for 21% -> 32% of each run, Pallas kernels for 0% -> 0%
where the time goes in v1:
time: 978 us; the launch traced here: 967 us
  waiting for transfers between devices  329 us (34%)
  matrix products  225 us (23%)
  local copies, waits for them, and re-layouts  132 us (13%)
  starting transfers between devices  122 us (12%)
  other arithmetic  103 us (11%)
  between operations  55.2 us (6%)
    ppermute x56, waiting for transfers between devices, ring_step(): return lax.ppermute(value, 'fsdp', pairs)  183 us
    ppermute x10, waiting for transfers between devices, swap_x(): return lax.ppermute(value, 'tensor', [(t, t ^ 2) for t in range(TENSOR)])  97.4 us
    dot_general x13, matrix products, dot_nn(): return jnp.dot(left, right, preferred_element_type=f32)  87.8 us
    dot_general x10, matrix products, dot_tn(): lax.dot_general(left, right, (((0,), (0,)), ((), ())), preferred_element_...  69.5 us
    dot_general x13, matrix products, dot_nt(): lax.dot_general(left, right, (((1,), (1,)), ((), ())), preferred_element_...  67.8 us
    ppermute x56, starting transfers between devices, ring_step(): return lax.ppermute(value, 'fsdp', pairs)  58.5 us
    unnamed x502, local copies, waits for them, and re-layouts  34.4 us
    ppermute x8, waiting for transfers between devices, swap_bit(): return lax.ppermute(value, 'fsdp', [(f, f ^ bit) for f in range(size)])  30.7 us
  transfers between devices with their start and end apart: 112, of which 48 were waited for; matrix products, arithmetic and copies ran while one was open for 32% of the time, Pallas kernels for 0%

profile of v1, /device:TPU:0, one launch (start us, length us, event | category | flops | bytes accessed | tf_op | source)
XLA Modules:
  0.0 967.0 jit_solution(13038622064340867155)
XLA Ops:
  106.1 14.7 %collective-permute-done.3 = bf16[4,40,512]{2,1,0:T(8,128)(2,1)S(1)} collective-permute-done((bf16[4,40,512]{2,1,0:T(8,128)(2,1)S(1)}, bf16[4,40,512]{2,1,0:T(8,128)(2,1)S(1)}, u32[]{:S(2)}, u32[]{:S(2)}) %collective-permute-start.3) | collective-permute-done | bytes 163872 | tf_op jit(solution)/shard_map/ppermute | solution.py:39
  165.0 9.1 collective-permute-done.32
  237.5 17.4 %collective-permute-done.16 = bf16[256,512]{1,0:T(8,128)(2,1)S(1)} collective-permute-done((bf16[256,512]{1,0:T(8,128)(2,1)S(1)}, bf16[256,512]{1,0:T(8,128)(2,1)S(1)}, u32[]{:S(2)}, u32[]{:S(2)}) %collective-permute-start.16) | collective-permute-done | bytes 262176 | tf_op jit(solution)/shard_map/ppermute | solution.py:53
  304.3 12.4 %collective-permute-done.43 = bf16[208,1728]{1,0:T(8,128)(2,1)} collective-permute-done((bf16[208,1728]{1,0:T(8,128)(2,1)S(1)}, bf16[208,1728]{1,0:T(8,128)(2,1)}, u32[]{:S(2)}, u32[]{:S(2)}) %collective-permute-start.43) | collective-permute-done | bytes 718880 | tf_op jit(solution)/shard_map/ppermute | solution.py:53
  356.3 20.6 %collective-permute-done.46 = bf16[512,1152]{1,0:T(8,128)(2,1)S(1)} collective-permute-done((bf16[512,1152]{1,0:T(8,128)(2,1)S(1)}, bf16[512,1152]{1,0:T(8,128)(2,1)S(1)}, u32[]{:S(2)}, u32[]{:S(2)}) %collective-permute-start.46) | collective-permute-done | bytes 1179680 | tf_op jit(solution)/shard_map/ppermute | solution.py:34
  378.2 11.7 %fusion.65 = f32[1024,1728]{0,1:T(8,128)} fusion(bf16[1152,1728]{1,0:T(8,128)(2,1)} %slice_dynamic-update-slice_fusion.7, bf16[512,1152]{1,0:T(8,128)(2,1)S(1)} %collective-permute-done.30, bf16[512,1152]{1,0:T(8,128)(2,1)S(1)} %multiply_convert_fusion.6), kind=kOutput, calls=%fused_computation.156 | convolution fusion | flops 4081582080 | bytes 13418496 | tf_op jit(solution)/shard_map/dot_general | solution.py:169
  390.1 9.3 fusion.351
  399.4 11.8 %multiply_convert_fusion.4 = (bf16[1024,1728]{0,1:T(8,128)(2,1)S(1)}, f32[1024,1728]{0,1:T(8,128)}) fusion(f32[1024,1728]{0,1:T(8,128)} %fusion.351, bf16[1024,1152]{1,0:T(8,128)(2,1)S(1)} %constant_dynamic-update-slice_fusion.34, bf16[1152,1728]{1,0:T(8,128)(2,1)} %slice_dynamic-update-slice_fusion), kind=kOutput, calls=%fused_computation.51 | convolution fusion | flops 4094558208 | bytes 24035328 | tf_op jit(solution)/shard_map/dot_general | solution.py:169
  417.2 12.7 %multiply_convert_fusion.5 = (bf16[1024,1728]{0,1:T(8,128)(2,1)S(1)}, f32[1024,1728]{0,1:T(8,128)}) fusion(f32[1024,1728]{0,1:T(8,128)} %fusion.65, bf16[1152,1728]{1,0:T(8,128)(2,1)} %slice_dynamic-update-slice_fusion, bf16[512,1152]{1,0:T(8,128)(2,1)S(1)} %collective-permute-done.30, bf16[512,1152]{1,0:T(8,128)(2,1)S(1)} %multiply_convert_fusion.6), kind=kOutput, calls=%fused_computation.52 | convolution fusion | flops 4099276800 | bytes 24035328 | tf_op jit(solution)/shard_map/dot_general | solution.py:169
  446.5 20.2 %collective-permute-done.49 = bf16[512,1152]{1,0:T(8,128)(2,1)} collective-permute-done((bf16[512,1152]{1,0:T(8,128)(2,1)}, bf16[512,1152]{1,0:T(8,128)(2,1)}, u32[]{:S(2)}, u32[]{:S(2)}) %collective-permute-start.49) | collective-permute-done | bytes 1179680 | tf_op jit(solution)/shard_map/ppermute | solution.py:34
  480.9 25.2 %collective-permute-done.52 = bf16[512,1152]{1,0:T(8,128)(2,1)} collective-permute-done((bf16[512,1152]{1,0:T(8,128)(2,1)}, bf16[512,1152]{1,0:T(8,128)(2,1)}, u32[]{:S(2)}, u32[]{:S(2)}) %collective-permute-start.52) | collective-permute-done | bytes 1179680 | tf_op jit(solution)/shard_map/ppermute | solution.py:34
  506.1 16.2 %fusion.10 = (bf16[1024,1728]{0,1:T(8,128)(2,1)}, bf16[1024,1728]{0,1:T(8,128)(2,1)S(1)}) fusion(f32[1024,1728]{0,1:T(8,128)} %fusion.65, f32[1024,1728]{0,1:T(8,128)} %get-tuple-element.345, bf16[1152,1728]{1,0:T(8,128)(2,1)} %copy-done.33, bf16[512,1152]{1,0:T(8,128)(2,1)} %collective-permute-done.50, bf16[512,1152]{1,0:T(8,128)(2,1)} %fusion.46), kind=kOutput, calls=%fused_computation.32 | convolution fusion | flops 4124049408 | bytes 27574272 | tf_op jit(solution)/shard_map/dot_general | solution.py:169
  522.3 10.3 %fusion.352 = f32[1024,1152]{1,0:T(8,128)} fusion(bf16[1024,1728]{0,1:T(8,128)(2,1)S(1)} %get-tuple-element.146, bf16[1152,1728]{1,0:T(8,128)(2,1)} %slice_dynamic-update-slice_fusion), kind=kOutput, calls=%fused_computation.747 | convolution fusion | flops 4076863488 | bytes 12238848 | tf_op jit(solution)/shard_map/dot_general | solution.py:177
  532.6 15.3 %convolution_convert_fusion.1 = bf16[1152,1728]{1,0:T(8,128)(2,1)} fusion(bf16[1024,1728]{0,1:T(8,128)(2,1)} %copy-done.209, bf16[1024,1728]{0,1:T(8,128)(2,1)} %copy-done.210, bf16[512,1152]{1,0:T(8,128)(2,1)} %collective-permute-done.53, bf16[512,1152]{1,0:T(8,128)(2,1)} %collective-permute-done.52, bf16[512,1152]{1,0:T(8,128)(2,1)} %collective-permute-done.50, ...), kind=kOutput, calls=%fused_computation.22 | convolution fusion | flops 8188747776 | bytes 15777792 | tf_op jit(solution)/shard_map/dot_general | solution.py:173
  553.9 15.1 %fusion.17 = (bf16[1024,1728]{0,1:T(8,128)(2,1)}, bf16[1024,1728]{0,1:T(8,128)(2,1)S(1)}) fusion(f32[1024,1728]{0,1:T(8,128)} %fusion.351, f32[1024,1728]{0,1:T(8,128)} %get-tuple-element.343, bf16[1152,1728]{1,0:T(8,128)(2,1)S(1)} %copy-done.34, bf16[512,1152]{1,0:T(8,128)(2,1)} %collective-permute-done.53, bf16[512,1152]{1,0:T(8,128)(2,1)} %collective-permute-done.52), kind=kOutput, calls=%fused_computation.39 | convolution fusion | flops 4124049408 | bytes 27574272 | tf_op jit(solution)/shard_map/dot_general | solution.py:169
  570.8 9.2 fusion.353
  580.0 15.2 %convolution_convert_fusion = bf16[1152,1728]{1,0:T(8,128)(2,1)} fusion(bf16[1024,1728]{0,1:T(8,128)(2,1)} %copy-done.214, bf16[1024,1728]{0,1:T(8,128)(2,1)} %copy-done.213, bf16[512,1152]{1,0:T(8,128)(2,1)} %copy-done.82, bf16[512,1152]{1,0:T(8,128)(2,1)} %copy-done.81, bf16[512,1152]{1,0:T(8,128)(2,1)} %copy-done.208, bf16[512,1152]{1,0:T(8,128)(2,1)} %copy-done.80), kind=kOutput, calls=%fused_computation.21 | convolution fusion | flops 8188747776 | bytes 15777792 | tf_op jit(solution)/shard_map/dot_general | solution.py:173
  601.3 15.2 %convolution_convert_fusion.2 = bf16[1152,1728]{1,0:T(8,128)(2,1)} fusion(bf16[1024,1728]{0,1:T(8,128)(2,1)} %get-tuple-element.147, bf16[1024,1728]{0,1:T(8,128)(2,1)} %get-tuple-element.145, bf16[512,1152]{1,0:T(8,128)(2,1)} %copy-done.82, bf16[512,1152]{1,0:T(8,128)(2,1)} %copy-done.81, bf16[512,1152]{1,0:T(8,128)(2,1)} %copy-done.208, ...), kind=kOutput, calls=%fused_computation.23 | convolution fusion | flops 8188747776 | bytes 15777792 | tf_op jit(solution)/shard_map/dot_general | solution.py:173
  621.4 8.5 add_convert_fusion
  641.7 7.6 add_convert_fusion.1
  760.6 9.2 collective-permute-done.93
  792.2 11.5 %collective-permute-done.64 = bf16[256,512]{1,0:T(8,128)(2,1)S(1)} collective-permute-done((bf16[256,512]{1,0:T(8,128)(2,1)S(1)}, bf16[256,512]{1,0:T(8,128)(2,1)S(1)}, u32[]{:S(2)}, u32[]{:S(2)}) %collective-permute-start.64) | collective-permute-done | bytes 262176 | tf_op jit(solution)/shard_map/ppermute | solution.py:53
  835.9 13.3 %collective-permute-done.61 = bf16[256,512]{1,0:T(8,128)(2,1)S(1)} collective-permute-done((bf16[256,512]{1,0:T(8,128)(2,1)S(1)}, bf16[256,512]{1,0:T(8,128)(2,1)S(1)}, u32[]{:S(2)}, u32[]{:S(2)}) %collective-permute-start.61) | collective-permute-done | bytes 262176 | tf_op jit(solution)/shard_map/ppermute | solution.py:53
  862.2 14.4 %collective-permute-done.63 = bf16[256,512]{1,0:T(8,128)(2,1)S(1)} collective-permute-done((bf16[256,512]{1,0:T(8,128)(2,1)S(1)}, bf16[256,512]{1,0:T(8,128)(2,1)S(1)}, u32[]{:S(2)}, u32[]{:S(2)}) %collective-permute-start.63) | collective-permute-done | bytes 262176 | tf_op jit(solution)/shard_map/ppermute | solution.py:53
  (1008 shorter events, 585.9 us)
Async XLA Ops:
  6.2 85.8 %collective-permute-start = (bf16[40,512]{1,0:T(8,128)(2,1)S(1)}, bf16[40,512]{1,0:T(8,128)(2,1)}, u32[]{:S(2)}, u32[]{:S(2)}) collective-permute-start(bf16[40,512]{1,0:T(8,128)(2,1)S(1)} %get-tuple-element.144), channel_id=1, source_target_pairs={{0,8},{4,12},{8,16},{12,20},{16,24},{20,28},{24,0},{28,4},{1,9},{5... | collective-permute-start | bytes 122888 | tf_op jit(solution)/shard_map/ppermute | solution.py:44
  9.2 87.0 %collective-permute-start.1 = (bf16[40,512]{1,0:T(8,128)(2,1)S(1)}, bf16[40,512]{1,0:T(8,128)(2,1)}, u32[]{:S(2)}, u32[]{:S(2)}) collective-permute-start(bf16[40,512]{1,0:T(8,128)(2,1)S(1)} %get-tuple-element.144), channel_id=1, source_target_pairs={{0,16},{4,20},{8,24},{12,28},{16,0},{20,4},{24,8},{28,12},{1,17},{... | collective-permute-start | bytes 122888 | tf_op jit(solution)/shard_map/ppermute | solution.py:44
  11.8 86.4 %collective-permute-start.2 = (bf16[40,512]{1,0:T(8,128)(2,1)S(1)}, bf16[40,512]{1,0:T(8,128)(2,1)}, u32[]{:S(2)}, u32[]{:S(2)}) collective-permute-start(bf16[40,512]{1,0:T(8,128)(2,1)S(1)} %get-tuple-element.144), channel_id=1, source_target_pairs={{0,24},{4,28},{8,0},{12,4},{16,8},{20,12},{24,16},{28,20},{1,25},{... | collective-permute-start | bytes 122888 | tf_op jit(solution)/shard_map/ppermute | solution.py:44
  14.8 87.1 %collective-permute-start.7 = (bf16[144,512]{1,0:T(8,128)(2,1)}, bf16[144,512]{1,0:T(8,128)(2,1)}, u32[]{:S(2)}, u32[]{:S(2)}) collective-permute-start(bf16[144,512]{1,0:T(8,128)(2,1)} %get-tuple-element.276), channel_id=1, source_target_pairs={{0,8},{4,12},{8,16},{12,20},{16,24},{20,28},{24,0},{28,4},{1,9},{5... | collective-permute-start | bytes 442376 | tf_op jit(solution)/shard_map/ppermute | solution.py:44
  15.4 88.1 %collective-permute-start.8 = (bf16[144,512]{1,0:T(8,128)(2,1)}, bf16[144,512]{1,0:T(8,128)(2,1)}, u32[]{:S(2)}, u32[]{:S(2)}) collective-permute-start(bf16[144,512]{1,0:T(8,128)(2,1)} %get-tuple-element.276), channel_id=1, source_target_pairs={{0,16},{4,20},{8,24},{12,28},{16,0},{20,4},{24,8},{28,12},{1,17},{... | collective-permute-start | bytes 442376 | tf_op jit(solution)/shard_map/ppermute | solution.py:44
  96.2 52.0 %collective-permute-start.31 = (bf16[224,1728]{1,0:T(8,128)(2,1)}, bf16[224,1728]{1,0:T(8,128)(2,1)}, u32[]{:S(2)}, u32[]{:S(2)}) collective-permute-start(bf16[224,1728]{1,0:T(8,128)(2,1)} %pad_maximum_fusion.20), channel_id=1, source_target_pairs={{0,8},{8,16},{16,24},{24,28},{28,20},{20,12},{12,4},{4,0},{1,9},{9... | collective-permute-start | bytes 2322440 | tf_op jit(solution)/shard_map/ppermute | solution.py:53
  98.2 36.6 %collective-permute-start.38 = (bf16[208,1728]{1,0:T(8,128)(2,1)}, bf16[208,1728]{1,0:T(8,128)(2,1)}, u32[]{:S(2)}, u32[]{:S(2)}) collective-permute-start(bf16[208,1728]{1,0:T(8,128)(2,1)} %pad_maximum_fusion.22), channel_id=1, source_target_pairs={{0,4},{8,0},{16,8},{24,16},{28,24},{20,28},{12,20},{4,12},{1,5},{9... | collective-permute-start | bytes 2156552 | tf_op jit(solution)/shard_map/ppermute | solution.py:53
  104.6 34.3 %collective-permute-start.10 = (bf16[4,144,512]{2,1,0:T(8,128)(2,1)S(1)}, bf16[4,144,512]{2,1,0:T(8,128)(2,1)S(1)}, u32[]{:S(2)}, u32[]{:S(2)}) collective-permute-start(bf16[4,144,512]{2,1,0:T(8,128)(2,1)S(1)} %pad_maximum_fusion.24), channel_id=1, source_target_pairs={{0,4},{4,0},{8,12},{12,8},{16,20},{20,16},{24,28},{28,24},{1,5},{5... | collective-permute-start | bytes 1769480 | tf_op jit(solution)/shard_map/ppermute | solution.py:39
  144.3 35.3 %collective-permute-start.12 = (bf16[1152,512]{1,0:T(8,128)(2,1)}, bf16[1152,512]{1,0:T(8,128)(2,1)}, u32[]{:S(2)}, u32[]{:S(2)}) collective-permute-start(bf16[1152,512]{1,0:T(8,128)(2,1)} %bitcast.25), channel_id=1, source_target_pairs={{0,2},{1,3},{2,0},{3,1},{4,6},{5,7},{6,4},{7,5},{8,10},{9,11},{10,... | collective-permute-start | bytes 3538952 | tf_op jit(solution)/shard_map/ppermute | solution.py:34
  148.2 33.6 %collective-permute-start.11 = (bf16[1152,512]{1,0:T(8,128)(2,1)}, bf16[1152,512]{1,0:T(8,128)(2,1)}, u32[]{:S(2)}, u32[]{:S(2)}) collective-permute-start(bf16[1152,512]{1,0:T(8,128)(2,1)} %bitcast.25), channel_id=1, source_target_pairs={{0,1},{1,0},{2,3},{3,2},{4,5},{5,4},{6,7},{7,6},{8,9},{9,8},{10,11... | collective-permute-start | bytes 3538952 | tf_op jit(solution)/shard_map/ppermute | solution.py:30
  193.8 34.3 %collective-permute-start.34 = (bf16[224,1728]{1,0:T(8,128)(2,1)S(1)}, bf16[224,1728]{1,0:T(8,128)(2,1)S(1)}, u32[]{:S(2)}, u32[]{:S(2)}) collective-permute-start(bf16[224,1728]{1,0:T(8,128)(2,1)S(1)} %collective-permute-done.33), channel_id=1, source_target_pairs={{0,8},{8,16},{16,24},{24,28},{28,20},{20,12},{12,4},{4,0},{1,9},{9... | collective-permute-start | bytes 2322440 | tf_op jit(solution)/shard_map/ppermute | solution.py:53
  203.3 95.9 %collective-permute-start.42 = (bf16[208,1728]{1,0:T(8,128)(2,1)S(1)}, bf16[208,1728]{1,0:T(8,128)(2,1)S(1)}, u32[]{:S(2)}, u32[]{:S(2)}) collective-permute-start(bf16[208,1728]{1,0:T(8,128)(2,1)S(1)} %collective-permute-done.41), channel_id=1, source_target_pairs={{0,4},{8,0},{16,8},{24,16},{28,24},{20,28},{12,20},{4,12},{1,5},{9... | collective-permute-start | bytes 2156552 | tf_op jit(solution)/shard_map/ppermute | solution.py:53
  228.1 73.6 %collective-permute-start.35 = (bf16[224,1728]{1,0:T(8,128)(2,1)S(1)}, bf16[224,1728]{1,0:T(8,128)(2,1)S(1)}, u32[]{:S(2)}, u32[]{:S(2)}) collective-permute-start(bf16[224,1728]{1,0:T(8,128)(2,1)S(1)} %collective-permute-done.34), channel_id=1, source_target_pairs={{0,8},{8,16},{16,24},{24,28},{28,20},{20,12},{12,4},{4,0},{1,9},{9... | collective-permute-start | bytes 2322440 | tf_op jit(solution)/shard_map/ppermute | solution.py:53
  316.7 34.8 %collective-permute-start.44 = (bf16[208,1728]{1,0:T(8,128)(2,1)}, bf16[208,1728]{1,0:T(8,128)(2,1)}, u32[]{:S(2)}, u32[]{:S(2)}) collective-permute-start(bf16[208,1728]{1,0:T(8,128)(2,1)} %collective-permute-done.43), channel_id=1, source_target_pairs={{0,4},{8,0},{16,8},{24,16},{28,24},{20,28},{12,20},{4,12},{1,5},{9... | collective-permute-start | bytes 2156552 | tf_op jit(solution)/shard_map/ppermute | solution.py:53
  320.5 32.9 %collective-permute-start.37 = (bf16[224,1728]{1,0:T(8,128)(2,1)}, bf16[224,1728]{1,0:T(8,128)(2,1)}, u32[]{:S(2)}, u32[]{:S(2)}) collective-permute-start(bf16[224,1728]{1,0:T(8,128)(2,1)} %collective-permute-done.36), channel_id=1, source_target_pairs={{0,8},{8,16},{16,24},{24,28},{28,20},{20,12},{12,4},{4,0},{1,9},{9... | collective-permute-start | bytes 2322440 | tf_op jit(solution)/shard_map/ppermute | solution.py:53
  630.1 31.2 %collective-permute-start.54 = (bf16[512,1152]{1,0:T(8,128)(2,1)S(1)}, bf16[512,1152]{1,0:T(8,128)(2,1)S(1)}, u32[]{:S(2)}, u32[]{:S(2)}) collective-permute-start(bf16[512,1152]{1,0:T(8,128)(2,1)S(1)} %slice.804), channel_id=1, source_target_pairs={{0,1},{1,0},{2,3},{3,2},{4,5},{5,4},{6,7},{7,6},{8,9},{9,8},{10,11... | collective-permute-start | bytes 3538952 | tf_op jit(solution)/shard_map/ppermute | solution.py:30
  649.5 31.3 %collective-permute-start.51 = (bf16[512,1152]{1,0:T(8,128)(2,1)S(1)}, bf16[512,1152]{1,0:T(8,128)(2,1)S(1)}, u32[]{:S(2)}, u32[]{:S(2)}) collective-permute-start(bf16[512,1152]{1,0:T(8,128)(2,1)S(1)} %slice.802), channel_id=1, source_target_pairs={{0,1},{1,0},{2,3},{3,2},{4,5},{5,4},{6,7},{7,6},{8,9},{9,8},{10,11... | collective-permute-start | bytes 3538952 | tf_op jit(solution)/shard_map/ppermute | solution.py:30
  670.7 85.0 %collective-permute-start.108 = (bf16[208,1728]{1,0:T(8,128)(2,1)}, bf16[208,1728]{1,0:T(8,128)(2,1)}, u32[]{:S(2)}, u32[]{:S(2)}) collective-permute-start(bf16[208,1728]{1,0:T(8,128)(2,1)} %add_convert_fusion.16), channel_id=1, source_target_pairs={{0,8},{8,16},{16,24},{24,28},{28,20},{20,12},{12,4},{4,0},{1,9},{9... | collective-permute-start | bytes 2156552 | tf_op jit(solution)/shard_map/ppermute | solution.py:53
  679.6 78.5 %collective-permute-start.101 = (bf16[224,1728]{1,0:T(8,128)(2,1)}, bf16[224,1728]{1,0:T(8,128)(2,1)}, u32[]{:S(2)}, u32[]{:S(2)}) collective-permute-start(bf16[224,1728]{1,0:T(8,128)(2,1)} %add_convert_fusion.10), channel_id=1, source_target_pairs={{0,4},{8,0},{16,8},{24,16},{28,24},{20,28},{12,20},{4,12},{1,5},{9... | collective-permute-start | bytes 2322440 | tf_op jit(solution)/shard_map/ppermute | solution.py:53
  721.3 31.8 %collective-permute-start.92 = (bf16[1152,256]{1,0:T(8,128)(2,1)}, bf16[1152,256]{1,0:T(8,128)(2,1)}, u32[]{:S(2)}, u32[]{:S(2)}) collective-permute-start(bf16[1152,256]{1,0:T(8,128)(2,1)} %get-tuple-element.188), channel_id=1, source_target_pairs={{0,1},{1,0},{2,3},{3,2},{4,5},{5,4},{6,7},{7,6},{8,9},{9,8},{10,11... | collective-permute-start | bytes 1769480 | tf_op jit(solution)/shard_map/ppermute | solution.py:30
  721.3 39.3 %collective-permute-start.91 = (bf16[1152,256]{1,0:T(8,128)(2,1)}, bf16[1152,256]{1,0:T(8,128)(2,1)}, u32[]{:S(2)}, u32[]{:S(2)}) collective-permute-start(bf16[1152,256]{1,0:T(8,128)(2,1)} %get-tuple-element.187), channel_id=1, source_target_pairs={{0,1},{1,0},{2,3},{3,2},{4,5},{5,4},{6,7},{7,6},{8,9},{9,8},{10,11... | collective-permute-start | bytes 1769480 | tf_op jit(solution)/shard_map/ppermute | solution.py:30
  759.4 53.8 %collective-permute-start.102 = (bf16[224,1728]{1,0:T(8,128)(2,1)S(1)}, bf16[224,1728]{1,0:T(8,128)(2,1)S(1)}, u32[]{:S(2)}, u32[]{:S(2)}) collective-permute-start(bf16[224,1728]{1,0:T(8,128)(2,1)S(1)} %add_convert_fusion.9), channel_id=1, source_target_pairs={{0,4},{8,0},{16,8},{24,16},{28,24},{20,28},{12,20},{4,12},{1,5},{9... | collective-permute-start | bytes 2322440 | tf_op jit(solution)/shard_map/ppermute | solution.py:53
  778.1 55.5 %collective-permute-start.110 = (bf16[208,1728]{1,0:T(8,128)(2,1)S(1)}, bf16[208,1728]{1,0:T(8,128)(2,1)S(1)}, u32[]{:S(2)}, u32[]{:S(2)}) collective-permute-start(bf16[208,1728]{1,0:T(8,128)(2,1)S(1)} %add_convert_fusion.14), channel_id=1, source_target_pairs={{0,8},{8,16},{16,24},{24,28},{28,20},{20,12},{12,4},{4,0},{1,9},{9... | collective-permute-start | bytes 2156552 | tf_op jit(solution)/shard_map/ppermute | solution.py:53
  915.6 33.5 %collective-permute-start.77 = (bf16[1152,256]{1,0:T(8,128)(2,1)}, bf16[1152,256]{1,0:T(8,128)(2,1)}, u32[]{:S(2)}, u32[]{:S(2)}) collective-permute-start(bf16[1152,256]{1,0:T(8,128)(2,1)} %get-tuple-element.189), channel_id=1, source_target_pairs={{0,1},{1,0},{2,3},{3,2},{4,5},{5,4},{6,7},{7,6},{8,9},{9,8},{10,11... | collective-permute-start | bytes 1769480 | tf_op jit(solution)/shard_map/ppermute | solution.py:30
  (318 other events, 3909.4 us)

commit v2 on v1

v2 whole, which is shorter than its diff:
```python
import functools
import math

import jax
import jax.numpy as jnp
import numpy as np
from jax import lax
from jax.experimental import pallas as pl
from jax.experimental.pallas import tpu as pltpu
from jax.sharding import PartitionSpec as P

HEAD = 256
HEADS = 4
PROMPT = 2048
CONT = 256
GROUP = 8
GROUPS_DEV = 4
PSLICE = 256
UNITS = 2
TENSOR = 4

RING = (0, 2, 4, 6, 7, 5, 3, 1)
PLACE = tuple(RING.index(member) for member in range(GROUP))

eps_norm = 1e-06
rope_base = 1000000.0
masked_score = -1e30
score_scale = 1.0 / math.sqrt(HEAD)
bf = jnp.bfloat16
f32 = jnp.float32


def swap_core(value):
    return lax.ppermute(value, "tensor", [(t, t ^ 1) for t in range(TENSOR)])


def swap_x(value):
    return lax.ppermute(value, "tensor", [(t, t ^ 2) for t in range(TENSOR)])


def swap_bit(value, bit):
    size = lax.axis_size("fsdp")
    return lax.ppermute(value, "fsdp", [(f, f ^ bit) for f in range(size)])


def shift_z(value, step):
    pairs = [(z * 2 + y, (z + step) % 4 * 2 + y) for z in range(4) for y in range(2)]
    return lax.ppermute(value, "fsdp", pairs)


def ring_step(value, way):
    size = lax.axis_size("fsdp")
    pairs = []
    for base in range(0, size, GROUP):
        for at in range(GROUP):
            pairs.append((base + RING[at], base + RING[(at + way) % GROUP]))
    return lax.ppermute(value, "fsdp", pairs)


def spread_tensor(own):
    far = swap_x(own)
    near = swap_core(own)
    return own, near, far, swap_core(far)


def spread_near(own):
    return swap_core(own), swap_x(own)


def collect_tensor(part_0, part_1, part_2, part_3):
    return collect_near(part_0, part_1, collect_far(part_2, part_3))


def collect_far(part_2, part_3):
    return (part_2.astype(f32) + swap_core(part_3.astype(bf)).astype(f32)).astype(bf)


def collect_near(part_0, part_1, far):
    far = swap_x(far)
    near = part_0.astype(f32) + swap_core(part_1.astype(bf)).astype(f32)
    return near + far.astype(f32)


def after(value, *earlier):
    return lax.optimization_barrier((value,) + earlier)[0]


def pick(stack, index, axis=0):
    return lax.dynamic_index_in_dim(stack, index, axis, keepdims=False)


def spread_fsdp(own, *earlier):
    if lax.axis_size("fsdp") != GROUP:
        return lax.all_gather(own, "fsdp", axis=0)
    column = jnp.stack([own] + [shift_z(own, step) for step in (1, 2, 3)])
    if earlier:
        column = after(column, *earlier)
    return jnp.concatenate([column, swap_bit(column, 1)])


def collect_fsdp(parts, fsdp_pos):
    if lax.axis_size("fsdp") != GROUP:
        return lax.psum_scatter(parts.astype(bf), "fsdp", scatter_dimension=0).astype(f32)
    z, y = fsdp_pos // 2, fsdp_pos % 2
    paired = parts.reshape((4, 2) + parts.shape[1:])
    give = pick(paired, 1 - y, 1).astype(bf)
    column = pick(paired, y, 1).astype(f32) + swap_bit(give, 1).astype(f32)
    total = pick(column, z)
    for step in (1, 2, 3):
        total = total + shift_z(pick(column, (z + step) % 4).astype(bf), step).astype(f32)
    return total


def order_tensor(blocks, tensor_pos):
    odd = tensor_pos % 2 == 1
    high = tensor_pos // 2 == 1
    a, b, c, d = blocks
    a, b = jnp.where(odd, b, a), jnp.where(odd, a, b)
    c, d = jnp.where(odd, d, c), jnp.where(odd, c, d)
    return (
        jnp.where(high, c, a),
        jnp.where(high, d, b),
        jnp.where(high, a, c),
        jnp.where(high, b, d),
    )


def sum_all(value):
    value = value + swap_core(value)
    value = value + swap_x(value)
    bit = 1
    while bit < lax.axis_size("fsdp"):
        value = value + swap_bit(value, bit)
        bit *= 2
    return value


class Spread:
    def __init__(self, first, second):
        self.firsts, self.seconds = [first], [second]

    def step(self, *earlier):
        first, second = self.firsts[-1], self.seconds[-1]
        if earlier:
            first, second = after(first, *earlier), after(second, *earlier)
        self.firsts.append(ring_step(first, 1))
        self.seconds.append(ring_step(second, -1))
        return self.firsts[-1], self.seconds[-1]


class Collect:
    def __init__(self, take_first, take_second):
        self.take_first, self.take_second = take_first, take_second
        self.at = GROUP - 1
        self.first, self.second = take_first(self.at), take_second(self.at)

    def step(self, *earlier):
        first, second = self.first.astype(bf), self.second.astype(bf)
        if earlier:
            first, second = after(first, *earlier), after(second, *earlier)
        self.at -= 1
        self.first = ring_step(first, -1).astype(f32) + self.take_first(self.at)
        self.second = ring_step(second, 1).astype(f32) + self.take_second(self.at)
        return self.first, self.second


def rms_scale(tensor_in, gain_vec):
    return (
        tensor_in
        * lax.rsqrt(jnp.mean(tensor_in * tensor_in, axis=-1, keepdims=True) + eps_norm)
        * (1.0 + gain_vec)
    )


def rotate(tensor_in, cosine, sine_part):
    half_dim = tensor_in.shape[-1] // 2
    first_half = tensor_in[..., :half_dim]
    second_half = tensor_in[..., half_dim:]
    return jnp.concatenate(
        [
            first_half * cosine - second_half * sine_part,
            second_half * cosine + first_half * sine_part,
        ],
        axis=-1,
    )


def head_prep(raw_in, gain_vec, cosine, sine_part):
    return rotate(rms_scale(raw_in, gain_vec), cosine, sine_part)


def dot_nn(left, right):
    return jnp.dot(left, right, preferred_element_type=f32)


def dot_tn(left, right):
    return lax.dot_general(left, right, (((0,), (0,)), ((), ())), preferred_element_type=f32)


def dot_nt(left, right):
    return lax.dot_general(left, right, (((1,), (1,)), ((), ())), preferred_element_type=f32)


AT_FSDP, AT_TENSOR, AT_REACH, AT_CONT, AT_CORE = 0, 64, 68, 84, 85
TABLE_WIDTH = 128
FAR = 1 << 20


def place_table(members):
    table = np.zeros((members * TENSOR, TABLE_WIDTH), np.int32)
    for f in range(members):
        slot = f % GROUP
        place = PLACE[slot]
        for t in range(TENSOR):
            row = table[f * TENSOR + t]
            for r in range(members):
                if members == GROUP:
                    row[AT_FSDP + r] = (f // 2 - r % 4) % 4 * 2 + (f % 2 ^ r // 4)
                else:
                    row[AT_FSDP + r] = r
            row[AT_TENSOR : AT_TENSOR + TENSOR] = [t ^ j for j in range(TENSOR)]
            for unit in range(UNITS):
                for s in range(GROUP):
                    source = RING[(place - s * (1 - 2 * unit)) % GROUP]
                    reach = FAR if t // 2 else (slot - source) * PSLICE
                    row[AT_REACH + unit * GROUP + s] = reach
            row[AT_CONT], row[AT_CORE] = t // 2, t % 2
    return table


KEYS = PROMPT + CONT
CHUNKS = 2 * UNITS * GROUP
smem = pl.BlockSpec(memory_space=pltpu.SMEM)
anywhere = pl.BlockSpec(memory_space=pl.ANY)


def place_kernel(table, *refs):
    for j in range(TENSOR):
        refs[TENSOR][0, table[AT_TENSOR + j]] = refs[j][0]


def place(table, blocks):
    members, rows, width = blocks[0].shape
    return pl.pallas_call(
        place_kernel,
        out_shape=jax.ShapeDtypeStruct((members, TENSOR, rows, width), bf),
        grid_spec=pltpu.PrefetchScalarGridSpec(
            num_scalar_prefetch=1,
            grid=(members,),
            in_specs=[pl.BlockSpec((1, rows, width), lambda r, table: (r, 0, 0))] * TENSOR,
            out_specs=pl.BlockSpec(
                (1, TENSOR, rows, width), lambda r, table: (table[AT_FSDP + r], 0, 0, 0)
            ),
        ),
        name="place_pairs",
    )(table, *blocks)


def place_heads_kernel(table, *refs):
    query_ref, out_ref = refs[TENSOR:]
    for j in range(TENSOR):
        at = slice(j * HEAD, (j + 1) * HEAD)
        query_ref[0, :, at] = refs[j][0, :, :HEAD]
        out_ref[0, :, at] = refs[j][0, :, HEAD:]


def place_heads(table, blocks):
    members, rows, width = blocks[0].shape
    shape = jax.ShapeDtypeStruct((members, rows, HEADS * HEAD), bf)
    spec = pl.BlockSpec(
        (1, rows, HEADS * HEAD), lambda r, table: (table[AT_FSDP + r], 0, 0)
    )
    return pl.pallas_call(
        place_heads_kernel,
        out_shape=(shape, shape),
        grid_spec=pltpu.PrefetchScalarGridSpec(
            num_scalar_prefetch=1,
            grid=(members,),
            in_specs=[pl.BlockSpec((1, rows, width), lambda r, table: (r, 0, 0))] * TENSOR,
            out_specs=(spec, spec),
        ),
        name="place_heads",
    )(table, *blocks)


def slot_of(table, mapped, unit):
    core = table[AT_CORE]
    target = mapped[core * UNITS + unit]
    other = jnp.where(target // UNITS == core, 0, UNITS)
    return jnp.where(table[AT_CONT] == 1, other + target % UNITS, unit)


def load_pairs(table, mapped, chunks, own_ref, pairs, sems, unit, start):
    slot = slot_of(table, mapped, unit)
    for s in range(GROUP):
        for option in range(2 * UNITS):

            @pl.when(slot == option)
            def _(s=s, option=option):
                copy = pltpu.make_async_copy(
                    chunks[option * GROUP + s],
                    pairs.at[unit, pl.ds(s * PSLICE, PSLICE)],
                    sems.at[unit, s],
                )
                copy.start() if start else copy.wait()

    copy = pltpu.make_async_copy(
        own_ref.at[pl.ds(unit * PSLICE, PSLICE)],
        pairs.at[unit, pl.ds(PROMPT, CONT)],
        sems.at[unit, GROUP],
    )
    copy.start() if start else copy.wait()


def all_pairs(table, mapped, chunks, own_ref, pairs, sems):
    unit, head = pl.program_id(0), pl.program_id(1)

    @pl.when((unit == 0) & (head == 0))
    def _():
        for number in range(UNITS):
            load_pairs(table, mapped, chunks, own_ref, pairs, sems, number, True)

    for number in range(UNITS):

        @pl.when((unit == number) & (head == 0))
        def _(number=number):
            load_pairs(table, mapped, chunks, own_ref, pairs, sems, number, False)


def masked(table, length, scores, unit):
    key_of = lax.broadcasted_iota(jnp.int32, (PSLICE, PSLICE), 0)
    lag = key_of - lax.broadcasted_iota(jnp.int32, (PSLICE, PSLICE), 1)
    parts = []
    for s in range(GROUP):
        reach = table[AT_REACH + unit * GROUP + s]
        part = scores[s * PSLICE : (s + 1) * PSLICE]
        parts.append(jnp.where(lag <= reach, part, masked_score))
    live = length[table[AT_CORE] * UNITS + unit]
    live = jnp.where(table[AT_CONT] == 1, live, 0)
    parts.append(jnp.where((lag <= 0) & (key_of < live), scores[PROMPT:], masked_score))
    return jnp.concatenate(parts, 0)


def attend_kernel(table, mapped, length, query_ref, own_ref, *refs):
    chunks = refs[:CHUNKS]
    out_ref, sum_ref, pairs, values_t, sems = refs[CHUNKS:]
    unit, head = pl.program_id(0), pl.program_id(1)
    all_pairs(table, mapped, chunks, own_ref, pairs, sems)

    @pl.when(head == 0)
    def _():
        values_t[...] = pairs[unit, :, HEAD:].T

    query = query_ref[...] * score_scale
    scores = masked(table, length, dot_nt(pairs[unit, :, :HEAD], query), unit)
    top = jnp.max(scores, axis=0, keepdims=True)
    shifted = jnp.exp(scores - top)
    total = jnp.sum(shifted, axis=0, keepdims=True)
    out = dot_nn(values_t[...], shifted.astype(bf)) / total
    out_ref[...] = out.T.astype(bf)
    sum_ref[0] = top + jnp.log(total)


unit_head = pl.BlockSpec((PSLICE, HEAD), lambda u, h: (u, h))
sum_spec = pl.BlockSpec((1, 1, PSLICE), lambda u, h: (u * HEADS + h, 0, 0))


def attend(table, mapped, length, query, own_pairs, chunks):
    rows = UNITS * PSLICE
    return pl.pallas_call(
        attend_kernel,
        out_shape=(
            jax.ShapeDtypeStruct((rows, HEADS * HEAD), bf),
            jax.ShapeDtypeStruct((UNITS * HEADS, 1, PSLICE), f32),
        ),
        grid=(UNITS, HEADS),
        in_specs=[smem, smem, smem, unit_head, anywhere] + [anywhere] * CHUNKS,
        out_specs=(unit_head, sum_spec),
        scratch_shapes=[
            pltpu.VMEM((UNITS, KEYS, 2 * HEAD), bf),
            pltpu.VMEM((HEAD, KEYS), bf),
            pltpu.SemaphoreType.DMA((UNITS, GROUP + 1)),
        ],
        compiler_params=pltpu.CompilerParams(vmem_limit_bytes=40 << 20),
        cost_estimate=pl.CostEstimate(
            flops=4 * rows * HEADS * KEYS * HEAD,
            bytes_accessed=2 * KEYS * 2 * HEAD * 2 + 4 * rows * HEADS * HEAD,
            transcendentals=rows * HEADS * KEYS,
        ),
        name="attend",
    )(table, mapped, length, query, own_pairs, *chunks)


def attend_back_kernel(table, mapped, length, query_ref, grad_ref, sum_ref, own_ref, *refs):
    chunks = refs[:CHUNKS]
    grad_query_ref, kept_ref, given_ref, grad_own_ref, pairs, keys_t, grads, sems = refs[CHUNKS:]
    unit, head = pl.program_id(0), pl.program_id(1)
    all_pairs(table, mapped, chunks, own_ref, pairs, sems)

    @pl.when(head == 0)
    def _():
        keys_t[...] = pairs[unit, :, :HEAD].T
        grads[unit] = jnp.zeros((KEYS, 2 * HEAD), f32)

    query = query_ref[...] * score_scale
    grad = grad_ref[...]
    scores = masked(table, length, dot_nt(pairs[unit, :, :HEAD], query), unit)
    probs = jnp.exp(scores - sum_ref[0])
    grad_probs = dot_nt(pairs[unit, :, HEAD:], grad)
    row_dot = jnp.sum(probs * grad_probs, axis=0, keepdims=True)
    grad_scores = (probs * (grad_probs - row_dot)).astype(bf)
    grads[unit, :, :HEAD] += dot_nn(grad_scores, query)
    grads[unit, :, HEAD:] += dot_nn(probs.astype(bf), grad)
    grad_query_ref[...] = dot_nn(keys_t[...], grad_scores).T * score_scale

    @pl.when((unit == UNITS - 1) & (head == HEADS - 1))
    def _():
        slots = [slot_of(table, mapped, number) for number in range(UNITS)]
        for s in range(GROUP):
            at = slice(s * PSLICE, (s + 1) * PSLICE)
            for option in range(2 * UNITS):
                total = jnp.zeros((PSLICE, 2 * HEAD), f32)
                for number in range(UNITS):
                    total += jnp.where(slots[number] == option, grads[number, at], 0.0)
                target = kept_ref if option < UNITS else given_ref
                target[option % UNITS, at] = total.astype(bf)
        for number in range(UNITS):
            grad_own_ref[number * PSLICE : (number + 1) * PSLICE] = grads[number, PROMPT:]


def attend_back(table, mapped, length, query, grad, log_sum, own_pairs, chunks):
    rows = UNITS * PSLICE
    whole = pl.BlockSpec(memory_space=pltpu.VMEM)
    return pl.pallas_call(
        attend_back_kernel,
        out_shape=(
            jax.ShapeDtypeStruct((rows, HEADS * HEAD), f32),
            jax.ShapeDtypeStruct((UNITS, PROMPT, 2 * HEAD), bf),
            jax.ShapeDtypeStruct((UNITS, PROMPT, 2 * HEAD), bf),
            jax.ShapeDtypeStruct((rows, 2 * HEAD), f32),
        ),
        grid=(UNITS, HEADS),
        in_specs=[smem, smem, smem, unit_head, unit_head, sum_spec, anywhere]
        + [anywhere] * CHUNKS,
        out_specs=(unit_head, whole, whole, whole),
        scratch_shapes=[
            pltpu.VMEM((UNITS, KEYS, 2 * HEAD), bf),
            pltpu.VMEM((HEAD, KEYS), bf),
            pltpu.VMEM((UNITS, KEYS, 2 * HEAD), f32),
            pltpu.SemaphoreType.DMA((UNITS, GROUP + 1)),
        ],
        compiler_params=pltpu.CompilerParams(vmem_limit_bytes=56 << 20),
        cost_estimate=pl.CostEstimate(
            flops=10 * rows * HEADS * KEYS * HEAD,
            bytes_accessed=2 * KEYS * 2 * HEAD * 6 + 10 * rows * HEADS * HEAD,
            transcendentals=rows * HEADS * KEYS,
        ),
        name="attend_back",
    )(table, mapped, length, query, grad, log_sum, own_pairs, *chunks)


GELU_SCALE = math.sqrt(2.0 / math.pi)
GELU_CUBE = 0.044715


def gelu_parts(gate):
    bent = jnp.tanh(GELU_SCALE * (gate + GELU_CUBE * (gate * gate * gate)))
    return bent, 0.5 * (1.0 + bent)


def whole_weight(ref):
    return ref[...].reshape(-1, ref.shape[-1])


def pick_rows(first_ref, second_ref, rows):
    step = pl.program_id(0)

    @pl.when(step == 0)
    def _():
        rows[...] = first_ref[...]

    @pl.when(step == 1)
    def _():
        rows[...] = second_ref[...]


def put_rows(first_ref, second_ref, total):
    step = pl.program_id(0)

    @pl.when(step == 0)
    def _():
        first_ref[...] = total

    @pl.when(step == 1)
    def _():
        second_ref[...] = total


def feed_kernel(first_ref, second_ref, gate_w, up_w, down_w, *refs):
    gate_ref, up_ref, act_ref, first_out, second_out, rows = refs
    pick_rows(first_ref, second_ref, rows)
    gate = dot_nn(rows[...], whole_weight(gate_w))
    up = dot_nn(rows[...], whole_weight(up_w))
    act = (gate * gelu_parts(gate)[1] * up).astype(bf)
    gate_ref[...] = gate.astype(bf)
    up_ref[...] = up.astype(bf)
    act_ref[...] = act
    put_rows(first_out, second_out, dot_nt(act, whole_weight(down_w)).astype(bf))


def feed_back_kernel(first_ref, second_ref, gate_ref, up_ref, gate_w, up_w, down_w, *refs):
    gate_out, up_out, first_out, second_out, rows = refs
    pick_rows(first_ref, second_ref, rows)
    grad_act = dot_nn(rows[...], whole_weight(down_w))
    gate, up = gate_ref[...].astype(f32), up_ref[...].astype(f32)
    bent, share = gelu_parts(gate)
    slope = share + 0.5 * gate * (1.0 - bent * bent) * (
        GELU_SCALE * (1.0 + 3.0 * GELU_CUBE * (gate * gate))
    )
    grad_gate = (grad_act * up * slope).astype(bf)
    grad_up = (grad_act * (gate * share)).astype(bf)
    gate_out[...] = grad_gate
    up_out[...] = grad_up
    total = dot_nt(grad_gate, whole_weight(gate_w)) + dot_nt(grad_up, whole_weight(up_w))
    put_rows(first_out, second_out, total.astype(bf))


def feed_call(kernel, name, first, second, hiddens, weights, n_out):
    rows, dim = first.shape
    parts, _, depth, hidden = weights.shape
    fixed = pl.BlockSpec((rows, dim), lambda i: (0, 0))
    wide = pl.BlockSpec((rows, hidden), lambda i: (i, 0))
    held = [
        pl.BlockSpec(
            (parts, 1, depth, hidden), lambda i, k=k: (0, k, 0, 0), pipeline_mode=pl.Buffered(1)
        )
        for k in range(3)
    ]
    row_shape = jax.ShapeDtypeStruct((rows, dim), bf)
    wide_shape = jax.ShapeDtypeStruct((2 * rows, hidden), bf)
    return pl.pallas_call(
        kernel,
        out_shape=(wide_shape,) * n_out + (row_shape, row_shape),
        grid=(2,),
        in_specs=[fixed, fixed] + [wide] * len(hiddens) + held,
        out_specs=(wide,) * n_out + (fixed, fixed),
        scratch_shapes=[pltpu.VMEM((rows, dim), bf)],
        compiler_params=pltpu.CompilerParams(vmem_limit_bytes=60 << 20),
        cost_estimate=pl.CostEstimate(
            flops=12 * rows * dim * hidden,
            bytes_accessed=6 * dim * hidden + 2 * rows * hidden * 2 * (n_out + len(hiddens)),
            transcendentals=2 * rows * hidden,
        ),
        name=name,
    )(first, second, *hiddens, weights, weights, weights)


def weight_grad_kernel(number, *refs):
    blocks, halves = refs[:TENSOR], refs[TENSOR : TENSOR + 2 * number]
    out_ref, turned = refs[TENSOR + 2 * number :]
    rows = blocks[0].shape[0]

    @pl.when(pl.program_id(0) == 0)
    def _():
        for j in range(TENSOR):
            turned[:, j * rows : (j + 1) * rows] = blocks[j][...].T

    for k in range(number):
        total = dot_nn(turned[:, : 2 * rows], halves[2 * k][...])
        total += dot_nn(turned[:, 2 * rows :], halves[2 * k + 1][...])
        out_ref[:, k] = total.astype(bf).reshape(out_ref.shape[0], out_ref.shape[2], -1)


def weight_grads(name, blocks, halves, parts):
    rows, dim = blocks[0].shape
    hidden = halves[0].shape[1]
    number = len(halves) // 2
    width = 256
    return pl.pallas_call(
        functools.partial(weight_grad_kernel, number),
        out_shape=jax.ShapeDtypeStruct((parts, number, dim // parts, hidden), bf),
        grid=(pl.cdiv(hidden, width),),
        in_specs=[pl.BlockSpec((rows, dim), lambda i: (0, 0), pipeline_mode=pl.Buffered(1))]
        * TENSOR
        + [pl.BlockSpec((2 * rows, width), lambda i: (0, i))] * (2 * number),
        out_specs=pl.BlockSpec((parts, number, dim // parts, width), lambda i: (0, 0, 0, i)),
        scratch_shapes=[pltpu.VMEM((dim, TENSOR * rows), bf)],
        compiler_params=pltpu.CompilerParams(vmem_limit_bytes=48 << 20),
        cost_estimate=pl.CostEstimate(
            flops=8 * number * rows * dim * hidden,
            bytes_accessed=8 * rows * dim + number * (8 * rows + 2 * dim) * hidden,
            transcendentals=0,
        ),
        name=name,
    )(*blocks, *halves)


def local(
    layer_in,
    teacher,
    query_proj,
    key_proj,
    value_proj,
    out_proj,
    gate_proj,
    up_proj,
    down_proj,
    attn_norm,
    attn_post,
    ffw_norm,
    ffw_post,
    query_norm,
    key_norm,
    cont_prompt,
    cont_length,
    token_count,
    loss_scale,
):
    members = lax.axis_size("fsdp")
    fsdp_pos = lax.axis_index("fsdp")
    tensor_pos = lax.axis_index("tensor")
    core, side = tensor_pos % 2, tensor_pos // 2
    is_cont = side == 1
    group_slot = fsdp_pos % GROUP
    table = lax.dynamic_index_in_dim(
        jnp.asarray(place_table(members)), fsdp_pos * TENSOR + tensor_pos, 0, keepdims=False
    )
    dim = layer_in.shape[1]

    shard_kv = key_proj.shape[0]
    shard_gain, shard_head = attn_norm.shape[0], query_norm.shape[0]
    gains_own = jnp.stack(
        [
            jnp.pad(gain, (0, 2 * HEAD - gain.shape[0]))
            for gain in (attn_norm, attn_post, ffw_norm, ffw_post, query_norm, key_norm)
        ]
    )
    packed = jnp.concatenate([jnp.concatenate([key_proj, value_proj], 1), gains_own], 0)
    packed = jnp.pad(packed, ((0, -packed.shape[0] % 16), (0, 0)))
    packed_all = place(table, spread_tensor(spread_fsdp(packed)))
    kv_full = packed_all[:, :, :shard_kv].reshape(dim, 2 * HEAD)
    gains_all = packed_all[:, :, shard_kv : shard_kv + 6].astype(f32)

    def gain_of(number):
        return gains_all[:, :, number, :shard_gain].reshape(dim)

    def head_gain_of(number):
        return gains_all[:, :, 4 + number, :shard_head].reshape(HEAD)

    attn_gain, attn_post_gain, ffw_gain, ffw_post_gain = (gain_of(k) for k in range(4))
    query_gain, key_gain = head_gain_of(0), head_gain_of(1)

    local_rows = layer_in.shape[0]
    unit_ids = jnp.arange(local_rows, dtype=jnp.int32) % PSLICE
    positions = unit_ids + jnp.where(is_cont, PROMPT, group_slot * PSLICE)
    inverse_freq = jnp.exp(
        -math.log(rope_base) * 2.0 * jnp.arange(HEAD // 2, dtype=f32) / HEAD
    )
    angles = positions.astype(f32)[:, None] * inverse_freq[None, :]
    cosine, sine_part = jnp.cos(angles), jnp.sin(angles)
    input_f = layer_in.astype(f32)
    normed_in = rms_scale(input_f, attn_gain).astype(bf)

    three = (gate_proj, up_proj, down_proj.T)
    if members == GROUP:
        parts = GROUP
        weights = lax.all_gather(jnp.stack(three), "fsdp", axis=0)
    else:
        parts = 1
        weights = jnp.stack([lax.all_gather(w, "fsdp", axis=0, tiled=True) for w in three])[None]

    kv_raw = dot_nn(normed_in, kv_full)
    key_raw = kv_raw[:, :HEAD]
    key_rot = head_prep(key_raw, key_gain, cosine, sine_part).astype(bf)
    own_pairs = jnp.concatenate([key_rot, kv_raw[:, HEAD:].astype(bf)], 1)
    across = lax.ppermute(own_pairs, "tensor", [(0, 2), (1, 3)])
    prompt_pairs = jnp.where(is_cont, across, own_pairs)
    prompts = Spread(prompt_pairs[:PSLICE], prompt_pairs[PSLICE:])
    passed = [prompts.step() for _ in range(GROUP - 1)]
    chunks = prompts.firsts + prompts.seconds
    chunks = chunks + [lax.ppermute(chunk, "tensor", [(2, 3), (3, 2)]) for chunk in chunks]

    qo_own = jnp.concatenate([query_proj, out_proj.T], 1)
    qo_column = after(spread_fsdp(after(qo_own, packed_all), *passed[0]), *passed[2])
    query_full, out_full = (
        part.reshape(dim, HEADS * HEAD)
        for part in place_heads(table, spread_tensor(qo_column))
    )
    query_raw = dot_nn(normed_in, query_full)
    query_heads = [
        head_prep(query_raw[:, h * HEAD : (h + 1) * HEAD], query_gain, cosine, sine_part).astype(bf)
        for h in range(HEADS)
    ]

    query_rot = jnp.concatenate(query_heads, 1)
    attn_low, log_sum = attend(
        table, cont_prompt, cont_length, query_rot, own_pairs, chunks
    )
    attn_sum = dot_nt(attn_low, out_full)
    mixed = input_f + rms_scale(attn_sum, attn_post_gain)
    normed_mid = rms_scale(mixed, ffw_gain).astype(bf)

    mid_near, mid_far = spread_near(normed_mid)
    gate_0, up_0, act_0, *downs = feed_call(
        feed_kernel, "feed", normed_mid, mid_near, (), weights, 3
    )
    mid_last = swap_core(after(mid_far, downs[0]))
    gate_1, up_1, act_1, *more = feed_call(
        feed_kernel, "feed", mid_far, mid_last, (), weights, 3
    )
    downs += more
    ffw_sum = collect_tensor(*downs)
    result = mixed + rms_scale(ffw_sum, ffw_post_gain)

    row_length = jnp.where(
        jnp.arange(local_rows) < PSLICE,
        cont_length[core * UNITS],
        cont_length[core * UNITS + 1],
    )
    live_rows = jnp.where(is_cont & (unit_ids >= row_length), 0.0, 1.0).astype(f32)
    diff = result - teacher.astype(f32)
    loss_part = jnp.sum(live_rows[:, None] * diff * diff)
    count_f = token_count.astype(f32)
    grad_result = loss_scale / count_f * 2.0 * live_rows[:, None] * diff

    _, ffw_pull = jax.vjp(rms_scale, ffw_sum, ffw_post_gain)
    grad_ffw_sum, grad_ffw_post_gain = ffw_pull(grad_result)
    grad_ffw_low = grad_ffw_sum.astype(bf)
    grad_near, grad_far = spread_near(grad_ffw_low)
    gate_low_0, up_low_0, *mids = feed_call(
        feed_back_kernel, "feed_back", grad_ffw_low, grad_near, (gate_0, up_0), weights, 2
    )
    grad_last = swap_core(after(grad_far, mids[0]))
    gate_low_1, up_low_1, *more = feed_call(
        feed_back_kernel, "feed_back", grad_far, grad_last, (gate_1, up_1), weights, 2
    )
    mids += more
    mids_far = collect_far(*mids[2:])
    grad_mid = collect_near(*mids[:2], mids_far)
    down_w = weight_grads(
        "down_grad",
        (after(grad_ffw_low, mids_far), grad_near, grad_far, grad_last),
        (act_0, act_1),
        parts,
    )
    gate_up_w = weight_grads(
        "gate_up_grad",
        (after(normed_mid, mids_far), mid_near, mid_far, mid_last),
        (gate_low_0, gate_low_1, up_low_0, up_low_1),
        parts,
    )
    if parts == GROUP:
        out_down = lax.psum_scatter(down_w, "fsdp", scatter_dimension=0)
        out_gate_up = lax.psum_scatter(gate_up_w, "fsdp", scatter_dimension=0)
    else:
        out_down = lax.psum_scatter(down_w[0], "fsdp", scatter_dimension=1, tiled=True)
        out_gate_up = lax.psum_scatter(gate_up_w[0], "fsdp", scatter_dimension=1, tiled=True)
    out_down = out_down[0].astype(f32).T
    out_gate, out_up = out_gate_up[0].astype(f32), out_gate_up[1].astype(f32)

    _, mid_pull = jax.vjp(rms_scale, mixed, ffw_gain)
    grad_mixed_part, grad_ffw_gain = mid_pull(grad_mid)
    grad_mixed = grad_result + grad_mixed_part
    _, post_pull = jax.vjp(rms_scale, attn_sum, attn_post_gain)
    grad_attn_sum, grad_attn_post_gain = post_pull(grad_mixed)
    grad_attn_low = grad_attn_sum.astype(bf)
    grad_out_w = dot_tn(grad_attn_low, attn_low)
    grad_attn_rows = dot_nn(grad_attn_low, out_full).astype(bf)
    grad_query_rot, kept, given, grad_own = attend_back(
        table, cont_prompt, cont_length, query_rot, grad_attn_rows, log_sum, own_pairs, chunks
    )
    given = lax.ppermute(given, "tensor", [(2, 3), (3, 2)])
    kept = kept.astype(f32) + given.astype(f32)
    pair_sums = Collect(
        lambda s: kept[0, s * PSLICE : (s + 1) * PSLICE],
        lambda s: kept[1, s * PSLICE : (s + 1) * PSLICE],
    )
    for _ in range(GROUP - 1):
        last_sums = pair_sums.step()
    summed = jnp.concatenate(last_sums, 0)
    back = lax.ppermute(summed.astype(bf), "tensor", [(2, 0), (3, 1)]).astype(f32)
    grad_pairs = jnp.where(is_cont, grad_own, summed + back)

    _, query_pull = jax.vjp(
        lambda raw, gain: tuple(
            head_prep(raw[:, h * HEAD : (h + 1) * HEAD], gain, cosine, sine_part)
            for h in range(HEADS)
        ),
        query_raw,
        query_gain,
    )
    grad_query_raw, grad_query_gain = query_pull(
        tuple(grad_query_rot[:, h * HEAD : (h + 1) * HEAD] for h in range(HEADS))
    )
    _, key_pull = jax.vjp(
        lambda raw, gain: head_prep(raw, gain, cosine, sine_part), key_raw, key_gain
    )
    grad_key_raw, grad_key_gain = key_pull(grad_pairs[:, :HEAD])
    grad_query_low = grad_query_raw.astype(bf)
    grad_kv_low = jnp.concatenate([grad_key_raw, grad_pairs[:, HEAD:]], 1).astype(bf)
    grad_query_w = dot_tn(normed_in, grad_query_low)
    grad_kv_w = dot_tn(normed_in, grad_kv_low)
    grad_normed = dot_nt(grad_query_low, query_full) + dot_nt(grad_kv_low, kv_full)
    _, input_pull = jax.vjp(rms_scale, input_f, attn_gain)
    grad_input_part, grad_attn_gain = input_pull(grad_normed)
    grad_input = grad_mixed + grad_input_part

    qo_sum = collect_tensor(
        *(
            jnp.concatenate(
                [grad_query_w[:, h * HEAD : (h + 1) * HEAD], grad_out_w[:, h * HEAD : (h + 1) * HEAD]],
                1,
            )
            for h in range(HEADS)
        )
    ).reshape(members, dim // members, 2 * HEAD)
    out_qo = collect_fsdp(after(qo_sum, summed), fsdp_pos)
    out_query, out_out = out_qo[:, :HEAD], out_qo[:, HEAD:].T
    kv_blocks = grad_kv_w.reshape(members, TENSOR, shard_kv, 2 * HEAD)
    kv_column = collect_tensor(
        *order_tensor([kv_blocks[:, t] for t in range(TENSOR)], tensor_pos)
    )
    out_kv = collect_fsdp(kv_column, fsdp_pos)

    small = jnp.concatenate(
        [
            grad_attn_gain,
            grad_attn_post_gain,
            grad_ffw_gain,
            grad_ffw_post_gain,
            grad_query_gain,
            grad_key_gain,
            loss_part[None],
        ]
    )
    length = small.shape[0]
    small = jnp.pad(small, (0, -length % 1024)).reshape(-1, 128)
    small = sum_all(small).reshape(-1)
    device = fsdp_pos * TENSOR + tensor_pos
    wide = [
        lax.dynamic_slice(small, (k * dim + device * shard_gain,), (shard_gain,)) for k in range(4)
    ]
    narrow = [
        lax.dynamic_slice(small, (4 * dim + k * HEAD + device * shard_head,), (shard_head,))
        for k in range(2)
    ]
    loss = small[length - 1] / count_f
    return (
        result.astype(bf),
        loss,
        grad_input.astype(bf),
        out_query,
        out_kv[:, :HEAD],
        out_kv[:, HEAD:],
        out_out,
        out_gate,
        out_up,
        out_down,
        *wide,
        *narrow,
    )


def solution(mesh):
    rows = P(("fsdp", "tensor"), None)
    split = P(("fsdp", "tensor"))
    inward, outward = P("fsdp", "tensor"), P("tensor", "fsdp")
    return jax.shard_map(
        local,
        mesh=mesh,
        in_specs=(
            rows,
            rows,
            inward,
            rows,
            rows,
            outward,
            inward,
            inward,
            outward,
            *(split,) * 6,
            P("fsdp"),
            P("fsdp"),
            P(),
            P(),
        ),
        out_specs=(
            rows,
            P(),
            rows,
            inward,
            rows,
            rows,
            outward,
            inward,
            inward,
            outward,
            *(split,) * 6,
        ),
        check_vma=False,
    )
```

time: 978 us -> 826 us (0.84)
  Pallas kernels: 0 us -> 206 us
  matrix products: 225 us -> 21.5 us
  local copies, waits for them, and re-layouts: 132 us -> 40.3 us
  between operations: 55.2 us -> 20.3 us
  other arithmetic: 103 us -> 85.3 us
  waiting for transfers between devices: 329 us -> 315 us
    pallas_call x0 -> x10, Pallas kernels: none -> 206 us  [the longest x4 102 us: feed_call(): pl.pallas_call(kernel, out_shape=(wide_shape,) * n_out + (row_shape, row_...]
    dot_general x13 -> x3, matrix products: 87.8 us -> 8.24 us  [dot_nn(): return jnp.dot(left, right, preferred_element_type=f32)]
    dot_general x10 -> x3, matrix products: 69.5 us -> 5.58 us  [dot_tn(): lax.dot_general(left, right, (((0,), (0,)), ((), ())), preferred_element_...]
    dot_general x13 -> x3, matrix products: 67.8 us -> 7.72 us  [dot_nt(): lax.dot_general(left, right, (((1,), (1,)), ((), ())), preferred_element_...]
    dynamic_update_slice x32 -> x0, local copies, waits for them, and re-layouts: 40.1 us -> none  [the longest x8 10.9 us: local(): lax.dynamic_update_slice(up_full, seconds[s][:rows], (at_second, 0))]
    ppermute x10 -> x9, waiting for transfers between devices: 97.4 us -> 63.4 us  [swap_x(): return lax.ppermute(value, 'tensor', [(t, t ^ 2) for t in range(TENSOR)])]
    ppermute x15 -> x12, waiting for transfers between devices: 2.37 us -> 24.8 us  [shift_z(): return lax.ppermute(value, 'fsdp', pairs)]
    ppermute x56 -> x28, starting transfers between devices: 58.5 us -> 37 us  [ring_step(): return lax.ppermute(value, 'fsdp', pairs)]
  transfers between devices with their start and end apart: 112 -> 95, of which waited for: 48 -> 50; matrix products, arithmetic and copies ran while one was open for 32% -> 14% of each run, Pallas kernels for 0% -> 17%
where the time goes in v2:
time: 826 us; the launch traced here: 816 us
  waiting for transfers between devices  315 us (38%)
  Pallas kernels  206 us (25%)
  starting transfers between devices  128 us (15%)
  other arithmetic  85.3 us (10%)
  local copies, waits for them, and re-layouts  40.3 us (5%)
  matrix products  21.5 us (3%)
  between operations  20.3 us (2%)
    ppermute x28, waiting for transfers between devices, ring_step(): return lax.ppermute(value, 'fsdp', pairs)  180 us
    pallas_call x4, Pallas kernels, feed_call(): pl.pallas_call(kernel, out_shape=(wide_shape,) * n_out + (row_shape, row_...  102 us
    ppermute x9, waiting for transfers between devices, swap_x(): return lax.ppermute(value, 'tensor', [(t, t ^ 2) for t in range(TENSOR)])  63.4 us
    ppermute x28, starting transfers between devices, ring_step(): return lax.ppermute(value, 'fsdp', pairs)  37 us
    pallas_call x2, Pallas kernels, weight_grads(): pl.pallas_call(functools.partial(weight_grad_kernel, number), out_shape=j...  36.7 us
    pallas_call x1, Pallas kernels, attend_back(): pl.pallas_call(attend_back_kernel, out_shape=(jax.ShapeDtypeStruct((rows,...  33.6 us
    ppermute x7, starting transfers between devices, swap_bit(): return lax.ppermute(value, 'fsdp', [(f, f ^ bit) for f in range(size)])  29.4 us
    ppermute x12, waiting for transfers between devices, shift_z(): return lax.ppermute(value, 'fsdp', pairs)  24.8 us
  transfers between devices with their start and end apart: 95, of which 50 were waited for; matrix products, arithmetic and copies ran while one was open for 14% of the time, Pallas kernels for 17%

profile of v2, /device:TPU:0, one launch (start us, length us, event | category | flops | bytes accessed | tf_op | source)
XLA Modules:
  0.0 816.2 jit_solution(1673399684704449233)
XLA Ops:
  79.3 9.1 %collective-permute-done.11.refs_1_ = bf16[256,512]{1,0:T(8,128)(2,1)S(1)} collective-permute-done((bf16[256,512]{1,0:T(8,128)(2,1)S(1)}, bf16[256,512]{1,0:T(8,128)(2,1)S(1)}, u32[]{:S(2)}, u32[]{:S(2)}) %collective-permute-start.11) | collective-permute-done | bytes 262176 | tf_op jit(solution)/shard_map/ppermute | solution.py:57
  97.1 26.1 %collective-permute-done.14.refs_2_ = bf16[256,512]{1,0:T(8,128)(2,1)S(1)} collective-permute-done((bf16[256,512]{1,0:T(8,128)(2,1)S(1)}, bf16[256,512]{1,0:T(8,128)(2,1)S(1)}, u32[]{:S(2)}, u32[]{:S(2)}) %collective-permute-start.14) | collective-permute-done | bytes 262176 | tf_op jit(solution)/shard_map/ppermute | solution.py:57
  127.6 9.5 %collective-permute-done.15.refs_3_ = bf16[256,512]{1,0:T(8,128)(2,1)S(1)} collective-permute-done((bf16[256,512]{1,0:T(8,128)(2,1)S(1)}, bf16[256,512]{1,0:T(8,128)(2,1)S(1)}, u32[]{:S(2)}, u32[]{:S(2)}) %collective-permute-start.15) | collective-permute-done | bytes 262176 | tf_op jit(solution)/shard_map/ppermute | solution.py:57
  145.4 26.7 %collective-permute-done.19.refs_2_ = bf16[8,144,512]{2,1,0:T(8,128)(2,1)} collective-permute-done((bf16[8,144,512]{2,1,0:T(8,128)(2,1)}, bf16[8,144,512]{2,1,0:T(8,128)(2,1)}, u32[]{:S(2)}, u32[]{:S(2)}) %collective-permute-start.19) | collective-permute-done | bytes 1179680 | tf_op jit(solution)/shard_map/ppermute | solution.py:38
  193.4 12.8 %collective-permute-done.25.refs_12_ = bf16[256,512]{1,0:T(8,128)(2,1)} collective-permute-done((bf16[256,512]{1,0:T(8,128)(2,1)S(1)}, bf16[256,512]{1,0:T(8,128)(2,1)}, u32[]{:S(2)}, u32[]{:S(2)}) %collective-permute-start.25) | collective-permute-done | bytes 262176 | tf_op jit(solution)/shard_map/ppermute | solution.py:57
  241.8 19.9 %attend.1 = (bf16[512,1024]{1,0:T(8,128)(2,1)S(1)}, f32[8,1,256]{2,1,0:T(1,128)S(1)}) custom-call(s32[128]{0:T(128)S(1)} %copy-done.17, s32[4]{0:T(128)S(1)} %copy-done.52, s32[4]{0:T(128)S(1)} %copy-done.16, bf16[512,1024]{1,0:T(8,128)(2,1)S(1)} %fusion.130.query_ref, bf16[512,512]{1,0:T(8,128)(2,1)S(1)} %pad_maximum_fusion.6.own_ref, ...), custom_call_target="tpu_custom_call" | custom-call | flops 4831838208 | bytes 6815744 | tf_op jit(solution)/shard_map/attend/pallas_call | solution.py:370
  266.9 8.7 %collective-permute-start.47 = (bf16[512,1152]{1,0:T(8,128)(2,1)S(1)}, bf16[512,1152]{1,0:T(8,128)(2,1)}, u32[]{:S(2)}, u32[]{:S(2)}) collective-permute-start(bf16[512,1152]{1,0:T(8,128)(2,1)S(1)} %multiply_convert_fusion.first_ref.refs_0_), channel_id=1, source_target_pairs={{0,2},{1,3},{2,0},{3,1},{4,6},{5,7},{6,4},{7,5},{8,10},{9,11},{10,... | collective-permute-start | bytes 3538952 | tf_op jit(solution)/shard_map/ppermute | solution.py:38
  276.7 24.2 %feed.2 = (bf16[1024,1728]{1,0:T(8,128)(2,1)}, bf16[1024,1728]{1,0:T(8,128)(2,1)}, bf16[1024,1728]{1,0:T(8,128)(2,1)}, bf16[512,1152]{1,0:T(8,128)(2,1)}, bf16[512,1152]{1,0:T(8,128)(2,1)}) custom-call(bf16[512,1152]{1,0:T(8,128)(2,1)} %copy-done.8, bf16[512,1152]{1,0:T(8,128)(2,1)} %copy-done.18, bf16[8,3,144,1728]{3,2,1,0:T(8,128)(2,1)} %bitcast.265, ...), custom_call_target="tpu_custom_call" | custom-call | flops 12230590464 | bytes 22560768 | tf_op jit(solution)/shard_map/feed/pallas_call | solution.py:541
  306.3 23.9 %feed.3 = (bf16[1024,1728]{1,0:T(8,128)(2,1)}, bf16[1024,1728]{1,0:T(8,128)(2,1)}, bf16[1024,1728]{1,0:T(8,128)(2,1)}, bf16[512,1152]{1,0:T(8,128)(2,1)}, bf16[512,1152]{1,0:T(8,128)(2,1)}) custom-call(bf16[512,1152]{1,0:T(8,128)(2,1)} %collective-permute-done.47.first_ref.refs_2_, bf16[512,1152]{1,0:T(8,128)(2,1)} %copy-done.20, ...), custom_call_target="tpu_custom_call" | custom-call | flops 12230590464 | bytes 22560768 | tf_op jit(solution)/shard_map/feed/pallas_call | solution.py:541
  343.2 21.4 %collective-permute-done.50 = bf16[512,1152]{1,0:T(8,128)(2,1)} collective-permute-done((bf16[512,1152]{1,0:T(8,128)(2,1)}, bf16[512,1152]{1,0:T(8,128)(2,1)}, u32[]{:S(2)}, u32[]{:S(2)}) %collective-permute-start.50) | collective-permute-done | bytes 1179680 | tf_op jit(solution)/shard_map/ppermute | solution.py:38
  379.2 26.6 %feed_back.2 = (bf16[1024,1728]{1,0:T(8,128)(2,1)}, bf16[1024,1728]{1,0:T(8,128)(2,1)}, bf16[512,1152]{1,0:T(8,128)(2,1)}, bf16[512,1152]{1,0:T(8,128)(2,1)}) custom-call(bf16[512,1152]{1,0:T(8,128)(2,1)} %copy-done, bf16[512,1152]{1,0:T(8,128)(2,1)} %copy-done.2, bf16[1024,1728]{1,0:T(8,128)(2,1)} %get-tuple-element.61.gate_ref, ...), custom_call_target="tpu_custom_call" | custom-call | flops 12230590464 | bytes 26099712 | tf_op jit(solution)/shard_map/feed_back/pallas_call | solution.py:541
  409.9 26.9 %feed_back.3 = (bf16[1024,1728]{1,0:T(8,128)(2,1)}, bf16[1024,1728]{1,0:T(8,128)(2,1)}, bf16[512,1152]{1,0:T(8,128)(2,1)}, bf16[512,1152]{1,0:T(8,128)(2,1)}) custom-call(bf16[512,1152]{1,0:T(8,128)(2,1)} %copy-done.4, bf16[512,1152]{1,0:T(8,128)(2,1)} %copy-done.6, bf16[1024,1728]{1,0:T(8,128)(2,1)} %get-tuple-element.66.gate_ref, ...), custom_call_target="tpu_custom_call" | custom-call | flops 12230590464 | bytes 26099712 | tf_op jit(solution)/shard_map/feed_back/pallas_call | solution.py:541
  443.8 13.4 %down_grad.1 = bf16[8,1,144,1728]{3,2,1,0:T(8,128)(2,1)} custom-call(bf16[512,1152]{1,0:T(8,128)(2,1)S(1)} %copy-done.1, bf16[512,1152]{1,0:T(8,128)(2,1)S(1)} %copy-done.3, bf16[512,1152]{1,0:T(8,128)(2,1)S(1)} %copy-done.5, bf16[512,1152]{1,0:T(8,128)(2,1)S(1)} %copy-done.7, bf16[1024,1728]{1,0:T(8,128)(2,1)} %get-tuple-element.82.refs_4_, ...), custom_call_target="tpu_custom_call" | custom-call | flops 8153726976 | bytes 15777792 | tf_op jit(solution)/shard_map/down_grad/pallas_call | solution.py:579
  459.2 23.3 %gate_up_grad.1 = bf16[8,2,144,1728]{3,2,1,0:T(8,128)(2,1)} custom-call(bf16[512,1152]{1,0:T(8,128)(2,1)S(1)} %copy-done.9, bf16[512,1152]{1,0:T(8,128)(2,1)S(1)} %copy-done.19, bf16[512,1152]{1,0:T(8,128)(2,1)} %collective-permute-done.47.first_ref.refs_2_, bf16[512,1152]{1,0:T(8,128)(2,1)S(1)} %copy-done.21, bf16[1024,1728]{1,0:T(8,128)(2,1)} %get-tuple-element.77.refs_4_, ...), custom_call_target="tpu_custom_call" | custom-call | flops 16307453952 | bytes 26836992 | tf_op jit(solution)/shard_map/gate_up_grad/pallas_call | solution.py:579
  499.0 33.6 %attend_back.1 = (f32[512,1024]{1,0:T(8,128)}, bf16[2,2048,512]{2,1,0:T(8,128)(2,1)}, bf16[2,2048,512]{2,1,0:T(8,128)(2,1)}, f32[512,512]{1,0:T(8,128)}) custom-call(s32[128]{0:T(128)} %fusion.160.table, s32[4]{0:T(128)} %mapped.3, s32[4]{0:T(128)} %length.3, bf16[512,1024]{1,0:T(8,128)(2,1)} %copy-done.15, ...), custom_call_target="tpu_custom_call" | custom-call | flops 12079595520 | bytes 19398656 | tf_op jit(solution)/shard_map/attend_back/pallas_call | solution.py:434
  562.0 16.4 %collective-permute-done.58 = bf16[256,512]{1,0:T(8,128)(2,1)S(1)} collective-permute-done((bf16[256,512]{1,0:T(8,128)(2,1)S(1)}, bf16[256,512]{1,0:T(8,128)(2,1)S(1)}, u32[]{:S(2)}, u32[]{:S(2)}) %collective-permute-start.58) | collective-permute-done | bytes 262176 | tf_op jit(solution)/shard_map/ppermute | solution.py:57
  585.3 13.3 %collective-permute-done.59 = bf16[256,512]{1,0:T(8,128)(2,1)S(1)} collective-permute-done((bf16[256,512]{1,0:T(8,128)(2,1)S(1)}, bf16[256,512]{1,0:T(8,128)(2,1)S(1)}, u32[]{:S(2)}, u32[]{:S(2)}) %collective-permute-start.59) | collective-permute-done | bytes 262176 | tf_op jit(solution)/shard_map/ppermute | solution.py:57
  600.9 18.1 %collective-permute-done.60 = bf16[256,512]{1,0:T(8,128)(2,1)S(1)} collective-permute-done((bf16[256,512]{1,0:T(8,128)(2,1)S(1)}, bf16[256,512]{1,0:T(8,128)(2,1)S(1)}, u32[]{:S(2)}, u32[]{:S(2)}) %collective-permute-start.60) | collective-permute-done | bytes 262176 | tf_op jit(solution)/shard_map/ppermute | solution.py:57
  621.2 18.6 %collective-permute-done.61 = bf16[256,512]{1,0:T(8,128)(2,1)S(1)} collective-permute-done((bf16[256,512]{1,0:T(8,128)(2,1)S(1)}, bf16[256,512]{1,0:T(8,128)(2,1)S(1)}, u32[]{:S(2)}, u32[]{:S(2)}) %collective-permute-start.61) | collective-permute-done | bytes 262176 | tf_op jit(solution)/shard_map/ppermute | solution.py:57
  660.8 25.2 %collective-permute-done.63 = bf16[256,512]{1,0:T(8,128)(2,1)S(1)} collective-permute-done((bf16[256,512]{1,0:T(8,128)(2,1)S(1)}, bf16[256,512]{1,0:T(8,128)(2,1)S(1)}, u32[]{:S(2)}, u32[]{:S(2)}) %collective-permute-start.63) | collective-permute-done | bytes 262176 | tf_op jit(solution)/shard_map/ppermute | solution.py:57
  701.0 9.5 %collective-permute-done.83 = bf16[144,512]{1,0:T(8,128)(2,1)S(1)} collective-permute-done((bf16[144,512]{1,0:T(8,128)(2,1)S(1)}, bf16[144,512]{1,0:T(8,128)(2,1)S(1)}, u32[]{:S(2)}, u32[]{:S(2)}) %collective-permute-start.83) | collective-permute-done | bytes 147488 | tf_op jit(solution)/shard_map/ppermute | solution.py:48
  712.6 8.0 collective-permute-done.71
  725.9 8.5 %collective-permute-done.72 = bf16[512,512]{1,0:T(8,128)(2,1)} collective-permute-done((bf16[512,512]{1,0:T(8,128)(2,1)S(1)}, bf16[512,512]{1,0:T(8,128)(2,1)}, u32[]{:S(2)}, u32[]{:S(2)}) %collective-permute-start.72) | collective-permute-done | bytes 524320 | tf_op jit(solution)/shard_map/ppermute | solution.py:781
  764.0 16.0 %collective-permute-start.76 = (f32[48,128]{1,0:T(8,128)S(1)}, f32[48,128]{1,0:T(8,128)S(1)}, u32[]{:S(2)}, u32[]{:S(2)}) collective-permute-start(f32[48,128]{1,0:T(8,128)S(1)} %add.578), channel_id=1, source_target_pairs={{0,8},{4,12},{8,0},{12,4},{16,24},{20,28},{24,16},{28,20},{1,9},{5... | collective-permute-start | bytes 73736 | tf_op jit(solution)/shard_map/ppermute | solution.py:43
  (654 shorter events, 356.2 us)
Async XLA Ops:
  7.3 268.4 %all-gather.3.cloned.1.call-start = ((), (), s32[]{:S(2)}) async-start(), calls=%async_computation.4 | async-start | bytes 13934592 | tf_op jit(solution)/shard_map/all_gather | solution.py:667
  10.0 713.8 %reduce-scatter.5.cloned.1.call-start = ((), (), s32[]{:S(2)}) async-start(), calls=%async_computation.3 | async-start | bytes 4644864 | tf_op jit(solution)/shard_map/reduce_scatter | solution.py:753
  89.4 37.1 %collective-permute-start.13 = (bf16[4,144,512]{2,1,0:T(8,128)(2,1)S(1)}, bf16[4,144,512]{2,1,0:T(8,128)(2,1)S(1)}, u32[]{:S(2)}, u32[]{:S(2)}) collective-permute-start(bf16[4,144,512]{2,1,0:T(8,128)(2,1)S(1)} %pad_maximum_fusion.5), channel_id=1, source_target_pairs={{0,4},{4,0},{8,12},{12,8},{16,20},{20,16},{24,28},{28,24},{1,5},{5... | collective-permute-start | bytes 1769480 | tf_op jit(solution)/shard_map/ppermute | solution.py:43
  91.2 32.1 %collective-permute-start.14 = (bf16[256,512]{1,0:T(8,128)(2,1)S(1)}, bf16[256,512]{1,0:T(8,128)(2,1)S(1)}, u32[]{:S(2)}, u32[]{:S(2)}) collective-permute-start(bf16[256,512]{1,0:T(8,128)(2,1)S(1)} %collective-permute-done.11.refs_1_), channel_id=1, source_target_pairs={{0,8},{8,16},{16,24},{24,28},{28,20},{20,12},{12,4},{4,0},{1,9},{9... | collective-permute-start | bytes 786440 | tf_op jit(solution)/shard_map/ppermute | solution.py:57
  97.1 26.9 %collective-permute-start.16 = (bf16[256,512]{1,0:T(8,128)(2,1)S(1)}, bf16[256,512]{1,0:T(8,128)(2,1)S(1)}, u32[]{:S(2)}, u32[]{:S(2)}) collective-permute-start(bf16[256,512]{1,0:T(8,128)(2,1)S(1)} %collective-permute-done.12.refs_9_), channel_id=1, source_target_pairs={{0,4},{8,0},{16,8},{24,16},{28,24},{20,28},{12,20},{4,12},{1,5},{9... | collective-permute-start | bytes 786440 | tf_op jit(solution)/shard_map/ppermute | solution.py:57
  144.9 27.2 %collective-permute-start.19 = (bf16[8,144,512]{2,1,0:T(8,128)(2,1)}, bf16[8,144,512]{2,1,0:T(8,128)(2,1)}, u32[]{:S(2)}, u32[]{:S(2)}) collective-permute-start(bf16[8,144,512]{2,1,0:T(8,128)(2,1)} %pad_maximum_fusion.1.refs_0_), channel_id=1, source_target_pairs={{0,2},{1,3},{2,0},{3,1},{4,6},{5,7},{6,4},{7,5},{8,10},{9,11},{10,... | collective-permute-start | bytes 3538952 | tf_op jit(solution)/shard_map/ppermute | solution.py:38
  145.4 29.8 %collective-permute-start.18 = (bf16[8,144,512]{2,1,0:T(8,128)(2,1)}, bf16[8,144,512]{2,1,0:T(8,128)(2,1)}, u32[]{:S(2)}, u32[]{:S(2)}) collective-permute-start(bf16[8,144,512]{2,1,0:T(8,128)(2,1)} %pad_maximum_fusion.1.refs_0_), channel_id=1, source_target_pairs={{0,1},{1,0},{2,3},{3,2},{4,5},{5,4},{6,7},{7,6},{8,9},{9,8},{10,11... | collective-permute-start | bytes 3538952 | tf_op jit(solution)/shard_map/ppermute | solution.py:34
  173.8 34.8 %collective-permute-start.30 = (bf16[256,512]{1,0:T(8,128)(2,1)S(1)}, bf16[256,512]{1,0:T(8,128)(2,1)}, u32[]{:S(2)}, u32[]{:S(2)}) collective-permute-start(bf16[256,512]{1,0:T(8,128)(2,1)S(1)} %collective-permute-done.11.refs_1_), channel_id=1, source_target_pairs={{2,3},{3,2},{6,7},{7,6},{10,11},{11,10},{14,15},{15,14},{18,19},{1... | collective-permute-start | bytes 786440 | tf_op jit(solution)/shard_map/ppermute | solution.py:681
  175.3 30.9 %collective-permute-start.25 = (bf16[256,512]{1,0:T(8,128)(2,1)S(1)}, bf16[256,512]{1,0:T(8,128)(2,1)}, u32[]{:S(2)}, u32[]{:S(2)}) collective-permute-start(bf16[256,512]{1,0:T(8,128)(2,1)S(1)} %collective-permute-done.17.refs_11_), channel_id=1, source_target_pairs={{0,4},{8,0},{16,8},{24,16},{28,24},{20,28},{12,20},{4,12},{1,5},{9... | collective-permute-start | bytes 786440 | tf_op jit(solution)/shard_map/ppermute | solution.py:57
  266.9 35.3 %collective-permute-start.47 = (bf16[512,1152]{1,0:T(8,128)(2,1)S(1)}, bf16[512,1152]{1,0:T(8,128)(2,1)}, u32[]{:S(2)}, u32[]{:S(2)}) collective-permute-start(bf16[512,1152]{1,0:T(8,128)(2,1)S(1)} %multiply_convert_fusion.first_ref.refs_0_), channel_id=1, source_target_pairs={{0,2},{1,3},{2,0},{3,1},{4,6},{5,7},{6,4},{7,5},{8,10},{9,11},{10,... | collective-permute-start | bytes 3538952 | tf_op jit(solution)/shard_map/ppermute | solution.py:38
  336.2 28.3 %collective-permute-start.50 = (bf16[512,1152]{1,0:T(8,128)(2,1)}, bf16[512,1152]{1,0:T(8,128)(2,1)}, u32[]{:S(2)}, u32[]{:S(2)}) collective-permute-start(bf16[512,1152]{1,0:T(8,128)(2,1)} %add_convert_fusion.1), channel_id=1, source_target_pairs={{0,2},{1,3},{2,0},{3,1},{4,6},{5,7},{6,4},{7,5},{8,10},{9,11},{10,... | collective-permute-start | bytes 3538952 | tf_op jit(solution)/shard_map/ppermute | solution.py:38
  375.3 30.6 %collective-permute-start.53 = (bf16[512,1152]{1,0:T(8,128)(2,1)S(1)}, bf16[512,1152]{1,0:T(8,128)(2,1)S(1)}, u32[]{:S(2)}, u32[]{:S(2)}) collective-permute-start(bf16[512,1152]{1,0:T(8,128)(2,1)S(1)} %fusion.4.first_ref.refs_0_), channel_id=1, source_target_pairs={{0,2},{1,3},{2,0},{3,1},{4,6},{5,7},{6,4},{7,5},{8,10},{9,11},{10,... | collective-permute-start | bytes 3538952 | tf_op jit(solution)/shard_map/ppermute | solution.py:38
  457.2 348.3 %reduce-scatter.3.cloned.1.call-start = ((), (), s32[]{:S(2)}) async-start(), calls=%async_computation.2 | async-start | bytes 9289728 | tf_op jit(solution)/shard_map/reduce_scatter | solution.py:754
  457.3 25.4 %collective-permute-start.52 = (bf16[512,1152]{1,0:T(8,128)(2,1)}, bf16[512,1152]{1,0:T(8,128)(2,1)}, u32[]{:S(2)}, u32[]{:S(2)}) collective-permute-start(bf16[512,1152]{1,0:T(8,128)(2,1)} %get-tuple-element.64), channel_id=1, source_target_pairs={{0,1},{1,0},{2,3},{3,2},{4,5},{5,4},{6,7},{7,6},{8,9},{9,8},{10,11... | collective-permute-start | bytes 3538952 | tf_op jit(solution)/shard_map/ppermute | solution.py:34
  457.5 28.6 %collective-permute-start.56 = (bf16[512,1152]{1,0:T(8,128)(2,1)}, bf16[512,1152]{1,0:T(8,128)(2,1)}, u32[]{:S(2)}, u32[]{:S(2)}) collective-permute-start(bf16[512,1152]{1,0:T(8,128)(2,1)} %add_convert_fusion), channel_id=1, source_target_pairs={{0,2},{1,3},{2,0},{3,1},{4,6},{5,7},{6,4},{7,5},{8,10},{9,11},{10,... | collective-permute-start | bytes 3538952 | tf_op jit(solution)/shard_map/ppermute | solution.py:38
  544.3 99.0 %collective-permute-start.78 = (bf16[1152,512]{0,1:T(8,128)(2,1)}, bf16[1152,512]{0,1:T(8,128)(2,1)}, u32[]{:S(2)}, u32[]{:S(2)}) collective-permute-start(bf16[1152,512]{0,1:T(8,128)(2,1)} %pad_maximum_fusion.2), channel_id=1, source_target_pairs={{0,1},{1,0},{2,3},{3,2},{4,5},{5,4},{6,7},{7,6},{8,9},{9,8},{10,11... | collective-permute-start | bytes 3538952 | tf_op jit(solution)/shard_map/ppermute | solution.py:34
  545.5 33.0 %collective-permute-start.79 = (bf16[1152,512]{0,1:T(8,128)(2,1)}, bf16[1152,512]{0,1:T(8,128)(2,1)}, u32[]{:S(2)}, u32[]{:S(2)}) collective-permute-start(bf16[1152,512]{0,1:T(8,128)(2,1)} %pad_maximum_fusion.3), channel_id=1, source_target_pairs={{0,1},{1,0},{2,3},{3,2},{4,5},{5,4},{6,7},{7,6},{8,9},{9,8},{10,11... | collective-permute-start | bytes 3538952 | tf_op jit(solution)/shard_map/ppermute | solution.py:34
  562.0 23.3 %collective-permute-start.65 = (bf16[256,512]{1,0:T(8,128)(2,1)S(1)}, bf16[256,512]{1,0:T(8,128)(2,1)S(1)}, u32[]{:S(2)}, u32[]{:S(2)}) collective-permute-start(bf16[256,512]{1,0:T(8,128)(2,1)S(1)} %get-tuple-element.140), channel_id=1, source_target_pairs={{0,8},{8,16},{16,24},{24,28},{28,20},{20,12},{12,4},{4,0},{1,9},{9... | collective-permute-start | bytes 786440 | tf_op jit(solution)/shard_map/ppermute | solution.py:57
  581.1 62.2 %collective-permute-start.80 = (bf16[1152,512]{0,1:T(8,128)(2,1)}, bf16[1152,512]{0,1:T(8,128)(2,1)}, u32[]{:S(2)}, u32[]{:S(2)}) collective-permute-start(bf16[1152,512]{0,1:T(8,128)(2,1)} %fusion.13), channel_id=1, source_target_pairs={{0,2},{1,3},{2,0},{3,1},{4,6},{5,7},{6,4},{7,5},{8,10},{9,11},{10,... | collective-permute-start | bytes 3538952 | tf_op jit(solution)/shard_map/ppermute | solution.py:38
  651.6 38.3 %collective-permute-start.81 = (bf16[4,144,512]{2,1,0:T(8,128)(2,1)S(1)}, bf16[4,144,512]{2,1,0:T(8,128)(2,1)S(1)}, u32[]{:S(2)}, u32[]{:S(2)}) collective-permute-start(bf16[4,144,512]{2,1,0:T(8,128)(2,1)S(1)} %fusion.20), channel_id=1, source_target_pairs={{0,4},{4,0},{8,12},{12,8},{16,20},{20,16},{24,28},{28,24},{1,5},{5... | collective-permute-start | bytes 1769480 | tf_op jit(solution)/shard_map/ppermute | solution.py:43
  658.7 27.2 %collective-permute-start.63 = (bf16[256,512]{1,0:T(8,128)(2,1)S(1)}, bf16[256,512]{1,0:T(8,128)(2,1)S(1)}, u32[]{:S(2)}, u32[]{:S(2)}) collective-permute-start(bf16[256,512]{1,0:T(8,128)(2,1)S(1)} %get-tuple-element.125), channel_id=1, source_target_pairs={{0,4},{8,0},{16,8},{24,16},{28,24},{20,28},{12,20},{4,12},{1,5},{9... | collective-permute-start | bytes 786440 | tf_op jit(solution)/shard_map/ppermute | solution.py:57
  658.7 27.2 %collective-permute-start.69 = (bf16[256,512]{1,0:T(8,128)(2,1)S(1)}, bf16[256,512]{1,0:T(8,128)(2,1)S(1)}, u32[]{:S(2)}, u32[]{:S(2)}) collective-permute-start(bf16[256,512]{1,0:T(8,128)(2,1)S(1)} %get-tuple-element.126), channel_id=1, source_target_pairs={{0,8},{8,16},{16,24},{24,28},{28,20},{20,12},{12,4},{4,0},{1,9},{9... | collective-permute-start | bytes 786440 | tf_op jit(solution)/shard_map/ppermute | solution.py:57
  751.7 30.1 %collective-permute-start.86 = (bf16[8,36,512]{2,1,0:T(8,128)(2,1)S(1)}, bf16[8,36,512]{2,1,0:T(8,128)(2,1)S(1)}, u32[]{:S(2)}, u32[]{:S(2)}) collective-permute-start(bf16[8,36,512]{2,1,0:T(8,128)(2,1)S(1)} %fusion.93), channel_id=1, source_target_pairs={{0,1},{1,0},{2,3},{3,2},{4,5},{5,4},{6,7},{7,6},{8,9},{9,8},{10,11... | collective-permute-start | bytes 884744 | tf_op jit(solution)/shard_map/ppermute | solution.py:34
  751.9 35.2 %collective-permute-start.85 = (bf16[8,36,512]{2,1,0:T(8,128)(2,1)S(1)}, bf16[8,36,512]{2,1,0:T(8,128)(2,1)S(1)}, u32[]{:S(2)}, u32[]{:S(2)}) collective-permute-start(bf16[8,36,512]{2,1,0:T(8,128)(2,1)S(1)} %fusion.92), channel_id=1, source_target_pairs={{0,1},{1,0},{2,3},{3,2},{4,5},{5,4},{6,7},{7,6},{8,9},{9,8},{10,11... | collective-permute-start | bytes 884744 | tf_op jit(solution)/shard_map/ppermute | solution.py:34
  (226 other events, 4357.0 us)
Sparse Core Ops, SparseCore 0:
  10.3 226.8 all-gather.2
  457.3 88.3 reduce-scatter.4
  549.8 193.4 reduce-scatter.2

commit v3 on v2

--- a/solution.py
+++ b/solution.py
@@ -89,12 +89,15 @@
     return lax.dynamic_index_in_dim(stack, index, axis, keepdims=False)
 
 
-def spread_fsdp(own, *earlier):
+def spread_z(own):
     if lax.axis_size("fsdp") != GROUP:
-        return lax.all_gather(own, "fsdp", axis=0)
-    column = jnp.stack([own] + [shift_z(own, step) for step in (1, 2, 3)])
-    if earlier:
-        column = after(column, *earlier)
+        return own
+    return jnp.stack([own] + [shift_z(own, step) for step in (1, 2, 3)])
+
+
+def spread_y(column):
+    if lax.axis_size("fsdp") != GROUP:
+        return lax.all_gather(column, "fsdp", axis=0)
     return jnp.concatenate([column, swap_bit(column, 1)])
 
 
@@ -148,22 +151,6 @@
         return self.firsts[-1], self.seconds[-1]
 
 
-class Collect:
-    def __init__(self, take_first, take_second):
-        self.take_first, self.take_second = take_first, take_second
-        self.at = GROUP - 1
-        self.first, self.second = take_first(self.at), take_second(self.at)
-
-    def step(self, *earlier):
-        first, second = self.first.astype(bf), self.second.astype(bf)
-        if earlier:
-            first, second = after(first, *earlier), after(second, *earlier)
-        self.at -= 1
-        self.first = ring_step(first, -1).astype(f32) + self.take_first(self.at)
-        self.second = ring_step(second, 1).astype(f32) + self.take_second(self.at)
-        return self.first, self.second
-
-
 def rms_scale(tensor_in, gain_vec):
     return (
         tensor_in
@@ -201,7 +188,7 @@
     return lax.dot_general(left, right, (((1,), (1,)), ((), ())), preferred_element_type=f32)
 
 
-AT_FSDP, AT_TENSOR, AT_REACH, AT_CONT, AT_CORE = 0, 64, 68, 84, 85
+AT_FSDP, AT_TENSOR, AT_REACH, AT_CONT, AT_CORE, AT_RING = 0, 64, 68, 84, 85, 88
 TABLE_WIDTH = 128
 FAR = 1 << 20
 
@@ -222,14 +209,15 @@
             for unit in range(UNITS):
                 for s in range(GROUP):
                     source = RING[(place - s * (1 - 2 * unit)) % GROUP]
-                    reach = FAR if t // 2 else (slot - source) * PSLICE
-                    row[AT_REACH + unit * GROUP + s] = reach
+                    row[AT_RING + unit * GROUP + s] = source
+            for s in range(GROUP):
+                source = s if members == GROUP else RING[(place - s) % GROUP]
+                row[AT_REACH + s] = FAR if t // 2 else (slot - source) * PSLICE
             row[AT_CONT], row[AT_CORE] = t // 2, t % 2
     return table
 
 
 KEYS = PROMPT + CONT
-CHUNKS = 2 * UNITS * GROUP
 smem = pl.BlockSpec(memory_space=pltpu.SMEM)
 anywhere = pl.BlockSpec(memory_space=pl.ANY)
 
@@ -290,41 +278,43 @@
     return jnp.where(table[AT_CONT] == 1, other + target % UNITS, unit)
 
 
-def load_pairs(table, mapped, chunks, own_ref, pairs, sems, unit, start):
+def load_pairs(table, mapped, sources, own_ref, pairs, sems, unit, start):
     slot = slot_of(table, mapped, unit)
-    for s in range(GROUP):
-        for option in range(2 * UNITS):
-
-            @pl.when(slot == option)
-            def _(s=s, option=option):
-                copy = pltpu.make_async_copy(
-                    chunks[option * GROUP + s],
-                    pairs.at[unit, pl.ds(s * PSLICE, PSLICE)],
-                    sems.at[unit, s],
-                )
-                copy.start() if start else copy.wait()
+    for option in range(2 * UNITS):
+
+        @pl.when(slot == option)
+        def _(option=option):
+            rows = pl.ds(option % UNITS * PSLICE, PSLICE)
+            copy = pltpu.make_async_copy(
+                sources[option // UNITS].at[:, rows],
+                pairs.at[unit, pl.ds(0, GROUP)],
+                sems.at[unit, 0],
+            )
+            copy.start() if start else copy.wait()
 
     copy = pltpu.make_async_copy(
-        own_ref.at[pl.ds(unit * PSLICE, PSLICE)],
-        pairs.at[unit, pl.ds(PROMPT, CONT)],
-        sems.at[unit, GROUP],
+        own_ref.at[pl.ds(unit * PSLICE, PSLICE)], pairs.at[unit, GROUP], sems.at[unit, 1]
     )
     copy.start() if start else copy.wait()
 
 
-def all_pairs(table, mapped, chunks, own_ref, pairs, sems):
+def pair_half(pairs, unit, half):
+    return pairs[unit, :, :, half * HEAD : (half + 1) * HEAD].reshape(KEYS, HEAD)
+
+
+def all_pairs(table, mapped, sources, own_ref, pairs, sems):
     unit, head = pl.program_id(0), pl.program_id(1)
 
     @pl.when((unit == 0) & (head == 0))
     def _():
         for number in range(UNITS):
-            load_pairs(table, mapped, chunks, own_ref, pairs, sems, number, True)
+            load_pairs(table, mapped, sources, own_ref, pairs, sems, number, True)
 
     for number in range(UNITS):
 
         @pl.when((unit == number) & (head == 0))
         def _(number=number):
-            load_pairs(table, mapped, chunks, own_ref, pairs, sems, number, False)
+            load_pairs(table, mapped, sources, own_ref, pairs, sems, number, False)
 
 
 def masked(table, length, scores, unit):
@@ -332,7 +322,7 @@
     lag = key_of - lax.broadcasted_iota(jnp.int32, (PSLICE, PSLICE), 1)
     parts = []
     for s in range(GROUP):
-        reach = table[AT_REACH + unit * GROUP + s]
+        reach = table[AT_REACH + s]
         part = scores[s * PSLICE : (s + 1) * PSLICE]
         parts.append(jnp.where(lag <= reach, part, masked_score))
     live = length[table[AT_CORE] * UNITS + unit]
@@ -342,17 +332,17 @@
 
 
 def attend_kernel(table, mapped, length, query_ref, own_ref, *refs):
-    chunks = refs[:CHUNKS]
-    out_ref, sum_ref, pairs, values_t, sems = refs[CHUNKS:]
+    sources = refs[:2]
+    out_ref, sum_ref, pairs, values_t, sems = refs[2:]
     unit, head = pl.program_id(0), pl.program_id(1)
-    all_pairs(table, mapped, chunks, own_ref, pairs, sems)
+    all_pairs(table, mapped, sources, own_ref, pairs, sems)
 
     @pl.when(head == 0)
     def _():
-        values_t[...] = pairs[unit, :, HEAD:].T
+        values_t[...] = pair_half(pairs, unit, 1).T
 
     query = query_ref[...] * score_scale
-    scores = masked(table, length, dot_nt(pairs[unit, :, :HEAD], query), unit)
+    scores = masked(table, length, dot_nt(pair_half(pairs, unit, 0), query), unit)
     top = jnp.max(scores, axis=0, keepdims=True)
     shifted = jnp.exp(scores - top)
     total = jnp.sum(shifted, axis=0, keepdims=True)
@@ -365,7 +355,7 @@
 sum_spec = pl.BlockSpec((1, 1, PSLICE), lambda u, h: (u * HEADS + h, 0, 0))
 
 
-def attend(table, mapped, length, query, own_pairs, chunks):
+def attend(table, mapped, length, query, own_pairs, sources):
     rows = UNITS * PSLICE
     return pl.pallas_call(
         attend_kernel,
@@ -374,12 +364,12 @@
             jax.ShapeDtypeStruct((UNITS * HEADS, 1, PSLICE), f32),
         ),
         grid=(UNITS, HEADS),
-        in_specs=[smem, smem, smem, unit_head, anywhere] + [anywhere] * CHUNKS,
+        in_specs=[smem, smem, smem, unit_head] + [anywhere] * 3,
         out_specs=(unit_head, sum_spec),
         scratch_shapes=[
-            pltpu.VMEM((UNITS, KEYS, 2 * HEAD), bf),
+            pltpu.VMEM((UNITS, GROUP + 1, PSLICE, 2 * HEAD), bf),
             pltpu.VMEM((HEAD, KEYS), bf),
-            pltpu.SemaphoreType.DMA((UNITS, GROUP + 1)),
+            pltpu.SemaphoreType.DMA((UNITS, 2)),
         ],
         compiler_params=pltpu.CompilerParams(vmem_limit_bytes=40 << 20),
         cost_estimate=pl.CostEstimate(
@@ -388,25 +378,25 @@
             transcendentals=rows * HEADS * KEYS,
         ),
         name="attend",
-    )(table, mapped, length, query, own_pairs, *chunks)
+    )(table, mapped, length, query, own_pairs, *sources)
 
 
 def attend_back_kernel(table, mapped, length, query_ref, grad_ref, sum_ref, own_ref, *refs):
-    chunks = refs[:CHUNKS]
-    grad_query_ref, kept_ref, given_ref, grad_own_ref, pairs, keys_t, grads, sems = refs[CHUNKS:]
+    sources = refs[:2]
+    grad_query_ref, grad_own_ref, *targets, pairs, keys_t, grads, sems = refs[-8:]
     unit, head = pl.program_id(0), pl.program_id(1)
-    all_pairs(table, mapped, chunks, own_ref, pairs, sems)
+    all_pairs(table, mapped, sources, own_ref, pairs, sems)
 
     @pl.when(head == 0)
     def _():
-        keys_t[...] = pairs[unit, :, :HEAD].T
+        keys_t[...] = pair_half(pairs, unit, 0).T
         grads[unit] = jnp.zeros((KEYS, 2 * HEAD), f32)
 
     query = query_ref[...] * score_scale
     grad = grad_ref[...]
-    scores = masked(table, length, dot_nt(pairs[unit, :, :HEAD], query), unit)
+    scores = masked(table, length, dot_nt(pair_half(pairs, unit, 0), query), unit)
     probs = jnp.exp(scores - sum_ref[0])
-    grad_probs = dot_nt(pairs[unit, :, HEAD:], grad)
+    grad_probs = dot_nt(pair_half(pairs, unit, 1), grad)
     row_dot = jnp.sum(probs * grad_probs, axis=0, keepdims=True)
     grad_scores = (probs * (grad_probs - row_dot)).astype(bf)
     grads[unit, :, :HEAD] += dot_nn(grad_scores, query)
@@ -422,32 +412,31 @@
                 total = jnp.zeros((PSLICE, 2 * HEAD), f32)
                 for number in range(UNITS):
                     total += jnp.where(slots[number] == option, grads[number, at], 0.0)
-                target = kept_ref if option < UNITS else given_ref
-                target[option % UNITS, at] = total.astype(bf)
+                rows = pl.ds(option % UNITS * PSLICE, PSLICE)
+                targets[option // UNITS][s, rows] = total.astype(bf)
         for number in range(UNITS):
             grad_own_ref[number * PSLICE : (number + 1) * PSLICE] = grads[number, PROMPT:]
 
 
-def attend_back(table, mapped, length, query, grad, log_sum, own_pairs, chunks):
+def attend_back(table, mapped, length, query, grad, log_sum, own_pairs, sources, earlier):
     rows = UNITS * PSLICE
     whole = pl.BlockSpec(memory_space=pltpu.VMEM)
     return pl.pallas_call(
         attend_back_kernel,
         out_shape=(
             jax.ShapeDtypeStruct((rows, HEADS * HEAD), f32),
-            jax.ShapeDtypeStruct((UNITS, PROMPT, 2 * HEAD), bf),
-            jax.ShapeDtypeStruct((UNITS, PROMPT, 2 * HEAD), bf),
             jax.ShapeDtypeStruct((rows, 2 * HEAD), f32),
-        ),
+        )
+        + (jax.ShapeDtypeStruct((GROUP, UNITS * PSLICE, 2 * HEAD), bf),) * 2,
         grid=(UNITS, HEADS),
-        in_specs=[smem, smem, smem, unit_head, unit_head, sum_spec, anywhere]
-        + [anywhere] * CHUNKS,
-        out_specs=(unit_head, whole, whole, whole),
+        in_specs=[smem, smem, smem, unit_head, unit_head, sum_spec]
+        + [anywhere] * (3 + len(earlier)),
+        out_specs=(unit_head,) + (whole,) * 3,
         scratch_shapes=[
-            pltpu.VMEM((UNITS, KEYS, 2 * HEAD), bf),
+            pltpu.VMEM((UNITS, GROUP + 1, PSLICE, 2 * HEAD), bf),
             pltpu.VMEM((HEAD, KEYS), bf),
             pltpu.VMEM((UNITS, KEYS, 2 * HEAD), f32),
-            pltpu.SemaphoreType.DMA((UNITS, GROUP + 1)),
+            pltpu.SemaphoreType.DMA((UNITS, 2)),
         ],
         compiler_params=pltpu.CompilerParams(vmem_limit_bytes=56 << 20),
         cost_estimate=pl.CostEstimate(
@@ -456,7 +445,7 @@
             transcendentals=rows * HEADS * KEYS,
         ),
         name="attend_back",
-    )(table, mapped, length, query, grad, log_sum, own_pairs, *chunks)
+    )(table, mapped, length, query, grad, log_sum, own_pairs, *sources, *earlier)
 
 
 GELU_SCALE = math.sqrt(2.0 / math.pi)
@@ -468,8 +457,41 @@
     return bent, 0.5 * (1.0 + bent)
 
 
-def whole_weight(ref):
-    return ref[...].reshape(-1, ref.shape[-1])
+CUT = 80
+
+
+def weight_copies(table, pieces, held, sems):
+    copies = ([], [], [])
+
+    def add(kind, source, target):
+        number = sum(len(kept) for kept in copies)
+        copies[kind].append(pltpu.make_async_copy(source, target, sems.at[number]))
+
+    if len(pieces) == 1:
+        for kind in range(3):
+            add(kind, pieces[0].at[kind], held[kind])
+        return copies
+    shard = held[0].shape[0] // GROUP
+    for way in range(2):
+        for s in range(GROUP):
+            piece = pieces[way * GROUP + s]
+            start = pl.multiple_of(table[AT_RING + way * GROUP + s] * shard, 16)
+            low, high = ((0, CUT), (CUT, shard))[way]
+            add(way, piece.at[pl.ds(0, shard)], held[way].at[pl.ds(start, shard)])
+            add(
+                2,
+                piece.at[pl.ds(shard, high - low)],
+                held[2].at[pl.ds(pl.multiple_of(start + low, 16), high - low)],
+            )
+    return copies
+
+
+def bring(copies, kinds, start):
+    @pl.when(pl.program_id(0) == 0)
+    def _():
+        for kind in kinds:
+            for copy in copies[kind]:
+                copy.start() if start else copy.wait()
 
 
 def pick_rows(first_ref, second_ref, rows):
@@ -496,55 +518,65 @@
         second_ref[...] = total
 
 
-def feed_kernel(first_ref, second_ref, gate_w, up_w, down_w, *refs):
-    gate_ref, up_ref, act_ref, first_out, second_out, rows = refs
+def feed_kernel(n_pieces, table, first_ref, second_ref, *refs):
+    pieces, refs = refs[:n_pieces], refs[n_pieces:]
+    gate_ref, up_ref, act_ref, first_out, second_out, rows, gate_w, up_w, down_w, sems = refs
+    copies = weight_copies(table, pieces, (gate_w, up_w, down_w), sems)
+    bring(copies, (0, 1, 2), True)
     pick_rows(first_ref, second_ref, rows)
-    gate = dot_nn(rows[...], whole_weight(gate_w))
-    up = dot_nn(rows[...], whole_weight(up_w))
+    bring(copies, (0,), False)
+    gate = dot_nn(rows[...], gate_w[...])
+    bring(copies, (1,), False)
+    up = dot_nn(rows[...], up_w[...])
     act = (gate * gelu_parts(gate)[1] * up).astype(bf)
     gate_ref[...] = gate.astype(bf)
     up_ref[...] = up.astype(bf)
     act_ref[...] = act
-    put_rows(first_out, second_out, dot_nt(act, whole_weight(down_w)).astype(bf))
-
-
-def feed_back_kernel(first_ref, second_ref, gate_ref, up_ref, gate_w, up_w, down_w, *refs):
-    gate_out, up_out, first_out, second_out, rows = refs
+    bring(copies, (2,), False)
+    put_rows(first_out, second_out, dot_nt(act, down_w[...]).astype(bf))
+
+
+def feed_back_kernel(n_pieces, table, first_ref, second_ref, gate_ref, up_ref, *refs):
+    pieces, refs = refs[:n_pieces], refs[n_pieces:]
+    gate_out, up_out, first_out, second_out, rows, gate_w, up_w, down_w, sems = refs
+    copies = weight_copies(table, pieces, (gate_w, up_w, down_w), sems)
+    bring(copies, (2, 0, 1), True)
     pick_rows(first_ref, second_ref, rows)
-    grad_act = dot_nn(rows[...], whole_weight(down_w))
-    gate, up = gate_ref[...].astype(f32), up_ref[...].astype(f32)
-    bent, share = gelu_parts(gate)
-    slope = share + 0.5 * gate * (1.0 - bent * bent) * (
-        GELU_SCALE * (1.0 + 3.0 * GELU_CUBE * (gate * gate))
-    )
-    grad_gate = (grad_act * up * slope).astype(bf)
-    grad_up = (grad_act * (gate * share)).astype(bf)
-    gate_out[...] = grad_gate
-    up_out[...] = grad_up
-    total = dot_nt(grad_gate, whole_weight(gate_w)) + dot_nt(grad_up, whole_weight(up_w))
+    bring(copies, (2, 0, 1), False)
+    total = jnp.zeros(rows.shape, f32)
+    hidden = gate_ref.shape[1]
+    for low in range(0, hidden, 512):
+        at = slice(low, min(low + 512, hidden))
+        grad_act = dot_nn(rows[...], down_w[:, at])
+        gate, up = gate_ref[:, at].astype(f32), up_ref[:, at].astype(f32)
+        bent, share = gelu_parts(gate)
+        slope = share + 0.5 * gate * (1.0 - bent * bent) * (
+            GELU_SCALE * (1.0 + 3.0 * GELU_CUBE * (gate * gate))
+        )
+        grad_gate = (grad_act * up * slope).astype(bf)
+        grad_up = (grad_act * (gate * share)).astype(bf)
+        gate_out[:, at] = grad_gate
+        up_out[:, at] = grad_up
+        total += dot_nt(grad_gate, gate_w[:, at]) + dot_nt(grad_up, up_w[:, at])
     put_rows(first_out, second_out, total.astype(bf))
 
 
-def feed_call(kernel, name, first, second, hiddens, weights, n_out):
+def feed_call(kernel, name, table, first, second, hiddens, pieces, n_out):
     rows, dim = first.shape
-    parts, _, depth, hidden = weights.shape
+    hidden = pieces[0].shape[-1]
     fixed = pl.BlockSpec((rows, dim), lambda i: (0, 0))
     wide = pl.BlockSpec((rows, hidden), lambda i: (i, 0))
-    held = [
-        pl.BlockSpec(
-            (parts, 1, depth, hidden), lambda i, k=k: (0, k, 0, 0), pipeline_mode=pl.Buffered(1)
-        )
-        for k in range(3)
-    ]
     row_shape = jax.ShapeDtypeStruct((rows, dim), bf)
     wide_shape = jax.ShapeDtypeStruct((2 * rows, hidden), bf)
     return pl.pallas_call(
-        kernel,
+        functools.partial(kernel, len(pieces)),
         out_shape=(wide_shape,) * n_out + (row_shape, row_shape),
         grid=(2,),
-        in_specs=[fixed, fixed] + [wide] * len(hiddens) + held,
+        in_specs=[smem, fixed, fixed] + [wide] * len(hiddens) + [anywhere] * len(pieces),
         out_specs=(wide,) * n_out + (fixed, fixed),
-        scratch_shapes=[pltpu.VMEM((rows, dim), bf)],
+        scratch_shapes=[pltpu.VMEM((rows, dim), bf)]
+        + [pltpu.VMEM((dim, hidden), bf)] * 3
+        + [pltpu.SemaphoreType.DMA((max(3, 2 * len(pieces)),))],
         compiler_params=pltpu.CompilerParams(vmem_limit_bytes=60 << 20),
         cost_estimate=pl.CostEstimate(
             flops=12 * rows * dim * hidden,
@@ -552,7 +584,64 @@
             transcendentals=2 * rows * hidden,
         ),
         name=name,
-    )(first, second, *hiddens, weights, weights, weights)
+    )(table, first, second, *hiddens, *pieces)
+
+
+def pass_on_kernel(moved, last, table, *refs):
+    if moved:
+        first_ref, second_ref, refs = refs[0], refs[1], refs[2:]
+    gate_ref, up_ref, down_first, down_second = refs[:4]
+    outs = refs[-3:] if last else refs[-2:]
+    shard = gate_ref.shape[2]
+    gate, up = gate_ref[0, 0].astype(f32), up_ref[0, 0].astype(f32)
+    low, high = down_first[0, 0, :CUT].astype(f32), down_second[0, 0, CUT:].astype(f32)
+    if moved:
+        gate += first_ref[:shard].astype(f32)
+        low += first_ref[shard:].astype(f32)
+        up += second_ref[:shard].astype(f32)
+        high += second_ref[shard:].astype(f32)
+    if last:
+        outs[0][...] = gate
+        outs[1][...] = up
+        outs[2][:CUT] = low
+        outs[2][CUT:] = high
+    else:
+        outs[0][:shard] = gate.astype(bf)
+        outs[0][shard:] = low.astype(bf)
+        outs[1][:shard] = up.astype(bf)
+        outs[1][shard:] = high.astype(bf)
+
+
+def pass_on(table, moved, gate_up_w, down_w, s, earlier=()):
+    _, _, shard, hidden = gate_up_w.shape
+    width = 896
+    last = s == 0
+
+    def block(rows):
+        return pl.BlockSpec((rows, width), lambda i, table: (0, i))
+
+    def term(way, kind):
+        return pl.BlockSpec(
+            (1, 1, shard, width),
+            lambda i, table: (table[AT_RING + way * GROUP + s], kind, 0, i),
+        )
+
+    heights = (shard,) * 3 if last else (shard + CUT, 2 * shard - CUT)
+    kind = f32 if last else bf
+    return pl.pallas_call(
+        functools.partial(pass_on_kernel, len(moved), last),
+        out_shape=tuple(jax.ShapeDtypeStruct((rows, hidden), kind) for rows in heights),
+        grid_spec=pltpu.PrefetchScalarGridSpec(
+            num_scalar_prefetch=1,
+            grid=(pl.cdiv(hidden, width),),
+            in_specs=[block(part.shape[0]) for part in moved]
+            + [term(0, 0), term(1, 1), term(0, 0), term(1, 0)]
+            + [anywhere] * len(earlier),
+            out_specs=tuple(block(rows) for rows in heights),
+        ),
+        compiler_params=pltpu.CompilerParams(vmem_limit_bytes=60 << 20),
+        name="pass_on",
+    )(table, *moved, gate_up_w, gate_up_w, down_w, down_w, *earlier)
 
 
 def weight_grad_kernel(number, *refs):
@@ -587,8 +676,8 @@
         scratch_shapes=[pltpu.VMEM((dim, TENSOR * rows), bf)],
         compiler_params=pltpu.CompilerParams(vmem_limit_bytes=48 << 20),
         cost_estimate=pl.CostEstimate(
-            flops=8 * number * rows * dim * hidden,
-            bytes_accessed=8 * rows * dim + number * (8 * rows + 2 * dim) * hidden,
+            flops=3 * number * rows * dim * hidden,
+            bytes_accessed=4 * rows * dim + number * (4 * rows + 2 * dim) * hidden,
             transcendentals=0,
         ),
         name=name,
@@ -627,6 +716,23 @@
     )
     dim = layer_in.shape[1]
 
+    ringed = members == GROUP
+    down_own = down_proj.T
+    if ringed:
+        parts = GROUP
+        weights = Spread(
+            jnp.concatenate([gate_proj, down_own[:CUT]], 0),
+            jnp.concatenate([up_proj, down_own[CUT:]], 0),
+        )
+        for _ in range(GROUP - 1):
+            weights.step()
+        came = list(zip(weights.firsts, weights.seconds, strict=True))
+    else:
+        came = [()] * GROUP
+        parts = 1
+        pieces = (gate_proj, up_proj, down_own)
+        pieces = [jnp.stack([lax.all_gather(w, "fsdp", axis=0, tiled=True) for w in pieces])]
+
     shard_kv = key_proj.shape[0]
     shard_gain, shard_head = attn_norm.shape[0], query_norm.shape[0]
     gains_own = jnp.stack(
@@ -637,7 +743,10 @@
     )
     packed = jnp.concatenate([jnp.concatenate([key_proj, value_proj], 1), gains_own], 0)
     packed = jnp.pad(packed, ((0, -packed.shape[0] % 16), (0, 0)))
-    packed_all = place(table, spread_tensor(spread_fsdp(packed)))
+    packed_f = spread_y(spread_z(packed))
+    packed_all = place(table, spread_tensor(packed_f))
+    qo_own = jnp.concatenate([query_proj, out_proj.T], 1)
+    qo_column = spread_z(after(qo_own, packed_f))
     kv_full = packed_all[:, :, :shard_kv].reshape(dim, 2 * HEAD)
     gains_all = packed_all[:, :, shard_kv : shard_kv + 6].astype(f32)
 
@@ -661,30 +770,28 @@
     input_f = layer_in.astype(f32)
     normed_in = rms_scale(input_f, attn_gain).astype(bf)
 
-    three = (gate_proj, up_proj, down_proj.T)
-    if members == GROUP:
-        parts = GROUP
-        weights = lax.all_gather(jnp.stack(three), "fsdp", axis=0)
-    else:
-        parts = 1
-        weights = jnp.stack([lax.all_gather(w, "fsdp", axis=0, tiled=True) for w in three])[None]
-
     kv_raw = dot_nn(normed_in, kv_full)
     key_raw = kv_raw[:, :HEAD]
     key_rot = head_prep(key_raw, key_gain, cosine, sine_part).astype(bf)
     own_pairs = jnp.concatenate([key_rot, kv_raw[:, HEAD:].astype(bf)], 1)
+    own_pairs = after(own_pairs, qo_column, *came[1])
+    qo_column = spread_y(after(qo_column, packed_all))
     across = lax.ppermute(own_pairs, "tensor", [(0, 2), (1, 3)])
-    prompt_pairs = jnp.where(is_cont, across, own_pairs)
-    prompts = Spread(prompt_pairs[:PSLICE], prompt_pairs[PSLICE:])
-    passed = [prompts.step() for _ in range(GROUP - 1)]
-    chunks = prompts.firsts + prompts.seconds
-    chunks = chunks + [lax.ppermute(chunk, "tensor", [(2, 3), (3, 2)]) for chunk in chunks]
-
-    qo_own = jnp.concatenate([query_proj, out_proj.T], 1)
-    qo_column = after(spread_fsdp(after(qo_own, packed_all), *passed[0]), *passed[2])
+    prompt_pairs = after(jnp.where(is_cont, across, own_pairs), qo_column, *came[2])
+    if ringed:
+        held_pairs = lax.all_gather(prompt_pairs, "fsdp", axis=0)
+    else:
+        held_pairs = [prompt_pairs]
+        while len(held_pairs) < GROUP:
+            held_pairs.append(ring_step(held_pairs[-1], 1))
+        held_pairs = jnp.stack(held_pairs)
+    qo_column = after(qo_column, across)
+    qo_near, qo_far = spread_near(qo_column)
     query_full, out_full = (
         part.reshape(dim, HEADS * HEAD)
-        for part in place_heads(table, spread_tensor(qo_column))
+        for part in place_heads(
+            table, (after(qo_column, *came[4]), qo_near, qo_far, swap_core(after(qo_far, *came[3])))
+        )
     )
     query_raw = dot_nn(normed_in, query_full)
     query_heads = [
@@ -693,20 +800,24 @@
     ]
 
     query_rot = jnp.concatenate(query_heads, 1)
+    held_pairs = after(held_pairs, query_rot, *came[6])
+    sources = held_pairs, lax.ppermute(held_pairs, "tensor", [(2, 3), (3, 2)])
     attn_low, log_sum = attend(
-        table, cont_prompt, cont_length, query_rot, own_pairs, chunks
+        table, cont_prompt, cont_length, query_rot, own_pairs, sources
     )
     attn_sum = dot_nt(attn_low, out_full)
+    if ringed:
+        pieces = weights.firsts + weights.seconds
     mixed = input_f + rms_scale(attn_sum, attn_post_gain)
     normed_mid = rms_scale(mixed, ffw_gain).astype(bf)
 
     mid_near, mid_far = spread_near(normed_mid)
     gate_0, up_0, act_0, *downs = feed_call(
-        feed_kernel, "feed", normed_mid, mid_near, (), weights, 3
+        feed_kernel, "feed", table, normed_mid, mid_near, (), pieces, 3
     )
     mid_last = swap_core(after(mid_far, downs[0]))
     gate_1, up_1, act_1, *more = feed_call(
-        feed_kernel, "feed", mid_far, mid_last, (), weights, 3
+        feed_kernel, "feed", table, mid_far, mid_last, (), pieces, 3
     )
     downs += more
     ffw_sum = collect_tensor(*downs)
@@ -728,11 +839,11 @@
     grad_ffw_low = grad_ffw_sum.astype(bf)
     grad_near, grad_far = spread_near(grad_ffw_low)
     gate_low_0, up_low_0, *mids = feed_call(
-        feed_back_kernel, "feed_back", grad_ffw_low, grad_near, (gate_0, up_0), weights, 2
+        feed_back_kernel, "feed_back", table, grad_ffw_low, grad_near, (gate_0, up_0), pieces, 2
     )
     grad_last = swap_core(after(grad_far, mids[0]))
     gate_low_1, up_low_1, *more = feed_call(
-        feed_back_kernel, "feed_back", grad_far, grad_last, (gate_1, up_1), weights, 2
+        feed_back_kernel, "feed_back", table, grad_far, grad_last, (gate_1, up_1), pieces, 2
     )
     mids += more
     mids_far = collect_far(*mids[2:])
@@ -749,14 +860,21 @@
         (gate_low_0, gate_low_1, up_low_0, up_low_1),
         parts,
     )
-    if parts == GROUP:
-        out_down = lax.psum_scatter(down_w, "fsdp", scatter_dimension=0)
-        out_gate_up = lax.psum_scatter(gate_up_w, "fsdp", scatter_dimension=0)
+    if ringed:
+        held_sums = pass_on(table, (), gate_up_w, down_w, GROUP - 1)
+
+        def move_sums():
+            return ring_step(held_sums[0], -1), ring_step(held_sums[1], 1)
+
+        def add_sums(moved, s, *earlier):
+            return pass_on(table, moved, gate_up_w, down_w, s, earlier)
+
     else:
-        out_down = lax.psum_scatter(down_w[0], "fsdp", scatter_dimension=1, tiled=True)
-        out_gate_up = lax.psum_scatter(gate_up_w[0], "fsdp", scatter_dimension=1, tiled=True)
-    out_down = out_down[0].astype(f32).T
-    out_gate, out_up = out_gate_up[0].astype(f32), out_gate_up[1].astype(f32)
+        out_down = lax.psum_scatter(down_w[0, 0], "fsdp", scatter_dimension=0, tiled=True)
+        out_down = out_down.astype(f32)
+        out_gate, out_up = lax.psum_scatter(
+            gate_up_w[0], "fsdp", scatter_dimension=1, tiled=True
+        ).astype(f32)
 
     _, mid_pull = jax.vjp(rms_scale, mixed, ffw_gain)
     grad_mixed_part, grad_ffw_gain = mid_pull(grad_mid)
@@ -766,18 +884,27 @@
     grad_attn_low = grad_attn_sum.astype(bf)
     grad_out_w = dot_tn(grad_attn_low, attn_low)
     grad_attn_rows = dot_nn(grad_attn_low, out_full).astype(bf)
-    grad_query_rot, kept, given, grad_own = attend_back(
-        table, cont_prompt, cont_length, query_rot, grad_attn_rows, log_sum, own_pairs, chunks
-    )
+    if ringed:
+        held_sums = add_sums(move_sums(), 6, grad_attn_rows)
+    grad_query_rot, grad_own, kept, given = attend_back(
+        table, cont_prompt, cont_length, query_rot, grad_attn_rows, log_sum, own_pairs, sources, held_sums if ringed else ()
+    )
+    if ringed:
+        moved = move_sums()
+        given = after(given, *moved)
+        held_sums = add_sums(moved, 5)
     given = lax.ppermute(given, "tensor", [(2, 3), (3, 2)])
-    kept = kept.astype(f32) + given.astype(f32)
-    pair_sums = Collect(
-        lambda s: kept[0, s * PSLICE : (s + 1) * PSLICE],
-        lambda s: kept[1, s * PSLICE : (s + 1) * PSLICE],
-    )
-    for _ in range(GROUP - 1):
-        last_sums = pair_sums.step()
-    summed = jnp.concatenate(last_sums, 0)
+    kept = (kept.astype(f32) + given.astype(f32)).astype(bf)
+    if ringed:
+        for s in (4, 3, 2):
+            held_sums = add_sums(move_sums(), s)
+        summed = lax.psum_scatter(kept, "fsdp", scatter_dimension=0)
+        summed = after(summed, *held_sums).astype(f32)
+    else:
+        summed = kept[GROUP - 1]
+        for s in reversed(range(GROUP - 1)):
+            summed = (ring_step(summed, -1).astype(f32) + kept[s].astype(f32)).astype(bf)
+        summed = summed.astype(f32)
     back = lax.ppermute(summed.astype(bf), "tensor", [(2, 0), (3, 1)]).astype(f32)
     grad_pairs = jnp.where(is_cont, grad_own, summed + back)
 
@@ -814,13 +941,19 @@
             for h in range(HEADS)
         )
     ).reshape(members, dim // members, 2 * HEAD)
-    out_qo = collect_fsdp(after(qo_sum, summed), fsdp_pos)
+    out_qo = collect_fsdp(qo_sum, fsdp_pos)
     out_query, out_out = out_qo[:, :HEAD], out_qo[:, HEAD:].T
     kv_blocks = grad_kv_w.reshape(members, TENSOR, shard_kv, 2 * HEAD)
     kv_column = collect_tensor(
         *order_tensor([kv_blocks[:, t] for t in range(TENSOR)], tensor_pos)
     )
     out_kv = collect_fsdp(kv_column, fsdp_pos)
+
+    if ringed:
+        held_sums = add_sums(move_sums(), 1, grad_kv_w)
+        held_sums = add_sums(move_sums(), 0)
+        out_gate, out_up, out_down = held_sums
+    out_down = out_down.T
 
     small = jnp.concatenate(
         [

time: 826 us -> 805 us (0.975)
  Pallas kernels: 206 us -> 240 us
  waiting for transfers between devices: 315 us -> 283 us
  other arithmetic: 85.3 us -> 73.3 us
  starting transfers between devices: 128 us -> 118 us
    ppermute x7, waiting for transfers between devices: 15 us -> 55.6 us  [swap_bit(): return lax.ppermute(value, 'fsdp', [(f, f ^ bit) for f in range(size)])]
    pallas_call x4 -> x12, Pallas kernels: 102 us -> 138 us  [the longest x4 108 us: feed_call(): pl.pallas_call(functools.partial(kernel, len(pieces)), out_shape=(wide_sh...]
    ppermute x9, waiting for transfers between devices: 63.4 us -> 36.8 us  [swap_x(): return lax.ppermute(value, 'tensor', [(t, t ^ 2) for t in range(TENSOR)])]
    ppermute x28, waiting for transfers between devices: 180 us -> 157 us  [ring_step(): return lax.ppermute(value, 'fsdp', pairs)]
    ppermute x7, starting transfers between devices: 29.4 us -> 7.8 us  [swap_bit(): return lax.ppermute(value, 'fsdp', [(f, f ^ bit) for f in range(size)])]
    ppermute x12, waiting for transfers between devices: 24.8 us -> 9.45 us  [shift_z(): return lax.ppermute(value, 'fsdp', pairs)]
    ppermute x9, starting transfers between devices: 20.4 us -> 31 us  [swap_x(): return lax.ppermute(value, 'tensor', [(t, t ^ 2) for t in range(TENSOR)])]
    ppermute x28, starting transfers between devices: 37 us -> 47.1 us  [ring_step(): return lax.ppermute(value, 'fsdp', pairs)]
  transfers between devices with their start and end apart: 95 -> 79, of which waited for: 50 -> 32; matrix products, arithmetic and copies ran while one was open for 14% -> 12% of each run, Pallas kernels for 17% -> 20%
where the time goes in v3:
time: 805 us; the launch traced here: 797 us
  waiting for transfers between devices  283 us (35%)
  Pallas kernels  240 us (30%)
  starting transfers between devices  118 us (15%)
  other arithmetic  73.3 us (9%)
  local copies, waits for them, and re-layouts  42.7 us (5%)
  matrix products  21.6 us (3%)
  between operations  19.5 us (2%)
    ppermute x28, waiting for transfers between devices, ring_step(): return lax.ppermute(value, 'fsdp', pairs)  157 us
    pallas_call x4, Pallas kernels, feed_call(): pl.pallas_call(functools.partial(kernel, len(pieces)), out_shape=(wide_sh...  108 us
    ppermute x7, waiting for transfers between devices, swap_bit(): return lax.ppermute(value, 'fsdp', [(f, f ^ bit) for f in range(size)])  55.6 us
    ppermute x28, starting transfers between devices, ring_step(): return lax.ppermute(value, 'fsdp', pairs)  47.1 us
    ppermute x9, waiting for transfers between devices, swap_x(): return lax.ppermute(value, 'tensor', [(t, t ^ 2) for t in range(TENSOR)])  36.8 us
    pallas_call x2, Pallas kernels, weight_grads(): pl.pallas_call(functools.partial(weight_grad_kernel, number), out_shape=j...  36.5 us
    pallas_call x1, Pallas kernels, attend_back(): pl.pallas_call(attend_back_kernel, out_shape=(jax.ShapeDtypeStruct((rows,...  33.2 us
    ppermute x9, starting transfers between devices, swap_x(): return lax.ppermute(value, 'tensor', [(t, t ^ 2) for t in range(TENSOR)])  31 us
  transfers between devices with their start and end apart: 79, of which 32 were waited for; matrix products, arithmetic and copies ran while one was open for 12% of the time, Pallas kernels for 20%

profile of v3, /device:TPU:0, one launch (start us, length us, event | category | flops | bytes accessed | tf_op | source)
XLA Modules:
  0.0 797.5 jit_solution(6658676172892995459)
XLA Ops:
  30.5 7.3 collective-permute-done.5.refs_2_
  85.7 20.3 %collective-permute-done.10 = bf16[4,144,512]{2,1,0:T(8,128)(2,1)S(1)} collective-permute-done((bf16[4,144,512]{2,1,0:T(8,128)(2,1)}, bf16[4,144,512]{2,1,0:T(8,128)(2,1)S(1)}, u32[]{:S(2)}, u32[]{:S(2)}) %collective-permute-start.10) | collective-permute-done | bytes 589856 | tf_op jit(solution)/shard_map/ppermute | solution.py:43
  108.3 26.2 %collective-permute-done.15.refs_3_ = bf16[224,1728]{1,0:T(8,128)(2,1)S(1)} collective-permute-done((bf16[224,1728]{1,0:T(8,128)(2,1)}, bf16[224,1728]{1,0:T(8,128)(2,1)S(1)}, u32[]{:S(2)}, u32[]{:S(2)}) %collective-permute-start.15) | collective-permute-done | bytes 774176 | tf_op jit(solution)/shard_map/ppermute | solution.py:57
  145.4 16.0 %collective-permute-done.16.refs_4_ = bf16[224,1728]{1,0:T(8,128)(2,1)} collective-permute-done((bf16[224,1728]{1,0:T(8,128)(2,1)S(1)}, bf16[224,1728]{1,0:T(8,128)(2,1)}, u32[]{:S(2)}, u32[]{:S(2)}) %collective-permute-start.16) | collective-permute-done | bytes 774176 | tf_op jit(solution)/shard_map/ppermute | solution.py:57
  164.0 12.5 %collective-permute-start.25 = (bf16[208,1728]{1,0:T(8,128)(2,1)}, bf16[208,1728]{1,0:T(8,128)(2,1)}, u32[]{:S(2)}, u32[]{:S(2)}) collective-permute-start(bf16[208,1728]{1,0:T(8,128)(2,1)} %collective-permute-done.19.refs_12_), channel_id=1, source_target_pairs={{0,4},{8,0},{16,8},{24,16},{28,24},{20,28},{12,20},{4,12},{1,5},{9... | collective-permute-start | bytes 2156552 | tf_op jit(solution)/shard_map/ppermute | solution.py:57
  176.6 29.8 %collective-permute-done.25.refs_13_ = bf16[208,1728]{1,0:T(8,128)(2,1)} collective-permute-done((bf16[208,1728]{1,0:T(8,128)(2,1)}, bf16[208,1728]{1,0:T(8,128)(2,1)}, u32[]{:S(2)}, u32[]{:S(2)}) %collective-permute-start.25) | collective-permute-done | bytes 718880 | tf_op jit(solution)/shard_map/ppermute | solution.py:57
  208.6 7.8 place_heads.1
  235.6 18.3 %attend.1 = (bf16[512,1024]{1,0:T(8,128)(2,1)S(1)}, f32[8,1,256]{2,1,0:T(1,128)S(1)}) custom-call(s32[128]{0:T(128)S(1)} %copy-done.19, s32[4]{0:T(128)S(1)} %copy-done.23, s32[4]{0:T(128)S(1)} %copy-done.21, bf16[512,1024]{1,0:T(8,128)(2,1)S(1)} %fusion.101.query_ref, bf16[512,512]{1,0:T(8,128)(2,1)S(1)} %pad_maximum_fusion.5.own_ref, ...), custom_call_target="tpu_custom_call" | custom-call | flops 4831838208 | bytes 6815744 | tf_op jit(solution)/shard_map/attend/pallas_call | solution.py:360
  261.8 9.8 %collective-permute-start.32 = (bf16[512,1152]{1,0:T(8,128)(2,1)S(1)}, bf16[512,1152]{1,0:T(8,128)(2,1)S(1)}, u32[]{:S(2)}, u32[]{:S(2)}) collective-permute-start(bf16[512,1152]{1,0:T(8,128)(2,1)S(1)} %multiply_convert_fusion.first_ref.refs_0_), channel_id=1, source_target_pairs={{0,2},{1,3},{2,0},{3,1},{4,6},{5,7},{6,4},{7,5},{8,10},{9,11},{10,... | collective-permute-start | bytes 3538952 | tf_op jit(solution)/shard_map/ppermute | solution.py:38
  271.6 9.8 %collective-permute-done.30.refs_15_ = bf16[208,1728]{1,0:T(8,128)(2,1)S(1)} collective-permute-done((bf16[208,1728]{1,0:T(8,128)(2,1)}, bf16[208,1728]{1,0:T(8,128)(2,1)S(1)}, u32[]{:S(2)}, u32[]{:S(2)}) %collective-permute-start.30) | collective-permute-done | bytes 718880 | tf_op jit(solution)/shard_map/ppermute | solution.py:57
  284.2 25.0 %feed.2 = (bf16[1024,1728]{1,0:T(8,128)(2,1)}, bf16[1024,1728]{1,0:T(8,128)(2,1)}, bf16[1024,1728]{1,0:T(8,128)(2,1)}, bf16[512,1152]{1,0:T(8,128)(2,1)}, bf16[512,1152]{1,0:T(8,128)(2,1)}) custom-call(s32[128]{0:T(128)} %fusion.131.table, bf16[512,1152]{1,0:T(8,128)(2,1)} %copy-done.2, bf16[512,1152]{1,0:T(8,128)(2,1)} %copy-done.5, ...), custom_call_target="tpu_custom_call" | custom-call | flops 12230590464 | bytes 22560768 | tf_op jit(solution)/shard_map/feed/pallas_call | solution.py:571
  313.2 25.6 %feed.3 = (bf16[1024,1728]{1,0:T(8,128)(2,1)}, bf16[1024,1728]{1,0:T(8,128)(2,1)}, bf16[1024,1728]{1,0:T(8,128)(2,1)}, bf16[512,1152]{1,0:T(8,128)(2,1)}, bf16[512,1152]{1,0:T(8,128)(2,1)}) custom-call(s32[128]{0:T(128)} %fusion.131.table, bf16[512,1152]{1,0:T(8,128)(2,1)} %copy-done.7, bf16[512,1152]{1,0:T(8,128)(2,1)} %copy-done.9, ...), custom_call_target="tpu_custom_call" | custom-call | flops 12230590464 | bytes 22560768 | tf_op jit(solution)/shard_map/feed/pallas_call | solution.py:571
  344.8 9.7 %collective-permute-start.35 = (bf16[512,1152]{1,0:T(8,128)(2,1)}, bf16[512,1152]{1,0:T(8,128)(2,1)}, u32[]{:S(2)}, u32[]{:S(2)}) collective-permute-start(bf16[512,1152]{1,0:T(8,128)(2,1)} %add_convert_fusion.2), channel_id=1, source_target_pairs={{0,2},{1,3},{2,0},{3,1},{4,6},{5,7},{6,4},{7,5},{8,10},{9,11},{10,... | collective-permute-start | bytes 3538952 | tf_op jit(solution)/shard_map/ppermute | solution.py:38
  357.9 23.2 %collective-permute-done.35 = bf16[512,1152]{1,0:T(8,128)(2,1)} collective-permute-done((bf16[512,1152]{1,0:T(8,128)(2,1)}, bf16[512,1152]{1,0:T(8,128)(2,1)}, u32[]{:S(2)}, u32[]{:S(2)}) %collective-permute-start.35) | collective-permute-done | bytes 1179680 | tf_op jit(solution)/shard_map/ppermute | solution.py:38
  395.7 28.8 %feed_back.2 = (bf16[1024,1728]{1,0:T(8,128)(2,1)}, bf16[1024,1728]{1,0:T(8,128)(2,1)}, bf16[512,1152]{1,0:T(8,128)(2,1)}, bf16[512,1152]{1,0:T(8,128)(2,1)}) custom-call(s32[128]{0:T(128)} %fusion.131.table, bf16[512,1152]{1,0:T(8,128)(2,1)} %copy-done, bf16[512,1152]{1,0:T(8,128)(2,1)} %copy-done.11, bf16[1024,1728]{1,0:T(8,128)(2,1)} %get-tuple-element.89.gate_ref, ...), custom_call_target="tpu_custom_call" | custom-call | flops 12230590464 | bytes 26099712 | tf_op jit(solution)/shard_map/feed_back/pallas_call | solution.py:571
  428.5 28.8 %feed_back.3 = (bf16[1024,1728]{1,0:T(8,128)(2,1)}, bf16[1024,1728]{1,0:T(8,128)(2,1)}, bf16[512,1152]{1,0:T(8,128)(2,1)}, bf16[512,1152]{1,0:T(8,128)(2,1)}) custom-call(s32[128]{0:T(128)} %fusion.131.table, bf16[512,1152]{1,0:T(8,128)(2,1)} %copy-done.13, bf16[512,1152]{1,0:T(8,128)(2,1)} %copy-done.15, bf16[1024,1728]{1,0:T(8,128)(2,1)} %get-tuple-element.94.gate_ref, ...), custom_call_target="tpu_custom_call" | custom-call | flops 12230590464 | bytes 26099712 | tf_op jit(solution)/shard_map/feed_back/pallas_call | solution.py:571
  466.4 13.5 %down_grad.1.refs_2_.refs_3_.refs_4_.refs_5_ = bf16[8,1,144,1728]{3,2,1,0:T(8,128)(2,1)} custom-call(bf16[512,1152]{1,0:T(8,128)(2,1)S(1)} %copy-done.1, bf16[512,1152]{1,0:T(8,128)(2,1)S(1)} %copy-done.12, bf16[512,1152]{1,0:T(8,128)(2,1)S(1)} %copy-done.14, bf16[512,1152]{1,0:T(8,128)(2,1)S(1)} %copy-done.16, ...), custom_call_target="tpu_custom_call" | custom-call | flops 3057647616 | bytes 9879552 | tf_op jit(solution)/shard_map/down_grad/pallas_call | solution.py:668
  480.0 23.0 %gate_up_grad.1.refs_0_.refs_1_.refs_2_.refs_3_ = bf16[8,2,144,1728]{3,2,1,0:T(8,128)(2,1)} custom-call(bf16[512,1152]{1,0:T(8,128)(2,1)S(1)} %copy-done.3, bf16[512,1152]{1,0:T(8,128)(2,1)S(1)} %copy-done.6, bf16[512,1152]{1,0:T(8,128)(2,1)S(1)} %copy-done.8, bf16[512,1152]{1,0:T(8,128)(2,1)S(1)} %copy-done.10, ...), custom_call_target="tpu_custom_call" | custom-call | flops 6115295232 | bytes 17399808 | tf_op jit(solution)/shard_map/gate_up_grad/pallas_call | solution.py:668
  532.3 33.2 %attend_back.1 = (f32[512,1024]{1,0:T(8,128)}, f32[512,512]{1,0:T(8,128)}, bf16[8,512,512]{2,1,0:T(8,128)(2,1)}, bf16[8,512,512]{2,1,0:T(8,128)(2,1)}) custom-call(s32[128]{0:T(128)} %fusion.131.table, s32[4]{0:T(128)} %mapped.3, s32[4]{0:T(128)} %length.3, bf16[512,1024]{1,0:T(8,128)(2,1)} %copy-done.20, ...), custom_call_target="tpu_custom_call" | custom-call | flops 12079595520 | bytes 19398656 | tf_op jit(solution)/shard_map/attend_back/pallas_call | solution.py:424
  600.3 32.8 %collective-permute-done.48.refs_1_ = bf16[208,1728]{1,0:T(8,128)(2,1)} collective-permute-done((bf16[208,1728]{1,0:T(8,128)(2,1)}, bf16[208,1728]{1,0:T(8,128)(2,1)}, u32[]{:S(2)}, u32[]{:S(2)}) %collective-permute-start.48) | collective-permute-done | bytes 718880 | tf_op jit(solution)/shard_map/ppermute | solution.py:57
  652.1 13.2 %collective-permute-done.50.refs_1_ = bf16[208,1728]{1,0:T(8,128)(2,1)} collective-permute-done((bf16[208,1728]{1,0:T(8,128)(2,1)}, bf16[208,1728]{1,0:T(8,128)(2,1)}, u32[]{:S(2)}, u32[]{:S(2)}) %collective-permute-start.50) | collective-permute-done | bytes 718880 | tf_op jit(solution)/shard_map/ppermute | solution.py:57
  672.4 11.2 %collective-permute-done.62 = bf16[4,144,512]{2,1,0:T(8,128)(2,1)} collective-permute-done((bf16[4,144,512]{2,1,0:T(8,128)(2,1)S(1)}, bf16[4,144,512]{2,1,0:T(8,128)(2,1)}, u32[]{:S(2)}, u32[]{:S(2)}) %collective-permute-start.62) | collective-permute-done | bytes 589856 | tf_op jit(solution)/shard_map/ppermute | solution.py:43
  691.0 8.7 %collective-permute-done.52.refs_1_ = bf16[208,1728]{1,0:T(8,128)(2,1)} collective-permute-done((bf16[208,1728]{1,0:T(8,128)(2,1)}, bf16[208,1728]{1,0:T(8,128)(2,1)}, u32[]{:S(2)}, u32[]{:S(2)}) %collective-permute-start.52) | collective-permute-done | bytes 718880 | tf_op jit(solution)/shard_map/ppermute | solution.py:57
  740.2 16.8 %collective-permute-done.56 = f32[48,128]{1,0:T(8,128)S(1)} collective-permute-done((f32[48,128]{1,0:T(8,128)S(1)}, f32[48,128]{1,0:T(8,128)S(1)}, u32[]{:S(2)}, u32[]{:S(2)}) %collective-permute-start.56) | collective-permute-done | bytes 24608 | tf_op jit(solution)/shard_map/ppermute | solution.py:43
  (539 shorter events, 326.7 us)
Async XLA Ops:
  7.2 223.2 %all-gather.3.cloned.1.call-start = ((), (), s32[]{:S(2)}) async-start(), calls=%async_computation.2 | async-start | bytes 4718592 | tf_op jit(solution)/shard_map/all_gather | solution.py:782
  106.1 604.6 %reduce-scatter.2.cloned.1.call-start = ((), (), s32[]{:S(2)}) async-start(), calls=%async_computation.1 | async-start | bytes 4718592 | tf_op jit(solution)/shard_map/reduce_scatter | solution.py:901
  106.2 38.7 %collective-permute-start.21 = (bf16[8,144,512]{2,1,0:T(8,128)(2,1)S(1)}, bf16[8,144,512]{2,1,0:T(8,128)(2,1)}, u32[]{:S(2)}, u32[]{:S(2)}) collective-permute-start(bf16[8,144,512]{2,1,0:T(8,128)(2,1)S(1)} %constant_dynamic-update-slice_fusion.5.refs_0_), channel_id=1, source_target_pairs={{0,2},{1,3},{2,0},{3,1},{4,6},{5,7},{6,4},{7,5},{8,10},{9,11},{10,... | collective-permute-start | bytes 3538952 | tf_op jit(solution)/shard_map/ppermute | solution.py:38
  106.3 35.8 %collective-permute-start.18 = (bf16[208,1728]{1,0:T(8,128)(2,1)}, bf16[208,1728]{1,0:T(8,128)(2,1)S(1)}, u32[]{:S(2)}, u32[]{:S(2)}) collective-permute-start(bf16[208,1728]{1,0:T(8,128)(2,1)} %collective-permute-done.17.refs_10_), channel_id=1, source_target_pairs={{0,4},{8,0},{16,8},{24,16},{28,24},{20,28},{12,20},{4,12},{1,5},{9... | collective-permute-start | bytes 2156552 | tf_op jit(solution)/shard_map/ppermute | solution.py:57
  144.9 63.7 %collective-permute-start.20 = (bf16[8,144,512]{2,1,0:T(8,128)(2,1)S(1)}, bf16[8,144,512]{2,1,0:T(8,128)(2,1)}, u32[]{:S(2)}, u32[]{:S(2)}) collective-permute-start(bf16[8,144,512]{2,1,0:T(8,128)(2,1)S(1)} %constant_dynamic-update-slice_fusion.5.refs_0_), channel_id=1, source_target_pairs={{0,1},{1,0},{2,3},{3,2},{4,5},{5,4},{6,7},{7,6},{8,9},{9,8},{10,11... | collective-permute-start | bytes 3538952 | tf_op jit(solution)/shard_map/ppermute | solution.py:34
  144.9 63.7 %collective-permute-start.22 = (bf16[8,144,512]{2,1,0:T(8,128)(2,1)}, bf16[8,144,512]{2,1,0:T(8,128)(2,1)}, u32[]{:S(2)}, u32[]{:S(2)}) collective-permute-start(bf16[8,144,512]{2,1,0:T(8,128)(2,1)} %collective-permute-done.21.refs_2_), channel_id=1, source_target_pairs={{0,1},{1,0},{2,3},{3,2},{4,5},{5,4},{6,7},{7,6},{8,9},{9,8},{10,11... | collective-permute-start | bytes 3538952 | tf_op jit(solution)/shard_map/ppermute | solution.py:34
  161.4 44.9 %collective-permute-start.23 = (bf16[224,1728]{1,0:T(8,128)(2,1)}, bf16[224,1728]{1,0:T(8,128)(2,1)}, u32[]{:S(2)}, u32[]{:S(2)}) collective-permute-start(bf16[224,1728]{1,0:T(8,128)(2,1)} %collective-permute-done.16.refs_4_), channel_id=1, source_target_pairs={{0,8},{8,16},{16,24},{24,28},{28,20},{20,12},{12,4},{4,0},{1,9},{9... | collective-permute-start | bytes 2322440 | tf_op jit(solution)/shard_map/ppermute | solution.py:57
  164.0 42.3 %collective-permute-start.25 = (bf16[208,1728]{1,0:T(8,128)(2,1)}, bf16[208,1728]{1,0:T(8,128)(2,1)}, u32[]{:S(2)}, u32[]{:S(2)}) collective-permute-start(bf16[208,1728]{1,0:T(8,128)(2,1)} %collective-permute-done.19.refs_12_), channel_id=1, source_target_pairs={{0,4},{8,0},{16,8},{24,16},{28,24},{20,28},{12,20},{4,12},{1,5},{9... | collective-permute-start | bytes 2156552 | tf_op jit(solution)/shard_map/ppermute | solution.py:57
  261.8 47.4 %collective-permute-start.32 = (bf16[512,1152]{1,0:T(8,128)(2,1)S(1)}, bf16[512,1152]{1,0:T(8,128)(2,1)S(1)}, u32[]{:S(2)}, u32[]{:S(2)}) collective-permute-start(bf16[512,1152]{1,0:T(8,128)(2,1)S(1)} %multiply_convert_fusion.first_ref.refs_0_), channel_id=1, source_target_pairs={{0,2},{1,3},{2,0},{3,1},{4,6},{5,7},{6,4},{7,5},{8,10},{9,11},{10,... | collective-permute-start | bytes 3538952 | tf_op jit(solution)/shard_map/ppermute | solution.py:38
  344.8 36.2 %collective-permute-start.35 = (bf16[512,1152]{1,0:T(8,128)(2,1)}, bf16[512,1152]{1,0:T(8,128)(2,1)}, u32[]{:S(2)}, u32[]{:S(2)}) collective-permute-start(bf16[512,1152]{1,0:T(8,128)(2,1)} %add_convert_fusion.2), channel_id=1, source_target_pairs={{0,2},{1,3},{2,0},{3,1},{4,6},{5,7},{6,4},{7,5},{8,10},{9,11},{10,... | collective-permute-start | bytes 3538952 | tf_op jit(solution)/shard_map/ppermute | solution.py:38
  391.8 32.7 %collective-permute-start.38 = (bf16[512,1152]{1,0:T(8,128)(2,1)S(1)}, bf16[512,1152]{1,0:T(8,128)(2,1)S(1)}, u32[]{:S(2)}, u32[]{:S(2)}) collective-permute-start(bf16[512,1152]{1,0:T(8,128)(2,1)S(1)} %fusion.4.first_ref.refs_0_), channel_id=1, source_target_pairs={{0,2},{1,3},{2,0},{3,1},{4,6},{5,7},{6,4},{7,5},{8,10},{9,11},{10,... | collective-permute-start | bytes 3538952 | tf_op jit(solution)/shard_map/ppermute | solution.py:38
  457.5 51.0 %collective-permute-start.37 = (bf16[512,1152]{1,0:T(8,128)(2,1)}, bf16[512,1152]{1,0:T(8,128)(2,1)}, u32[]{:S(2)}, u32[]{:S(2)}) collective-permute-start(bf16[512,1152]{1,0:T(8,128)(2,1)} %get-tuple-element.92), channel_id=1, source_target_pairs={{0,1},{1,0},{2,3},{3,2},{4,5},{5,4},{6,7},{7,6},{8,9},{9,8},{10,11... | collective-permute-start | bytes 3538952 | tf_op jit(solution)/shard_map/ppermute | solution.py:34
  463.4 45.2 %collective-permute-start.41 = (bf16[512,1152]{1,0:T(8,128)(2,1)}, bf16[512,1152]{1,0:T(8,128)(2,1)}, u32[]{:S(2)}, u32[]{:S(2)}) collective-permute-start(bf16[512,1152]{1,0:T(8,128)(2,1)} %add_convert_fusion.1), channel_id=1, source_target_pairs={{0,2},{1,3},{2,0},{3,1},{4,6},{5,7},{6,4},{7,5},{8,10},{9,11},{10,... | collective-permute-start | bytes 3538952 | tf_op jit(solution)/shard_map/ppermute | solution.py:38
  530.3 35.2 %collective-permute-start.44 = (bf16[224,1728]{1,0:T(8,128)(2,1)}, bf16[224,1728]{1,0:T(8,128)(2,1)S(1)}, u32[]{:S(2)}, u32[]{:S(2)}) collective-permute-start(bf16[224,1728]{1,0:T(8,128)(2,1)} %get-tuple-element.109.refs_2_), channel_id=1, source_target_pairs={{0,4},{8,0},{16,8},{24,16},{28,24},{20,28},{12,20},{4,12},{1,5},{9... | collective-permute-start | bytes 2322440 | tf_op jit(solution)/shard_map/ppermute | solution.py:57
  530.6 34.9 %collective-permute-start.45 = (bf16[208,1728]{1,0:T(8,128)(2,1)}, bf16[208,1728]{1,0:T(8,128)(2,1)S(1)}, u32[]{:S(2)}, u32[]{:S(2)}) collective-permute-start(bf16[208,1728]{1,0:T(8,128)(2,1)} %get-tuple-element.110.refs_3_), channel_id=1, source_target_pairs={{0,8},{8,16},{16,24},{24,28},{28,20},{20,12},{12,4},{4,0},{1,9},{9... | collective-permute-start | bytes 2156552 | tf_op jit(solution)/shard_map/ppermute | solution.py:57
  584.2 59.2 %collective-permute-start.59 = (bf16[1152,512]{0,1:T(8,128)(2,1)}, bf16[1152,512]{0,1:T(8,128)(2,1)}, u32[]{:S(2)}, u32[]{:S(2)}) collective-permute-start(bf16[1152,512]{0,1:T(8,128)(2,1)} %pad_maximum_fusion), channel_id=1, source_target_pairs={{0,1},{1,0},{2,3},{3,2},{4,5},{5,4},{6,7},{7,6},{8,9},{9,8},{10,11... | collective-permute-start | bytes 3538952 | tf_op jit(solution)/shard_map/ppermute | solution.py:34
  590.0 53.4 %collective-permute-start.61 = (bf16[1152,512]{0,1:T(8,128)(2,1)}, bf16[1152,512]{0,1:T(8,128)(2,1)}, u32[]{:S(2)}, u32[]{:S(2)}) collective-permute-start(bf16[1152,512]{0,1:T(8,128)(2,1)} %fusion.13), channel_id=1, source_target_pairs={{0,2},{1,3},{2,0},{3,1},{4,6},{5,7},{6,4},{7,5},{8,10},{9,11},{10,... | collective-permute-start | bytes 3538952 | tf_op jit(solution)/shard_map/ppermute | solution.py:38
  598.3 38.5 %collective-permute-start.47 = (bf16[224,1728]{1,0:T(8,128)(2,1)}, bf16[224,1728]{1,0:T(8,128)(2,1)S(1)}, u32[]{:S(2)}, u32[]{:S(2)}) collective-permute-start(bf16[224,1728]{1,0:T(8,128)(2,1)} %get-tuple-element.116), channel_id=1, source_target_pairs={{0,4},{8,0},{16,8},{24,16},{28,24},{20,28},{12,20},{4,12},{1,5},{9... | collective-permute-start | bytes 2322440 | tf_op jit(solution)/shard_map/ppermute | solution.py:57
  598.6 34.4 %collective-permute-start.48 = (bf16[208,1728]{1,0:T(8,128)(2,1)}, bf16[208,1728]{1,0:T(8,128)(2,1)}, u32[]{:S(2)}, u32[]{:S(2)}) collective-permute-start(bf16[208,1728]{1,0:T(8,128)(2,1)} %get-tuple-element.117), channel_id=1, source_target_pairs={{0,8},{8,16},{16,24},{24,28},{28,20},{20,12},{12,4},{4,0},{1,9},{9... | collective-permute-start | bytes 2156552 | tf_op jit(solution)/shard_map/ppermute | solution.py:57
  651.7 32.0 %collective-permute-start.62 = (bf16[4,144,512]{2,1,0:T(8,128)(2,1)S(1)}, bf16[4,144,512]{2,1,0:T(8,128)(2,1)}, u32[]{:S(2)}, u32[]{:S(2)}) collective-permute-start(bf16[4,144,512]{2,1,0:T(8,128)(2,1)S(1)} %fusion.20), channel_id=1, source_target_pairs={{0,4},{4,0},{8,12},{12,8},{16,20},{20,16},{24,28},{28,24},{1,5},{5... | collective-permute-start | bytes 1769480 | tf_op jit(solution)/shard_map/ppermute | solution.py:43
  670.0 37.0 %collective-permute-start.51 = (bf16[224,1728]{1,0:T(8,128)(2,1)}, bf16[224,1728]{1,0:T(8,128)(2,1)}, u32[]{:S(2)}, u32[]{:S(2)}) collective-permute-start(bf16[224,1728]{1,0:T(8,128)(2,1)} %get-tuple-element.120), channel_id=1, source_target_pairs={{0,4},{8,0},{16,8},{24,16},{28,24},{20,28},{12,20},{4,12},{1,5},{9... | collective-permute-start | bytes 2322440 | tf_op jit(solution)/shard_map/ppermute | solution.py:57
  686.1 32.0 %collective-permute-start.64 = (bf16[144,512]{1,0:T(8,128)(2,1)}, bf16[144,512]{1,0:T(8,128)(2,1)S(1)}, u32[]{:S(2)}, u32[]{:S(2)}) collective-permute-start(bf16[144,512]{1,0:T(8,128)(2,1)} %get-tuple-element.194), channel_id=1, source_target_pairs={{0,16},{4,20},{8,24},{12,28},{16,0},{20,4},{24,8},{28,12},{1,17},{... | collective-permute-start | bytes 442376 | tf_op jit(solution)/shard_map/ppermute | solution.py:48
  737.5 47.2 %collective-permute-start.75 = (bf16[224,1728]{1,0:T(8,128)(2,1)}, bf16[224,1728]{1,0:T(8,128)(2,1)}, u32[]{:S(2)}, u32[]{:S(2)}) collective-permute-start(bf16[224,1728]{1,0:T(8,128)(2,1)} %get-tuple-element.125), channel_id=1, source_target_pairs={{0,4},{8,0},{16,8},{24,16},{28,24},{20,28},{12,20},{4,12},{1,5},{9... | collective-permute-start | bytes 2322440 | tf_op jit(solution)/shard_map/ppermute | solution.py:57
  737.5 47.1 %collective-permute-start.76 = (bf16[208,1728]{1,0:T(8,128)(2,1)}, bf16[208,1728]{1,0:T(8,128)(2,1)}, u32[]{:S(2)}, u32[]{:S(2)}) collective-permute-start(bf16[208,1728]{1,0:T(8,128)(2,1)} %get-tuple-element.126), channel_id=1, source_target_pairs={{0,8},{8,16},{16,24},{24,28},{28,20},{20,12},{12,4},{4,0},{1,9},{9... | collective-permute-start | bytes 2156552 | tf_op jit(solution)/shard_map/ppermute | solution.py:57
  (170 other events, 3051.7 us)
Sparse Core Ops, SparseCore 0:
  106.2 101.9 all-gather.2
  574.5 121.2 reduce-scatter.1

commit v4 on v3

--- a/solution.py
+++ b/solution.py
@@ -223,8 +223,9 @@
 
 
 def place_kernel(table, *refs):
-    for j in range(TENSOR):
-        refs[TENSOR][0, table[AT_TENSOR + j]] = refs[j][0]
+    for r in range(refs[0].shape[0]):
+        for j in range(TENSOR):
+            refs[TENSOR][table[AT_FSDP + r], table[AT_TENSOR + j]] = refs[j][r]
 
 
 def place(table, blocks):
@@ -232,14 +233,8 @@
     return pl.pallas_call(
         place_kernel,
         out_shape=jax.ShapeDtypeStruct((members, TENSOR, rows, width), bf),
-        grid_spec=pltpu.PrefetchScalarGridSpec(
-            num_scalar_prefetch=1,
-            grid=(members,),
-            in_specs=[pl.BlockSpec((1, rows, width), lambda r, table: (r, 0, 0))] * TENSOR,
-            out_specs=pl.BlockSpec(
-                (1, TENSOR, rows, width), lambda r, table: (table[AT_FSDP + r], 0, 0, 0)
-            ),
-        ),
+        in_specs=[smem] + [pl.BlockSpec(memory_space=pltpu.VMEM)] * TENSOR,
+        out_specs=pl.BlockSpec(memory_space=pltpu.VMEM),
         name="place_pairs",
     )(table, *blocks)
 
@@ -682,6 +677,94 @@
         ),
         name=name,
     )(*blocks, *halves)
+
+
+def norm_rate(value):
+    return lax.rsqrt(jnp.mean(value * value, axis=-1, keepdims=True) + eps_norm)
+
+
+def norm_back(value, gain, grad):
+    rate = norm_rate(value)
+    scaled = (1.0 + gain) * grad
+    back = rate * scaled - value * (rate * rate * rate) * jnp.mean(
+        value * scaled, axis=-1, keepdims=True
+    )
+    return back, jnp.sum(value * rate * grad, axis=0, keepdims=True)
+
+
+def add_up(ref, value):
+    step = pl.program_id(0)
+
+    @pl.when(step == 0)
+    def _():
+        ref[...] = value
+
+    @pl.when(step > 0)
+    def _():
+        ref[...] += value
+
+
+def three_parts(refs):
+    return refs[0][...].astype(f32) + refs[1][...].astype(f32) + refs[2][...].astype(f32)
+
+
+def result_kernel(table, length, scale, *refs):
+    mixed_ref, teacher_ref, gain_ref = refs[3:6]
+    result_ref, grad_ref, low_ref, gain_out, loss_out = refs[6:]
+    gain = gain_ref[...]
+    value = three_parts(refs)
+    result = mixed_ref[...] + value * norm_rate(value) * (1.0 + gain)
+    result_ref[...] = result.astype(bf)
+    row = lax.broadcasted_iota(jnp.int32, (PSLICE, 1), 0)
+    live = length[table[AT_CORE] * UNITS + pl.program_id(0)]
+    live = jnp.where(table[AT_CONT] == 1, live, PSLICE)
+    diff = jnp.where(row < live, result - teacher_ref[...].astype(f32), 0.0)
+    add_up(loss_out, jnp.sum(diff * diff, axis=0, keepdims=True))
+    grad = scale[0] * diff
+    grad_ref[...] = grad
+    back, gain_grad = norm_back(value, gain, grad)
+    low_ref[...] = back.astype(bf)
+    add_up(gain_out, gain_grad)
+
+
+def mixed_kernel(*refs):
+    mixed_ref, sum_ref, grad_ref, ffw_gain_ref, post_gain_ref = refs[3:8]
+    mixed_out, low_out, ffw_out, post_out = refs[8:]
+    back, ffw_grad = norm_back(mixed_ref[...], ffw_gain_ref[...], three_parts(refs))
+    grad_mixed = grad_ref[...] + back
+    mixed_out[...] = grad_mixed
+    add_up(ffw_out, ffw_grad)
+    back, post_grad = norm_back(sum_ref[...], post_gain_ref[...], grad_mixed)
+    low_out[...] = back.astype(bf)
+    add_up(post_out, post_grad)
+
+
+def input_kernel(part_ref, low_ref, kv_ref, input_ref, grad_ref, gain_ref, out_ref, gain_out):
+    grad = part_ref[...] + dot_nt(low_ref[...], kv_ref[...])
+    back, gain_grad = norm_back(input_ref[...].astype(f32), gain_ref[...], grad)
+    out_ref[...] = (grad_ref[...] + back).astype(bf)
+    add_up(gain_out, gain_grad)
+
+
+def by_rows(kernel, name, scalars, operands, outs):
+    def spec(shape, whole=False):
+        if whole or shape[0] == 1:
+            return pl.BlockSpec(shape, lambda i: (0, 0))
+        return pl.BlockSpec((PSLICE, shape[1]), lambda i: (i, 0))
+
+    operands = [part if isinstance(part, tuple) else (part, False) for part in operands]
+    return pl.pallas_call(
+        kernel,
+        out_shape=tuple(jax.ShapeDtypeStruct(shape, kind) for shape, kind in outs),
+        grid=(UNITS,),
+        in_specs=[smem] * len(scalars) + [spec(part.shape, whole) for part, whole in operands],
+        out_specs=tuple(spec(shape) for shape, _ in outs),
+        compiler_params=pltpu.CompilerParams(vmem_limit_bytes=48 << 20),
+        cost_estimate=pl.CostEstimate(
+            flops=20 * UNITS * PSLICE * 1152, bytes_accessed=16 << 20, transcendentals=0
+        ),
+        name=name,
+    )(*scalars, *[part for part, _ in operands])
 
 
 def local(
@@ -724,11 +807,9 @@
             jnp.concatenate([gate_proj, down_own[:CUT]], 0),
             jnp.concatenate([up_proj, down_own[CUT:]], 0),
         )
-        for _ in range(GROUP - 1):
-            weights.step()
-        came = list(zip(weights.firsts, weights.seconds, strict=True))
+        came = [()] + [weights.step() for _ in range(4)]
     else:
-        came = [()] * GROUP
+        came = [()] * (GROUP + 1)
         parts = 1
         pieces = (gate_proj, up_proj, down_own)
         pieces = [jnp.stack([lax.all_gather(w, "fsdp", axis=0, tiled=True) for w in pieces])]
@@ -790,7 +871,7 @@
     query_full, out_full = (
         part.reshape(dim, HEADS * HEAD)
         for part in place_heads(
-            table, (after(qo_column, *came[4]), qo_near, qo_far, swap_core(after(qo_far, *came[3])))
+            table, (qo_column, qo_near, qo_far, swap_core(after(qo_far, *came[3])))
         )
     )
     query_raw = dot_nn(normed_in, query_full)
@@ -800,7 +881,10 @@
     ]
 
     query_rot = jnp.concatenate(query_heads, 1)
-    held_pairs = after(held_pairs, query_rot, *came[6])
+    if ringed:
+        came += [weights.step(query_rot), weights.step(), weights.step()]
+    held_pairs = after(held_pairs, query_rot, *came[5])
+    query_rot = after(query_rot, *came[6])
     sources = held_pairs, lax.ppermute(held_pairs, "tensor", [(2, 3), (3, 2)])
     attn_low, log_sum = attend(
         table, cont_prompt, cont_length, query_rot, own_pairs, sources
@@ -811,7 +895,7 @@
     mixed = input_f + rms_scale(attn_sum, attn_post_gain)
     normed_mid = rms_scale(mixed, ffw_gain).astype(bf)
 
-    mid_near, mid_far = spread_near(normed_mid)
+    mid_near, mid_far = spread_near(after(normed_mid, *came[7]))
     gate_0, up_0, act_0, *downs = feed_call(
         feed_kernel, "feed", table, normed_mid, mid_near, (), pieces, 3
     )
@@ -820,23 +904,18 @@
         feed_kernel, "feed", table, mid_far, mid_last, (), pieces, 3
     )
     downs += more
-    ffw_sum = collect_tensor(*downs)
-    result = mixed + rms_scale(ffw_sum, ffw_post_gain)
-
-    row_length = jnp.where(
-        jnp.arange(local_rows) < PSLICE,
-        cont_length[core * UNITS],
-        cont_length[core * UNITS + 1],
-    )
-    live_rows = jnp.where(is_cont & (unit_ids >= row_length), 0.0, 1.0).astype(f32)
-    diff = result - teacher.astype(f32)
-    loss_part = jnp.sum(live_rows[:, None] * diff * diff)
+    downs_moved = swap_core(downs[1]), swap_x(collect_far(*downs[2:]))
     count_f = token_count.astype(f32)
-    grad_result = loss_scale / count_f * 2.0 * live_rows[:, None] * diff
-
-    _, ffw_pull = jax.vjp(rms_scale, ffw_sum, ffw_post_gain)
-    grad_ffw_sum, grad_ffw_post_gain = ffw_pull(grad_result)
-    grad_ffw_low = grad_ffw_sum.astype(bf)
+    row_kind, gain_kind = (local_rows, dim), ((1, dim), f32)
+    result_low, grad_result, grad_ffw_low, grad_ffw_post_gain, loss_lanes = by_rows(
+        result_kernel,
+        "result",
+        (table, cont_length, (loss_scale / count_f * 2.0)[None]),
+        (downs[0], *downs_moved, mixed, teacher, ffw_post_gain[None]),
+        ((row_kind, bf), (row_kind, f32), (row_kind, bf), gain_kind, gain_kind),
+    )
+    loss_part = jnp.sum(loss_lanes)
+
     grad_near, grad_far = spread_near(grad_ffw_low)
     gate_low_0, up_low_0, *mids = feed_call(
         feed_back_kernel, "feed_back", table, grad_ffw_low, grad_near, (gate_0, up_0), pieces, 2
@@ -847,7 +926,7 @@
     )
     mids += more
     mids_far = collect_far(*mids[2:])
-    grad_mid = collect_near(*mids[:2], mids_far)
+    mids_moved = swap_core(mids[1]), swap_x(mids_far)
     down_w = weight_grads(
         "down_grad",
         (after(grad_ffw_low, mids_far), grad_near, grad_far, grad_last),
@@ -876,12 +955,13 @@
             gate_up_w[0], "fsdp", scatter_dimension=1, tiled=True
         ).astype(f32)
 
-    _, mid_pull = jax.vjp(rms_scale, mixed, ffw_gain)
-    grad_mixed_part, grad_ffw_gain = mid_pull(grad_mid)
-    grad_mixed = grad_result + grad_mixed_part
-    _, post_pull = jax.vjp(rms_scale, attn_sum, attn_post_gain)
-    grad_attn_sum, grad_attn_post_gain = post_pull(grad_mixed)
-    grad_attn_low = grad_attn_sum.astype(bf)
+    grad_mixed, grad_attn_low, grad_ffw_gain, grad_attn_post_gain = by_rows(
+        mixed_kernel,
+        "mixed_back",
+        (),
+        (mids[0], *mids_moved, mixed, attn_sum, grad_result, ffw_gain[None], attn_post_gain[None]),
+        ((row_kind, f32), (row_kind, bf), gain_kind, gain_kind),
+    )
     grad_out_w = dot_tn(grad_attn_low, attn_low)
     grad_attn_rows = dot_nn(grad_attn_low, out_full).astype(bf)
     if ringed:
@@ -927,10 +1007,20 @@
     grad_kv_low = jnp.concatenate([grad_key_raw, grad_pairs[:, HEAD:]], 1).astype(bf)
     grad_query_w = dot_tn(normed_in, grad_query_low)
     grad_kv_w = dot_tn(normed_in, grad_kv_low)
-    grad_normed = dot_nt(grad_query_low, query_full) + dot_nt(grad_kv_low, kv_full)
-    _, input_pull = jax.vjp(rms_scale, input_f, attn_gain)
-    grad_input_part, grad_attn_gain = input_pull(grad_normed)
-    grad_input = grad_mixed + grad_input_part
+    grad_input, grad_attn_gain = by_rows(
+        input_kernel,
+        "input_back",
+        (),
+        (
+            dot_nt(grad_query_low, query_full),
+            grad_kv_low,
+            (kv_full, True),
+            layer_in,
+            grad_mixed,
+            attn_gain[None],
+        ),
+        ((row_kind, bf), gain_kind),
+    )
 
     qo_sum = collect_tensor(
         *(
@@ -957,10 +1047,10 @@
 
     small = jnp.concatenate(
         [
-            grad_attn_gain,
-            grad_attn_post_gain,
-            grad_ffw_gain,
-            grad_ffw_post_gain,
+            grad_attn_gain[0],
+            grad_attn_post_gain[0],
+            grad_ffw_gain[0],
+            grad_ffw_post_gain[0],
             grad_query_gain,
             grad_key_gain,
             loss_part[None],
@@ -979,9 +1069,9 @@
     ]
     loss = small[length - 1] / count_f
     return (
-        result.astype(bf),
+        result_low,
         loss,
-        grad_input.astype(bf),
+        grad_input,
         out_query,
         out_kv[:, :HEAD],
         out_kv[:, HEAD:],

time: 805 us -> 779 us (0.968)
  starting transfers between devices: 118 us -> 94.2 us
  Pallas kernels: 240 us -> 254 us
  other arithmetic: 73.3 us -> 59.5 us
  local copies, waits for them, and re-layouts: 42.7 us -> 55 us
  waiting for transfers between devices: 283 us -> 272 us
    pallas_call x0 -> x3, Pallas kernels: none -> 15.9 us  [by_rows(): pl.pallas_call(kernel, out_shape=tuple((jax.ShapeDtypeStruct(shape, kind)...]
    ppermute x9, starting transfers between devices: 31 us -> 15.2 us  [swap_x(): return lax.ppermute(value, 'tensor', [(t, t ^ 2) for t in range(TENSOR)])]
    ppermute x28, waiting for transfers between devices: 157 us -> 145 us  [ring_step(): return lax.ppermute(value, 'fsdp', pairs)]
    reduce_sum x6 -> x3, other arithmetic: 15.6 us -> 4.2 us  [rms_scale(): tensor_in * lax.rsqrt(jnp.mean(tensor_in * tensor_in, axis=-1, keepdims=T...]
    convert_element_type x3 -> x0, other arithmetic: 8.44 us -> none  [the longest x1 4.41 us: local(): grad_input.astype(bf)]
    unnamed x243 -> x257, local copies, waits for them, and re-layouts: 20.6 us -> 25 us
  transfers between devices with their start and end apart: 79 -> 79, of which waited for: 32 -> 35; matrix products, arithmetic and copies ran while one was open for 12% -> 13% of each run, Pallas kernels for 20% -> 25%
where the time goes in v4:
time: 779 us; the launch traced here: 773 us
  waiting for transfers between devices  272 us (35%)
  Pallas kernels  254 us (33%)
  starting transfers between devices  94.2 us (12%)
  other arithmetic  59.5 us (8%)
  local copies, waits for them, and re-layouts  55 us (7%)
  between operations  19.7 us (3%)
  matrix products  18.9 us (2%)
    ppermute x28, waiting for transfers between devices, ring_step(): return lax.ppermute(value, 'fsdp', pairs)  145 us
    pallas_call x4, Pallas kernels, feed_call(): pl.pallas_call(functools.partial(kernel, len(pieces)), out_shape=(wide_sh...  109 us
    ppermute x7, waiting for transfers between devices, swap_bit(): return lax.ppermute(value, 'fsdp', [(f, f ^ bit) for f in range(size)])  59.1 us
    ppermute x28, starting transfers between devices, ring_step(): return lax.ppermute(value, 'fsdp', pairs)  41.2 us
    pallas_call x2, Pallas kernels, weight_grads(): pl.pallas_call(functools.partial(weight_grad_kernel, number), out_shape=j...  38 us
    ppermute x9, waiting for transfers between devices, swap_x(): return lax.ppermute(value, 'tensor', [(t, t ^ 2) for t in range(TENSOR)])  34.2 us
    pallas_call x1, Pallas kernels, attend_back(): pl.pallas_call(attend_back_kernel, out_shape=(jax.ShapeDtypeStruct((rows,...  33.2 us
    pallas_call x8, Pallas kernels, pass_on(): pl.pallas_call(functools.partial(pass_on_kernel, len(moved), last), out_s...  29.4 us
  transfers between devices with their start and end apart: 79, of which 35 were waited for; matrix products, arithmetic and copies ran while one was open for 13% of the time, Pallas kernels for 25%

profile of v4, /device:TPU:0, one launch (start us, length us, event | category | flops | bytes accessed | tf_op | source)
XLA Modules:
  0.0 772.7 jit_solution(17839980325756231813)
XLA Ops:
  32.2 6.6 collective-permute-done.5.refs_2_
  46.9 7.3 collective-permute-done.8
  87.7 20.4 %collective-permute-done.10 = bf16[4,144,512]{2,1,0:T(8,128)(2,1)S(1)} collective-permute-done((bf16[4,144,512]{2,1,0:T(8,128)(2,1)}, bf16[4,144,512]{2,1,0:T(8,128)(2,1)S(1)}, u32[]{:S(2)}, u32[]{:S(2)}) %collective-permute-start.10) | collective-permute-done | bytes 589856 | tf_op jit(solution)/shard_map/ppermute | solution.py:43
  111.2 31.0 %collective-permute-done.19.refs_11_ = bf16[208,1728]{1,0:T(8,128)(2,1)S(1)} collective-permute-done((bf16[208,1728]{1,0:T(8,128)(2,1)}, bf16[208,1728]{1,0:T(8,128)(2,1)S(1)}, u32[]{:S(2)}, u32[]{:S(2)}) %collective-permute-start.19) | collective-permute-done | bytes 718880 | tf_op jit(solution)/shard_map/ppermute | solution.py:57
  145.8 7.9 %place_heads.1 = (bf16[8,144,1024]{2,1,0:T(8,128)(2,1)}, bf16[8,144,1024]{2,1,0:T(8,128)(2,1)}) custom-call(s32[128]{0:T(128)} %fusion.113.table, bf16[8,144,512]{2,1,0:T(8,128)(2,1)} %constant_dynamic-update-slice_fusion.5.refs_0_, bf16[8,144,512]{2,1,0:T(8,128)(2,1)} %collective-permute-done.14.refs_1_, ...), custom_call_target="tpu_custom_call" | custom-call | tf_op jit(solution)/shard_map/place_heads/pallas_call | solution.py:256
  172.0 9.7 %collective-permute-done.21.refs_4_ = bf16[224,1728]{1,0:T(8,128)(2,1)} collective-permute-done((bf16[224,1728]{1,0:T(8,128)(2,1)}, bf16[224,1728]{1,0:T(8,128)(2,1)}, u32[]{:S(2)}, u32[]{:S(2)}) %collective-permute-start.21) | collective-permute-done | bytes 774176 | tf_op jit(solution)/shard_map/ppermute | solution.py:57
  181.7 8.5 %collective-permute-start.22 = (bf16[224,1728]{1,0:T(8,128)(2,1)}, bf16[224,1728]{1,0:T(8,128)(2,1)}, u32[]{:S(2)}, u32[]{:S(2)}) collective-permute-start(bf16[224,1728]{1,0:T(8,128)(2,1)} %collective-permute-done.21.refs_4_), channel_id=1, source_target_pairs={{0,8},{8,16},{16,24},{24,28},{28,20},{20,12},{12,4},{4,0},{1,9},{9... | collective-permute-start | bytes 2322440 | tf_op jit(solution)/shard_map/ppermute | solution.py:57
  198.2 13.3 %collective-permute-done.25.refs_13_ = bf16[208,1728]{1,0:T(8,128)(2,1)} collective-permute-done((bf16[208,1728]{1,0:T(8,128)(2,1)}, bf16[208,1728]{1,0:T(8,128)(2,1)}, u32[]{:S(2)}, u32[]{:S(2)}) %collective-permute-start.25) | collective-permute-done | bytes 718880 | tf_op jit(solution)/shard_map/ppermute | solution.py:57
  219.5 16.0 %collective-permute-done.26.refs_14_ = bf16[208,1728]{1,0:T(8,128)(2,1)} collective-permute-done((bf16[208,1728]{1,0:T(8,128)(2,1)}, bf16[208,1728]{1,0:T(8,128)(2,1)}, u32[]{:S(2)}, u32[]{:S(2)}) %collective-permute-start.26) | collective-permute-done | bytes 718880 | tf_op jit(solution)/shard_map/ppermute | solution.py:57
  241.5 18.3 %attend.1 = (bf16[512,1024]{1,0:T(8,128)(2,1)S(1)}, f32[8,1,256]{2,1,0:T(1,128)S(1)}) custom-call(s32[128]{0:T(128)S(1)} %copy-done.18, s32[4]{0:T(128)S(1)} %copy-done.32, s32[4]{0:T(128)S(1)} %copy-done.30, bf16[512,1024]{1,0:T(8,128)(2,1)S(1)} %copy-done.21, bf16[512,512]{1,0:T(8,128)(2,1)S(1)} %pad_maximum_fusion.5.own_ref, ...), custom_call_target="tpu_custom_call" | custom-call | flops 4831838208 | bytes 6815744 | tf_op jit(solution)/shard_map/attend/pallas_call | solution.py:355
  270.2 25.2 %feed.2 = (bf16[1024,1728]{1,0:T(8,128)(2,1)}, bf16[1024,1728]{1,0:T(8,128)(2,1)}, bf16[1024,1728]{1,0:T(8,128)(2,1)}, bf16[512,1152]{1,0:T(8,128)(2,1)}, bf16[512,1152]{1,0:T(8,128)(2,1)}) custom-call(s32[128]{0:T(128)} %fusion.113.table, bf16[512,1152]{1,0:T(8,128)(2,1)} %copy-done.1, bf16[512,1152]{1,0:T(8,128)(2,1)} %collective-permute-done.30.second_ref.refs_1_, ...), custom_call_target="tpu_custom_call" | custom-call | flops 12230590464 | bytes 22560768 | tf_op jit(solution)/shard_map/feed/pallas_call | solution.py:566
  300.2 25.5 %feed.3 = (bf16[1024,1728]{1,0:T(8,128)(2,1)}, bf16[1024,1728]{1,0:T(8,128)(2,1)}, bf16[1024,1728]{1,0:T(8,128)(2,1)}, bf16[512,1152]{1,0:T(8,128)(2,1)}, bf16[512,1152]{1,0:T(8,128)(2,1)}) custom-call(s32[128]{0:T(128)} %fusion.113.table, bf16[512,1152]{1,0:T(8,128)(2,1)} %collective-permute-done.32.first_ref.refs_2_, bf16[512,1152]{1,0:T(8,128)(2,1)} %copy-done.10, ...), custom_call_target="tpu_custom_call" | custom-call | flops 12230590464 | bytes 22560768 | tf_op jit(solution)/shard_map/feed/pallas_call | solution.py:566
  335.6 24.4 %collective-permute-done.35.refs_2_ = bf16[512,1152]{1,0:T(8,128)(2,1)} collective-permute-done((bf16[512,1152]{1,0:T(8,128)(2,1)}, bf16[512,1152]{1,0:T(8,128)(2,1)}, u32[]{:S(2)}, u32[]{:S(2)}) %collective-permute-start.35) | collective-permute-done | bytes 1179680 | tf_op jit(solution)/shard_map/ppermute | solution.py:38
  372.6 28.9 %feed_back.2 = (bf16[1024,1728]{1,0:T(8,128)(2,1)}, bf16[1024,1728]{1,0:T(8,128)(2,1)}, bf16[512,1152]{1,0:T(8,128)(2,1)}, bf16[512,1152]{1,0:T(8,128)(2,1)}) custom-call(s32[128]{0:T(128)} %fusion.113.table, bf16[512,1152]{1,0:T(8,128)(2,1)} %get-tuple-element.125.first_ref.refs_0_, bf16[512,1152]{1,0:T(8,128)(2,1)} %copy-done.12, ...), custom_call_target="tpu_custom_call" | custom-call | flops 12230590464 | bytes 26099712 | tf_op jit(solution)/shard_map/feed_back/pallas_call | solution.py:566
  405.6 29.0 %feed_back.3 = (bf16[1024,1728]{1,0:T(8,128)(2,1)}, bf16[1024,1728]{1,0:T(8,128)(2,1)}, bf16[512,1152]{1,0:T(8,128)(2,1)}, bf16[512,1152]{1,0:T(8,128)(2,1)}) custom-call(s32[128]{0:T(128)} %fusion.113.table, bf16[512,1152]{1,0:T(8,128)(2,1)} %collective-permute-done.38.first_ref.refs_2_, bf16[512,1152]{1,0:T(8,128)(2,1)} %copy-done.14, ...), custom_call_target="tpu_custom_call" | custom-call | flops 12230590464 | bytes 26099712 | tf_op jit(solution)/shard_map/feed_back/pallas_call | solution.py:566
  442.1 14.3 %down_grad.1.refs_2_.refs_3_.refs_4_.refs_5_ = bf16[8,1,144,1728]{3,2,1,0:T(8,128)(2,1)} custom-call(bf16[512,1152]{1,0:T(8,128)(2,1)} %get-tuple-element.125.first_ref.refs_0_, bf16[512,1152]{1,0:T(8,128)(2,1)S(1)} %copy-done.13, bf16[512,1152]{1,0:T(8,128)(2,1)} %collective-permute-done.38.first_ref.refs_2_, bf16[512,1152]{1,0:T(8,128)(2,1)S(1)} %copy-done.15, ...), custom_call_target="tpu_custom_call" | custom-call | flops 3057647616 | bytes 9879552 | tf_op jit(solution)/shard_map/down_grad/pallas_call | solution.py:663
  456.4 23.7 %gate_up_grad.1.refs_0_.refs_1_.refs_2_.refs_3_ = bf16[8,2,144,1728]{3,2,1,0:T(8,128)(2,1)} custom-call(bf16[512,1152]{1,0:T(8,128)(2,1)S(1)} %copy-done.2, bf16[512,1152]{1,0:T(8,128)(2,1)} %collective-permute-done.30.second_ref.refs_1_, bf16[512,1152]{1,0:T(8,128)(2,1)} %collective-permute-done.32.first_ref.refs_2_, bf16[512,1152]{1,0:T(8,128)(2,1)S(1)} %copy-done.11, ...), custom_call_target="tpu_custom_call" | custom-call | flops 6115295232 | bytes 17399808 | tf_op jit(solution)/shard_map/gate_up_grad/pallas_call | solution.py:663
  490.7 6.0 mixed_back.1
  509.1 33.2 %attend_back.1 = (f32[512,1024]{1,0:T(8,128)}, f32[512,512]{1,0:T(8,128)}, bf16[8,512,512]{2,1,0:T(8,128)(2,1)}, bf16[8,512,512]{2,1,0:T(8,128)(2,1)}) custom-call(s32[128]{0:T(128)} %fusion.113.table, s32[4]{0:T(128)} %mapped.3, s32[4]{0:T(128)} %length.5, bf16[512,1024]{1,0:T(8,128)(2,1)} %copy-done.20, ...), custom_call_target="tpu_custom_call" | custom-call | flops 12079595520 | bytes 19398656 | tf_op jit(solution)/shard_map/attend_back/pallas_call | solution.py:419
  575.8 32.9 %collective-permute-done.48.refs_1_ = bf16[208,1728]{1,0:T(8,128)(2,1)} collective-permute-done((bf16[208,1728]{1,0:T(8,128)(2,1)}, bf16[208,1728]{1,0:T(8,128)(2,1)}, u32[]{:S(2)}, u32[]{:S(2)}) %collective-permute-start.48) | collective-permute-done | bytes 718880 | tf_op jit(solution)/shard_map/ppermute | solution.py:57
  627.8 14.1 %collective-permute-done.50.refs_1_ = bf16[208,1728]{1,0:T(8,128)(2,1)} collective-permute-done((bf16[208,1728]{1,0:T(8,128)(2,1)}, bf16[208,1728]{1,0:T(8,128)(2,1)}, u32[]{:S(2)}, u32[]{:S(2)}) %collective-permute-start.50) | collective-permute-done | bytes 718880 | tf_op jit(solution)/shard_map/ppermute | solution.py:57
  649.9 10.9 %collective-permute-done.62 = bf16[4,144,512]{2,1,0:T(8,128)(2,1)} collective-permute-done((bf16[4,144,512]{2,1,0:T(8,128)(2,1)S(1)}, bf16[4,144,512]{2,1,0:T(8,128)(2,1)}, u32[]{:S(2)}, u32[]{:S(2)}) %collective-permute-start.62) | collective-permute-done | bytes 589856 | tf_op jit(solution)/shard_map/ppermute | solution.py:43
  669.2 7.2 collective-permute-done.52.refs_1_
  729.6 18.7 %collective-permute-done.58 = f32[48,128]{1,0:T(8,128)S(1)} collective-permute-done((f32[48,128]{1,0:T(8,128)S(1)}, f32[48,128]{1,0:T(8,128)S(1)}, u32[]{:S(2)}, u32[]{:S(2)}) %collective-permute-start.58) | collective-permute-done | bytes 24608 | tf_op jit(solution)/shard_map/ppermute | solution.py:43
  (550 shorter events, 319.9 us)
Async XLA Ops:
  7.2 206.4 %all-gather.3.cloned.1.call-start = ((), (), s32[]{:S(2)}) async-start(), calls=%async_computation.2 | async-start | bytes 4718592 | tf_op jit(solution)/shard_map/all_gather | solution.py:863
  77.1 31.8 %collective-permute-start.16 = (bf16[224,1728]{1,0:T(8,128)(2,1)}, bf16[224,1728]{1,0:T(8,128)(2,1)}, u32[]{:S(2)}, u32[]{:S(2)}) collective-permute-start(bf16[224,1728]{1,0:T(8,128)(2,1)} %collective-permute-done.11.refs_1_), channel_id=1, source_target_pairs={{0,8},{8,16},{16,24},{24,28},{28,20},{20,12},{12,4},{4,0},{1,9},{9... | collective-permute-start | bytes 2322440 | tf_op jit(solution)/shard_map/ppermute | solution.py:57
  77.4 31.5 %collective-permute-start.18 = (bf16[208,1728]{1,0:T(8,128)(2,1)}, bf16[208,1728]{1,0:T(8,128)(2,1)}, u32[]{:S(2)}, u32[]{:S(2)}) collective-permute-start(bf16[208,1728]{1,0:T(8,128)(2,1)} %collective-permute-done.12.refs_9_), channel_id=1, source_target_pairs={{0,4},{8,0},{16,8},{24,16},{28,24},{20,28},{12,20},{4,12},{1,5},{9... | collective-permute-start | bytes 2156552 | tf_op jit(solution)/shard_map/ppermute | solution.py:57
  109.0 574.4 %reduce-scatter.2.cloned.1.call-start = ((), (), s32[]{:S(2)}) async-start(), calls=%async_computation.1 | async-start | bytes 4718592 | tf_op jit(solution)/shard_map/reduce_scatter | solution.py:981
  109.0 33.2 %collective-permute-start.15 = (bf16[8,144,512]{2,1,0:T(8,128)(2,1)}, bf16[8,144,512]{2,1,0:T(8,128)(2,1)}, u32[]{:S(2)}, u32[]{:S(2)}) collective-permute-start(bf16[8,144,512]{2,1,0:T(8,128)(2,1)} %constant_dynamic-update-slice_fusion.5.refs_0_), channel_id=1, source_target_pairs={{0,2},{1,3},{2,0},{3,1},{4,6},{5,7},{6,4},{7,5},{8,10},{9,11},{10,... | collective-permute-start | bytes 3538952 | tf_op jit(solution)/shard_map/ppermute | solution.py:38
  109.1 33.1 %collective-permute-start.17 = (bf16[224,1728]{1,0:T(8,128)(2,1)}, bf16[224,1728]{1,0:T(8,128)(2,1)S(1)}, u32[]{:S(2)}, u32[]{:S(2)}) collective-permute-start(bf16[224,1728]{1,0:T(8,128)(2,1)} %collective-permute-done.16.refs_2_), channel_id=1, source_target_pairs={{0,8},{8,16},{16,24},{24,28},{28,20},{20,12},{12,4},{4,0},{1,9},{9... | collective-permute-start | bytes 2322440 | tf_op jit(solution)/shard_map/ppermute | solution.py:57
  109.2 33.1 %collective-permute-start.19 = (bf16[208,1728]{1,0:T(8,128)(2,1)}, bf16[208,1728]{1,0:T(8,128)(2,1)S(1)}, u32[]{:S(2)}, u32[]{:S(2)}) collective-permute-start(bf16[208,1728]{1,0:T(8,128)(2,1)} %collective-permute-done.18.refs_10_), channel_id=1, source_target_pairs={{0,4},{8,0},{16,8},{24,16},{28,24},{20,28},{12,20},{4,12},{1,5},{9... | collective-permute-start | bytes 2156552 | tf_op jit(solution)/shard_map/ppermute | solution.py:57
  111.2 34.6 %collective-permute-start.14 = (bf16[8,144,512]{2,1,0:T(8,128)(2,1)}, bf16[8,144,512]{2,1,0:T(8,128)(2,1)}, u32[]{:S(2)}, u32[]{:S(2)}) collective-permute-start(bf16[8,144,512]{2,1,0:T(8,128)(2,1)} %constant_dynamic-update-slice_fusion.5.refs_0_), channel_id=1, source_target_pairs={{0,1},{1,0},{2,3},{3,2},{4,5},{5,4},{6,7},{7,6},{8,9},{9,8},{10,11... | collective-permute-start | bytes 3538952 | tf_op jit(solution)/shard_map/ppermute | solution.py:34
  143.5 49.8 %collective-permute-start.24 = (bf16[208,1728]{1,0:T(8,128)(2,1)}, bf16[208,1728]{1,0:T(8,128)(2,1)}, u32[]{:S(2)}, u32[]{:S(2)}) collective-permute-start(bf16[208,1728]{1,0:T(8,128)(2,1)} %copy-done.119), channel_id=1, source_target_pairs={{0,4},{8,0},{16,8},{24,16},{28,24},{20,28},{12,20},{4,12},{1,5},{9... | collective-permute-start | bytes 2156552 | tf_op jit(solution)/shard_map/ppermute | solution.py:57
  144.8 36.9 %collective-permute-start.21 = (bf16[224,1728]{1,0:T(8,128)(2,1)}, bf16[224,1728]{1,0:T(8,128)(2,1)}, u32[]{:S(2)}, u32[]{:S(2)}) collective-permute-start(bf16[224,1728]{1,0:T(8,128)(2,1)} %copy-done.117), channel_id=1, source_target_pairs={{0,8},{8,16},{16,24},{24,28},{28,20},{20,12},{12,4},{4,0},{1,9},{9... | collective-permute-start | bytes 2322440 | tf_op jit(solution)/shard_map/ppermute | solution.py:57
  181.7 31.9 %collective-permute-start.22 = (bf16[224,1728]{1,0:T(8,128)(2,1)}, bf16[224,1728]{1,0:T(8,128)(2,1)}, u32[]{:S(2)}, u32[]{:S(2)}) collective-permute-start(bf16[224,1728]{1,0:T(8,128)(2,1)} %collective-permute-done.21.refs_4_), channel_id=1, source_target_pairs={{0,8},{8,16},{16,24},{24,28},{28,20},{20,12},{12,4},{4,0},{1,9},{9... | collective-permute-start | bytes 2322440 | tf_op jit(solution)/shard_map/ppermute | solution.py:57
  368.5 33.0 %collective-permute-start.38 = (bf16[512,1152]{1,0:T(8,128)(2,1)}, bf16[512,1152]{1,0:T(8,128)(2,1)}, u32[]{:S(2)}, u32[]{:S(2)}) collective-permute-start(bf16[512,1152]{1,0:T(8,128)(2,1)} %get-tuple-element.125.first_ref.refs_0_), channel_id=1, source_target_pairs={{0,2},{1,3},{2,0},{3,1},{4,6},{5,7},{6,4},{7,5},{8,10},{9,11},{10,... | collective-permute-start | bytes 3538952 | tf_op jit(solution)/shard_map/ppermute | solution.py:38
  434.9 52.2 %collective-permute-start.37 = (bf16[512,1152]{1,0:T(8,128)(2,1)}, bf16[512,1152]{1,0:T(8,128)(2,1)S(1)}, u32[]{:S(2)}, u32[]{:S(2)}) collective-permute-start(bf16[512,1152]{1,0:T(8,128)(2,1)} %get-tuple-element.111), channel_id=1, source_target_pairs={{0,1},{1,0},{2,3},{3,2},{4,5},{5,4},{6,7},{7,6},{8,9},{9,8},{10,11... | collective-permute-start | bytes 3538952 | tf_op jit(solution)/shard_map/ppermute | solution.py:34
  440.4 47.7 %collective-permute-start.41 = (bf16[512,1152]{1,0:T(8,128)(2,1)}, bf16[512,1152]{1,0:T(8,128)(2,1)}, u32[]{:S(2)}, u32[]{:S(2)}) collective-permute-start(bf16[512,1152]{1,0:T(8,128)(2,1)} %add_convert_fusion.1), channel_id=1, source_target_pairs={{0,2},{1,3},{2,0},{3,1},{4,6},{5,7},{6,4},{7,5},{8,10},{9,11},{10,... | collective-permute-start | bytes 3538952 | tf_op jit(solution)/shard_map/ppermute | solution.py:38
  507.0 35.3 %collective-permute-start.45 = (bf16[208,1728]{1,0:T(8,128)(2,1)}, bf16[208,1728]{1,0:T(8,128)(2,1)S(1)}, u32[]{:S(2)}, u32[]{:S(2)}) collective-permute-start(bf16[208,1728]{1,0:T(8,128)(2,1)} %get-tuple-element.131.refs_3_), channel_id=1, source_target_pairs={{0,8},{8,16},{16,24},{24,28},{28,20},{20,12},{12,4},{4,0},{1,9},{9... | collective-permute-start | bytes 2156552 | tf_op jit(solution)/shard_map/ppermute | solution.py:57
  508.0 34.4 %collective-permute-start.44 = (bf16[224,1728]{1,0:T(8,128)(2,1)}, bf16[224,1728]{1,0:T(8,128)(2,1)S(1)}, u32[]{:S(2)}, u32[]{:S(2)}) collective-permute-start(bf16[224,1728]{1,0:T(8,128)(2,1)} %get-tuple-element.130.refs_2_), channel_id=1, source_target_pairs={{0,4},{8,0},{16,8},{24,16},{28,24},{20,28},{12,20},{4,12},{1,5},{9... | collective-permute-start | bytes 2322440 | tf_op jit(solution)/shard_map/ppermute | solution.py:57
  563.2 56.0 %collective-permute-start.59 = (bf16[1152,512]{0,1:T(8,128)(2,1)}, bf16[1152,512]{0,1:T(8,128)(2,1)}, u32[]{:S(2)}, u32[]{:S(2)}) collective-permute-start(bf16[1152,512]{0,1:T(8,128)(2,1)} %pad_maximum_fusion), channel_id=1, source_target_pairs={{0,1},{1,0},{2,3},{3,2},{4,5},{5,4},{6,7},{7,6},{8,9},{9,8},{10,11... | collective-permute-start | bytes 3538952 | tf_op jit(solution)/shard_map/ppermute | solution.py:34
  566.2 52.9 %collective-permute-start.61 = (bf16[1152,512]{0,1:T(8,128)(2,1)}, bf16[1152,512]{0,1:T(8,128)(2,1)}, u32[]{:S(2)}, u32[]{:S(2)}) collective-permute-start(bf16[1152,512]{0,1:T(8,128)(2,1)} %fusion.4), channel_id=1, source_target_pairs={{0,2},{1,3},{2,0},{3,1},{4,6},{5,7},{6,4},{7,5},{8,10},{9,11},{10,... | collective-permute-start | bytes 3538952 | tf_op jit(solution)/shard_map/ppermute | solution.py:38
  573.7 39.7 %collective-permute-start.47 = (bf16[224,1728]{1,0:T(8,128)(2,1)}, bf16[224,1728]{1,0:T(8,128)(2,1)}, u32[]{:S(2)}, u32[]{:S(2)}) collective-permute-start(bf16[224,1728]{1,0:T(8,128)(2,1)} %get-tuple-element.137), channel_id=1, source_target_pairs={{0,4},{8,0},{16,8},{24,16},{28,24},{20,28},{12,20},{4,12},{1,5},{9... | collective-permute-start | bytes 2322440 | tf_op jit(solution)/shard_map/ppermute | solution.py:57
  574.0 34.6 %collective-permute-start.48 = (bf16[208,1728]{1,0:T(8,128)(2,1)}, bf16[208,1728]{1,0:T(8,128)(2,1)}, u32[]{:S(2)}, u32[]{:S(2)}) collective-permute-start(bf16[208,1728]{1,0:T(8,128)(2,1)} %get-tuple-element.138), channel_id=1, source_target_pairs={{0,8},{8,16},{16,24},{24,28},{28,20},{20,12},{12,4},{4,0},{1,9},{9... | collective-permute-start | bytes 2156552 | tf_op jit(solution)/shard_map/ppermute | solution.py:57
  627.4 33.3 %collective-permute-start.62 = (bf16[4,144,512]{2,1,0:T(8,128)(2,1)S(1)}, bf16[4,144,512]{2,1,0:T(8,128)(2,1)}, u32[]{:S(2)}, u32[]{:S(2)}) collective-permute-start(bf16[4,144,512]{2,1,0:T(8,128)(2,1)S(1)} %fusion.11), channel_id=1, source_target_pairs={{0,4},{4,0},{8,12},{12,8},{16,20},{20,16},{24,28},{28,24},{1,5},{5... | collective-permute-start | bytes 1769480 | tf_op jit(solution)/shard_map/ppermute | solution.py:43
  646.7 33.1 %collective-permute-start.51 = (bf16[224,1728]{1,0:T(8,128)(2,1)}, bf16[224,1728]{1,0:T(8,128)(2,1)}, u32[]{:S(2)}, u32[]{:S(2)}) collective-permute-start(bf16[224,1728]{1,0:T(8,128)(2,1)} %get-tuple-element.141), channel_id=1, source_target_pairs={{0,4},{8,0},{16,8},{24,16},{28,24},{20,28},{12,20},{4,12},{1,5},{9... | collective-permute-start | bytes 2322440 | tf_op jit(solution)/shard_map/ppermute | solution.py:57
  723.0 34.8 %collective-permute-start.76 = (bf16[208,1728]{1,0:T(8,128)(2,1)}, bf16[208,1728]{1,0:T(8,128)(2,1)}, u32[]{:S(2)}, u32[]{:S(2)}) collective-permute-start(bf16[208,1728]{1,0:T(8,128)(2,1)} %get-tuple-element.154), channel_id=1, source_target_pairs={{0,8},{8,16},{16,24},{24,28},{28,20},{20,12},{12,4},{4,0},{1,9},{9... | collective-permute-start | bytes 2156552 | tf_op jit(solution)/shard_map/ppermute | solution.py:57
  725.0 32.8 %collective-permute-start.75 = (bf16[224,1728]{1,0:T(8,128)(2,1)}, bf16[224,1728]{1,0:T(8,128)(2,1)}, u32[]{:S(2)}, u32[]{:S(2)}) collective-permute-start(bf16[224,1728]{1,0:T(8,128)(2,1)} %get-tuple-element.153), channel_id=1, source_target_pairs={{0,4},{8,0},{16,8},{24,16},{28,24},{20,28},{12,20},{4,12},{1,5},{9... | collective-permute-start | bytes 2322440 | tf_op jit(solution)/shard_map/ppermute | solution.py:57
  (176 other events, 2492.2 us)
Sparse Core Ops, SparseCore 0:
  109.1 100.2 all-gather.2
  551.9 120.3 reduce-scatter.1

commit v5 on v4

--- a/solution.py
+++ b/solution.py
@@ -136,6 +136,27 @@
         value = value + swap_bit(value, bit)
         bit *= 2
     return value
+
+
+def sum_both(parts, small, fsdp_pos):
+    z, y = fsdp_pos // 2, fsdp_pos % 2
+    moved = swap_core(parts[1].astype(bf)), swap_core(parts[3].astype(bf)), swap_core(small)
+    far = (parts[2].astype(f32) + moved[1].astype(f32)).astype(bf)
+    near = parts[0].astype(f32) + moved[0].astype(f32)
+    far, near, small = lax.optimization_barrier((far, near, small + moved[2]))
+    moved = swap_x(far), swap_x(small)
+    column = near + moved[0].astype(f32)
+    column, small = lax.optimization_barrier((column, small + moved[1]))
+    paired = column.reshape((4, 2) + column.shape[1:])
+    moved = swap_bit(pick(paired, 1 - y, 1).astype(bf), 1), swap_bit(small, 1)
+    column = pick(paired, y, 1) + moved[0].astype(f32)
+    column, small = lax.optimization_barrier((column, small + moved[1]))
+    moved = [shift_z(pick(column, (z + step) % 4).astype(bf), step) for step in (1, 2, 3)]
+    small = small + swap_bit(small, 2)
+    total = pick(column, z)
+    for part in moved:
+        total = total + part.astype(f32)
+    return total, small + swap_bit(small, 4), column
 
 
 class Spread:
@@ -969,6 +990,30 @@
     grad_query_rot, grad_own, kept, given = attend_back(
         table, cont_prompt, cont_length, query_rot, grad_attn_rows, log_sum, own_pairs, sources, held_sums if ringed else ()
     )
+    _, query_pull = jax.vjp(
+        lambda raw, gain: tuple(
+            head_prep(raw[:, h * HEAD : (h + 1) * HEAD], gain, cosine, sine_part)
+            for h in range(HEADS)
+        ),
+        query_raw,
+        query_gain,
+    )
+    grad_query_raw, grad_query_gain = query_pull(
+        tuple(grad_query_rot[:, h * HEAD : (h + 1) * HEAD] for h in range(HEADS))
+    )
+    grad_query_low = grad_query_raw.astype(bf)
+    grad_query_w = dot_tn(normed_in, grad_query_low)
+    qo_sum = collect_tensor(
+        *(
+            jnp.concatenate(
+                [grad_query_w[:, h * HEAD : (h + 1) * HEAD], grad_out_w[:, h * HEAD : (h + 1) * HEAD]],
+                1,
+            )
+            for h in range(HEADS)
+        )
+    ).reshape(members, dim // members, 2 * HEAD)
+    out_qo = collect_fsdp(qo_sum, fsdp_pos)
+    out_query, out_out = out_qo[:, :HEAD], out_qo[:, HEAD:].T
     if ringed:
         moved = move_sums()
         given = after(given, *moved)
@@ -988,24 +1033,11 @@
     back = lax.ppermute(summed.astype(bf), "tensor", [(2, 0), (3, 1)]).astype(f32)
     grad_pairs = jnp.where(is_cont, grad_own, summed + back)
 
-    _, query_pull = jax.vjp(
-        lambda raw, gain: tuple(
-            head_prep(raw[:, h * HEAD : (h + 1) * HEAD], gain, cosine, sine_part)
-            for h in range(HEADS)
-        ),
-        query_raw,
-        query_gain,
-    )
-    grad_query_raw, grad_query_gain = query_pull(
-        tuple(grad_query_rot[:, h * HEAD : (h + 1) * HEAD] for h in range(HEADS))
-    )
     _, key_pull = jax.vjp(
         lambda raw, gain: head_prep(raw, gain, cosine, sine_part), key_raw, key_gain
     )
     grad_key_raw, grad_key_gain = key_pull(grad_pairs[:, :HEAD])
-    grad_query_low = grad_query_raw.astype(bf)
     grad_kv_low = jnp.concatenate([grad_key_raw, grad_pairs[:, HEAD:]], 1).astype(bf)
-    grad_query_w = dot_tn(normed_in, grad_query_low)
     grad_kv_w = dot_tn(normed_in, grad_kv_low)
     grad_input, grad_attn_gain = by_rows(
         input_kernel,
@@ -1022,28 +1054,13 @@
         ((row_kind, bf), gain_kind),
     )
 
-    qo_sum = collect_tensor(
-        *(
-            jnp.concatenate(
-                [grad_query_w[:, h * HEAD : (h + 1) * HEAD], grad_out_w[:, h * HEAD : (h + 1) * HEAD]],
-                1,
-            )
-            for h in range(HEADS)
-        )
-    ).reshape(members, dim // members, 2 * HEAD)
-    out_qo = collect_fsdp(qo_sum, fsdp_pos)
-    out_query, out_out = out_qo[:, :HEAD], out_qo[:, HEAD:].T
     kv_blocks = grad_kv_w.reshape(members, TENSOR, shard_kv, 2 * HEAD)
-    kv_column = collect_tensor(
-        *order_tensor([kv_blocks[:, t] for t in range(TENSOR)], tensor_pos)
-    )
-    out_kv = collect_fsdp(kv_column, fsdp_pos)
+    kv_parts = order_tensor([kv_blocks[:, t] for t in range(TENSOR)], tensor_pos)
 
     if ringed:
-        held_sums = add_sums(move_sums(), 1, grad_kv_w)
-        held_sums = add_sums(move_sums(), 0)
-        out_gate, out_up, out_down = held_sums
-    out_down = out_down.T
+        moved = move_sums()
+        kv_parts = kv_parts[:1] + (after(kv_parts[1], out_qo, *moved),) + kv_parts[2:]
+        held_sums = add_sums(moved, 1)
 
     small = jnp.concatenate(
         [
@@ -1058,7 +1075,14 @@
     )
     length = small.shape[0]
     small = jnp.pad(small, (0, -length % 1024)).reshape(-1, 128)
-    small = sum_all(small).reshape(-1)
+    if ringed:
+        out_kv, small, column = sum_both(kv_parts, small, fsdp_pos)
+        out_gate, out_up, out_down = add_sums(move_sums(), 0, column)
+    else:
+        out_kv = collect_fsdp(collect_tensor(*kv_parts), fsdp_pos)
+        small = sum_all(small)
+    out_down = out_down.T
+    small = small.reshape(-1)
     device = fsdp_pos * TENSOR + tensor_pos
     wide = [
         lax.dynamic_slice(small, (k * dim + device * shard_gain,), (shard_gain,)) for k in range(4)

time: 779 us -> 777 us (level)
  waiting for transfers between devices: 272 us -> 264 us
    unnamed x257 -> x260, local copies, waits for them, and re-layouts: 25 us -> 25.5 us
  transfers between devices with their start and end apart: 79 -> 79, of which waited for: 35 -> 34; matrix products, arithmetic and copies ran while one was open for 13% -> 13% of each run, Pallas kernels for 25% -> 25%
where the time goes in v5:
time: 777 us; the launch traced here: 770 us
  waiting for transfers between devices  264 us (34%)
  Pallas kernels  254 us (33%)
  starting transfers between devices  98.5 us (13%)
  other arithmetic  60.3 us (8%)
  local copies, waits for them, and re-layouts  55.1 us (7%)
  between operations  19.6 us (3%)
  matrix products  18.9 us (2%)
    ppermute x28, waiting for transfers between devices, ring_step(): return lax.ppermute(value, 'fsdp', pairs)  143 us
    pallas_call x4, Pallas kernels, feed_call(): pl.pallas_call(functools.partial(kernel, len(pieces)), out_shape=(wide_sh...  109 us
    ppermute x7, waiting for transfers between devices, swap_bit(): return lax.ppermute(value, 'fsdp', [(f, f ^ bit) for f in range(size)])  53.5 us
    ppermute x28, starting transfers between devices, ring_step(): return lax.ppermute(value, 'fsdp', pairs)  41.8 us
    pallas_call x2, Pallas kernels, weight_grads(): pl.pallas_call(functools.partial(weight_grad_kernel, number), out_shape=j...  38 us
    ppermute x9, waiting for transfers between devices, swap_x(): return lax.ppermute(value, 'tensor', [(t, t ^ 2) for t in range(TENSOR)])  34.5 us
    pallas_call x1, Pallas kernels, attend_back(): pl.pallas_call(attend_back_kernel, out_shape=(jax.ShapeDtypeStruct((rows,...  33.2 us
    pallas_call x8, Pallas kernels, pass_on(): pl.pallas_call(functools.partial(pass_on_kernel, len(moved), last), out_s...  29.3 us
  transfers between devices with their start and end apart: 79, of which 34 were waited for; matrix products, arithmetic and copies ran while one was open for 13% of the time, Pallas kernels for 25%

profile of v5, /device:TPU:0, one launch (start us, length us, event | category | flops | bytes accessed | tf_op | source)
XLA Modules:
  0.0 769.9 jit_solution(15149330777363557801)
XLA Ops:
  32.2 6.6 collective-permute-done.5.refs_2_
  46.9 7.3 collective-permute-done.8
  87.7 20.4 %collective-permute-done.10 = bf16[4,144,512]{2,1,0:T(8,128)(2,1)S(1)} collective-permute-done((bf16[4,144,512]{2,1,0:T(8,128)(2,1)}, bf16[4,144,512]{2,1,0:T(8,128)(2,1)S(1)}, u32[]{:S(2)}, u32[]{:S(2)}) %collective-permute-start.10) | collective-permute-done | bytes 589856 | tf_op jit(solution)/shard_map/ppermute | solution.py:43
  111.2 31.0 %collective-permute-done.19.refs_11_ = bf16[208,1728]{1,0:T(8,128)(2,1)S(1)} collective-permute-done((bf16[208,1728]{1,0:T(8,128)(2,1)}, bf16[208,1728]{1,0:T(8,128)(2,1)S(1)}, u32[]{:S(2)}, u32[]{:S(2)}) %collective-permute-start.19) | collective-permute-done | bytes 718880 | tf_op jit(solution)/shard_map/ppermute | solution.py:57
  145.8 7.9 %place_heads.1 = (bf16[8,144,1024]{2,1,0:T(8,128)(2,1)}, bf16[8,144,1024]{2,1,0:T(8,128)(2,1)}) custom-call(s32[128]{0:T(128)} %fusion.114.table, bf16[8,144,512]{2,1,0:T(8,128)(2,1)} %constant_dynamic-update-slice_fusion.5.refs_0_, bf16[8,144,512]{2,1,0:T(8,128)(2,1)} %collective-permute-done.14.refs_1_, ...), custom_call_target="tpu_custom_call" | custom-call | tf_op jit(solution)/shard_map/place_heads/pallas_call | solution.py:277
  171.9 9.8 %collective-permute-done.21.refs_4_ = bf16[224,1728]{1,0:T(8,128)(2,1)} collective-permute-done((bf16[224,1728]{1,0:T(8,128)(2,1)}, bf16[224,1728]{1,0:T(8,128)(2,1)}, u32[]{:S(2)}, u32[]{:S(2)}) %collective-permute-start.21) | collective-permute-done | bytes 774176 | tf_op jit(solution)/shard_map/ppermute | solution.py:57
  181.8 8.9 %collective-permute-start.22 = (bf16[224,1728]{1,0:T(8,128)(2,1)}, bf16[224,1728]{1,0:T(8,128)(2,1)}, u32[]{:S(2)}, u32[]{:S(2)}) collective-permute-start(bf16[224,1728]{1,0:T(8,128)(2,1)} %collective-permute-done.21.refs_4_), channel_id=1, source_target_pairs={{0,8},{8,16},{16,24},{24,28},{28,20},{20,12},{12,4},{4,0},{1,9},{9... | collective-permute-start | bytes 2322440 | tf_op jit(solution)/shard_map/ppermute | solution.py:57
  198.5 13.1 %collective-permute-done.25.refs_13_ = bf16[208,1728]{1,0:T(8,128)(2,1)} collective-permute-done((bf16[208,1728]{1,0:T(8,128)(2,1)}, bf16[208,1728]{1,0:T(8,128)(2,1)}, u32[]{:S(2)}, u32[]{:S(2)}) %collective-permute-start.25) | collective-permute-done | bytes 718880 | tf_op jit(solution)/shard_map/ppermute | solution.py:57
  219.5 16.0 %collective-permute-done.26.refs_14_ = bf16[208,1728]{1,0:T(8,128)(2,1)} collective-permute-done((bf16[208,1728]{1,0:T(8,128)(2,1)}, bf16[208,1728]{1,0:T(8,128)(2,1)}, u32[]{:S(2)}, u32[]{:S(2)}) %collective-permute-start.26) | collective-permute-done | bytes 718880 | tf_op jit(solution)/shard_map/ppermute | solution.py:57
  241.5 18.3 %attend.1 = (bf16[512,1024]{1,0:T(8,128)(2,1)S(1)}, f32[8,1,256]{2,1,0:T(1,128)S(1)}) custom-call(s32[128]{0:T(128)S(1)} %copy-done.18, s32[4]{0:T(128)S(1)} %copy-done.32, s32[4]{0:T(128)S(1)} %copy-done.30, bf16[512,1024]{1,0:T(8,128)(2,1)S(1)} %copy-done.21, bf16[512,512]{1,0:T(8,128)(2,1)S(1)} %pad_maximum_fusion.5.own_ref, ...), custom_call_target="tpu_custom_call" | custom-call | flops 4831838208 | bytes 6815744 | tf_op jit(solution)/shard_map/attend/pallas_call | solution.py:376
  270.2 25.2 %feed.2 = (bf16[1024,1728]{1,0:T(8,128)(2,1)}, bf16[1024,1728]{1,0:T(8,128)(2,1)}, bf16[1024,1728]{1,0:T(8,128)(2,1)}, bf16[512,1152]{1,0:T(8,128)(2,1)}, bf16[512,1152]{1,0:T(8,128)(2,1)}) custom-call(s32[128]{0:T(128)} %fusion.114.table, bf16[512,1152]{1,0:T(8,128)(2,1)} %copy-done.1, bf16[512,1152]{1,0:T(8,128)(2,1)} %collective-permute-done.30.second_ref.refs_1_, ...), custom_call_target="tpu_custom_call" | custom-call | flops 12230590464 | bytes 22560768 | tf_op jit(solution)/shard_map/feed/pallas_call | solution.py:587
  300.2 25.5 %feed.3 = (bf16[1024,1728]{1,0:T(8,128)(2,1)}, bf16[1024,1728]{1,0:T(8,128)(2,1)}, bf16[1024,1728]{1,0:T(8,128)(2,1)}, bf16[512,1152]{1,0:T(8,128)(2,1)}, bf16[512,1152]{1,0:T(8,128)(2,1)}) custom-call(s32[128]{0:T(128)} %fusion.114.table, bf16[512,1152]{1,0:T(8,128)(2,1)} %collective-permute-done.32.first_ref.refs_2_, bf16[512,1152]{1,0:T(8,128)(2,1)} %copy-done.10, ...), custom_call_target="tpu_custom_call" | custom-call | flops 12230590464 | bytes 22560768 | tf_op jit(solution)/shard_map/feed/pallas_call | solution.py:587
  335.7 24.4 %collective-permute-done.35.refs_2_ = bf16[512,1152]{1,0:T(8,128)(2,1)} collective-permute-done((bf16[512,1152]{1,0:T(8,128)(2,1)}, bf16[512,1152]{1,0:T(8,128)(2,1)}, u32[]{:S(2)}, u32[]{:S(2)}) %collective-permute-start.35) | collective-permute-done | bytes 1179680 | tf_op jit(solution)/shard_map/ppermute | solution.py:38
  372.6 28.9 %feed_back.2 = (bf16[1024,1728]{1,0:T(8,128)(2,1)}, bf16[1024,1728]{1,0:T(8,128)(2,1)}, bf16[512,1152]{1,0:T(8,128)(2,1)}, bf16[512,1152]{1,0:T(8,128)(2,1)}) custom-call(s32[128]{0:T(128)} %fusion.114.table, bf16[512,1152]{1,0:T(8,128)(2,1)} %get-tuple-element.133.first_ref.refs_0_, bf16[512,1152]{1,0:T(8,128)(2,1)} %copy-done.12, ...), custom_call_target="tpu_custom_call" | custom-call | flops 12230590464 | bytes 26099712 | tf_op jit(solution)/shard_map/feed_back/pallas_call | solution.py:587
  405.6 29.0 %feed_back.3 = (bf16[1024,1728]{1,0:T(8,128)(2,1)}, bf16[1024,1728]{1,0:T(8,128)(2,1)}, bf16[512,1152]{1,0:T(8,128)(2,1)}, bf16[512,1152]{1,0:T(8,128)(2,1)}) custom-call(s32[128]{0:T(128)} %fusion.114.table, bf16[512,1152]{1,0:T(8,128)(2,1)} %collective-permute-done.38.first_ref.refs_2_, bf16[512,1152]{1,0:T(8,128)(2,1)} %copy-done.14, ...), custom_call_target="tpu_custom_call" | custom-call | flops 12230590464 | bytes 26099712 | tf_op jit(solution)/shard_map/feed_back/pallas_call | solution.py:587
  442.1 14.3 %down_grad.1.refs_2_.refs_3_.refs_4_.refs_5_ = bf16[8,1,144,1728]{3,2,1,0:T(8,128)(2,1)} custom-call(bf16[512,1152]{1,0:T(8,128)(2,1)} %get-tuple-element.133.first_ref.refs_0_, bf16[512,1152]{1,0:T(8,128)(2,1)S(1)} %copy-done.13, bf16[512,1152]{1,0:T(8,128)(2,1)} %collective-permute-done.38.first_ref.refs_2_, bf16[512,1152]{1,0:T(8,128)(2,1)S(1)} %copy-done.15, ...), custom_call_target="tpu_custom_call" | custom-call | flops 3057647616 | bytes 9879552 | tf_op jit(solution)/shard_map/down_grad/pallas_call | solution.py:684
  456.4 23.7 %gate_up_grad.1.refs_0_.refs_1_.refs_2_.refs_3_ = bf16[8,2,144,1728]{3,2,1,0:T(8,128)(2,1)} custom-call(bf16[512,1152]{1,0:T(8,128)(2,1)S(1)} %copy-done.2, bf16[512,1152]{1,0:T(8,128)(2,1)} %collective-permute-done.30.second_ref.refs_1_, bf16[512,1152]{1,0:T(8,128)(2,1)} %collective-permute-done.32.first_ref.refs_2_, bf16[512,1152]{1,0:T(8,128)(2,1)S(1)} %copy-done.11, ...), custom_call_target="tpu_custom_call" | custom-call | flops 6115295232 | bytes 17399808 | tf_op jit(solution)/shard_map/gate_up_grad/pallas_call | solution.py:684
  490.7 6.0 mixed_back.1
  509.2 33.2 %attend_back.1 = (f32[512,1024]{1,0:T(8,128)}, f32[512,512]{1,0:T(8,128)}, bf16[8,512,512]{2,1,0:T(8,128)(2,1)}, bf16[8,512,512]{2,1,0:T(8,128)(2,1)}) custom-call(s32[128]{0:T(128)} %fusion.114.table, s32[4]{0:T(128)} %mapped.3, s32[4]{0:T(128)} %length.5, bf16[512,1024]{1,0:T(8,128)(2,1)} %copy-done.20, ...), custom_call_target="tpu_custom_call" | custom-call | flops 12079595520 | bytes 19398656 | tf_op jit(solution)/shard_map/attend_back/pallas_call | solution.py:440
  575.8 32.9 %collective-permute-done.48.refs_1_ = bf16[208,1728]{1,0:T(8,128)(2,1)} collective-permute-done((bf16[208,1728]{1,0:T(8,128)(2,1)}, bf16[208,1728]{1,0:T(8,128)(2,1)}, u32[]{:S(2)}, u32[]{:S(2)}) %collective-permute-start.48) | collective-permute-done | bytes 718880 | tf_op jit(solution)/shard_map/ppermute | solution.py:57
  627.2 14.0 %collective-permute-done.50.refs_1_ = bf16[208,1728]{1,0:T(8,128)(2,1)} collective-permute-done((bf16[208,1728]{1,0:T(8,128)(2,1)}, bf16[208,1728]{1,0:T(8,128)(2,1)}, u32[]{:S(2)}, u32[]{:S(2)}) %collective-permute-start.50) | collective-permute-done | bytes 718880 | tf_op jit(solution)/shard_map/ppermute | solution.py:57
  649.2 10.9 %collective-permute-done.58 = bf16[4,144,512]{2,1,0:T(8,128)(2,1)} collective-permute-done((bf16[4,144,512]{2,1,0:T(8,128)(2,1)S(1)}, bf16[4,144,512]{2,1,0:T(8,128)(2,1)}, u32[]{:S(2)}, u32[]{:S(2)}) %collective-permute-start.58) | collective-permute-done | bytes 589856 | tf_op jit(solution)/shard_map/ppermute | solution.py:43
  668.6 7.2 collective-permute-done.52.refs_1_
  726.8 15.3 %collective-permute-done.69 = f32[48,128]{1,0:T(8,128)S(1)} collective-permute-done((f32[48,128]{1,0:T(8,128)S(1)}, f32[48,128]{1,0:T(8,128)S(1)}, u32[]{:S(2)}, u32[]{:S(2)}) %collective-permute-start.69) | collective-permute-done | bytes 24608 | tf_op jit(solution)/shard_map/ppermute | solution.py:43
  (551 shorter events, 320.4 us)
Async XLA Ops:
  7.2 206.4 %all-gather.3.cloned.1.call-start = ((), (), s32[]{:S(2)}) async-start(), calls=%async_computation.2 | async-start | bytes 4718592 | tf_op jit(solution)/shard_map/all_gather | solution.py:884
  77.1 31.8 %collective-permute-start.16 = (bf16[224,1728]{1,0:T(8,128)(2,1)}, bf16[224,1728]{1,0:T(8,128)(2,1)}, u32[]{:S(2)}, u32[]{:S(2)}) collective-permute-start(bf16[224,1728]{1,0:T(8,128)(2,1)} %collective-permute-done.11.refs_1_), channel_id=1, source_target_pairs={{0,8},{8,16},{16,24},{24,28},{28,20},{20,12},{12,4},{4,0},{1,9},{9... | collective-permute-start | bytes 2322440 | tf_op jit(solution)/shard_map/ppermute | solution.py:57
  77.5 31.5 %collective-permute-start.18 = (bf16[208,1728]{1,0:T(8,128)(2,1)}, bf16[208,1728]{1,0:T(8,128)(2,1)}, u32[]{:S(2)}, u32[]{:S(2)}) collective-permute-start(bf16[208,1728]{1,0:T(8,128)(2,1)} %collective-permute-done.12.refs_9_), channel_id=1, source_target_pairs={{0,4},{8,0},{16,8},{24,16},{28,24},{20,28},{12,20},{4,12},{1,5},{9... | collective-permute-start | bytes 2156552 | tf_op jit(solution)/shard_map/ppermute | solution.py:57
  109.0 573.8 %reduce-scatter.2.cloned.1.call-start = ((), (), s32[]{:S(2)}) async-start(), calls=%async_computation.1 | async-start | bytes 4718592 | tf_op jit(solution)/shard_map/reduce_scatter | solution.py:1026
  109.0 33.2 %collective-permute-start.15 = (bf16[8,144,512]{2,1,0:T(8,128)(2,1)}, bf16[8,144,512]{2,1,0:T(8,128)(2,1)}, u32[]{:S(2)}, u32[]{:S(2)}) collective-permute-start(bf16[8,144,512]{2,1,0:T(8,128)(2,1)} %constant_dynamic-update-slice_fusion.5.refs_0_), channel_id=1, source_target_pairs={{0,2},{1,3},{2,0},{3,1},{4,6},{5,7},{6,4},{7,5},{8,10},{9,11},{10,... | collective-permute-start | bytes 3538952 | tf_op jit(solution)/shard_map/ppermute | solution.py:38
  109.1 33.1 %collective-permute-start.17 = (bf16[224,1728]{1,0:T(8,128)(2,1)}, bf16[224,1728]{1,0:T(8,128)(2,1)S(1)}, u32[]{:S(2)}, u32[]{:S(2)}) collective-permute-start(bf16[224,1728]{1,0:T(8,128)(2,1)} %collective-permute-done.16.refs_2_), channel_id=1, source_target_pairs={{0,8},{8,16},{16,24},{24,28},{28,20},{20,12},{12,4},{4,0},{1,9},{9... | collective-permute-start | bytes 2322440 | tf_op jit(solution)/shard_map/ppermute | solution.py:57
  109.2 33.1 %collective-permute-start.19 = (bf16[208,1728]{1,0:T(8,128)(2,1)}, bf16[208,1728]{1,0:T(8,128)(2,1)S(1)}, u32[]{:S(2)}, u32[]{:S(2)}) collective-permute-start(bf16[208,1728]{1,0:T(8,128)(2,1)} %collective-permute-done.18.refs_10_), channel_id=1, source_target_pairs={{0,4},{8,0},{16,8},{24,16},{28,24},{20,28},{12,20},{4,12},{1,5},{9... | collective-permute-start | bytes 2156552 | tf_op jit(solution)/shard_map/ppermute | solution.py:57
  111.2 34.6 %collective-permute-start.14 = (bf16[8,144,512]{2,1,0:T(8,128)(2,1)}, bf16[8,144,512]{2,1,0:T(8,128)(2,1)}, u32[]{:S(2)}, u32[]{:S(2)}) collective-permute-start(bf16[8,144,512]{2,1,0:T(8,128)(2,1)} %constant_dynamic-update-slice_fusion.5.refs_0_), channel_id=1, source_target_pairs={{0,1},{1,0},{2,3},{3,2},{4,5},{5,4},{6,7},{7,6},{8,9},{9,8},{10,11... | collective-permute-start | bytes 3538952 | tf_op jit(solution)/shard_map/ppermute | solution.py:34
  143.5 49.9 %collective-permute-start.24 = (bf16[208,1728]{1,0:T(8,128)(2,1)}, bf16[208,1728]{1,0:T(8,128)(2,1)}, u32[]{:S(2)}, u32[]{:S(2)}) collective-permute-start(bf16[208,1728]{1,0:T(8,128)(2,1)} %copy-done.123), channel_id=1, source_target_pairs={{0,4},{8,0},{16,8},{24,16},{28,24},{20,28},{12,20},{4,12},{1,5},{9... | collective-permute-start | bytes 2156552 | tf_op jit(solution)/shard_map/ppermute | solution.py:57
  144.8 36.9 %collective-permute-start.21 = (bf16[224,1728]{1,0:T(8,128)(2,1)}, bf16[224,1728]{1,0:T(8,128)(2,1)}, u32[]{:S(2)}, u32[]{:S(2)}) collective-permute-start(bf16[224,1728]{1,0:T(8,128)(2,1)} %copy-done.121), channel_id=1, source_target_pairs={{0,8},{8,16},{16,24},{24,28},{28,20},{20,12},{12,4},{4,0},{1,9},{9... | collective-permute-start | bytes 2322440 | tf_op jit(solution)/shard_map/ppermute | solution.py:57
  181.8 31.9 %collective-permute-start.22 = (bf16[224,1728]{1,0:T(8,128)(2,1)}, bf16[224,1728]{1,0:T(8,128)(2,1)}, u32[]{:S(2)}, u32[]{:S(2)}) collective-permute-start(bf16[224,1728]{1,0:T(8,128)(2,1)} %collective-permute-done.21.refs_4_), channel_id=1, source_target_pairs={{0,8},{8,16},{16,24},{24,28},{28,20},{20,12},{12,4},{4,0},{1,9},{9... | collective-permute-start | bytes 2322440 | tf_op jit(solution)/shard_map/ppermute | solution.py:57
  265.7 30.4 %collective-permute-start.32 = (bf16[512,1152]{1,0:T(8,128)(2,1)S(1)}, bf16[512,1152]{1,0:T(8,128)(2,1)}, u32[]{:S(2)}, u32[]{:S(2)}) collective-permute-start(bf16[512,1152]{1,0:T(8,128)(2,1)S(1)} %multiply_convert_fusion.first_ref.refs_0_), channel_id=1, source_target_pairs={{0,2},{1,3},{2,0},{3,1},{4,6},{5,7},{6,4},{7,5},{8,10},{9,11},{10,... | collective-permute-start | bytes 3538952 | tf_op jit(solution)/shard_map/ppermute | solution.py:38
  368.5 32.9 %collective-permute-start.38 = (bf16[512,1152]{1,0:T(8,128)(2,1)}, bf16[512,1152]{1,0:T(8,128)(2,1)}, u32[]{:S(2)}, u32[]{:S(2)}) collective-permute-start(bf16[512,1152]{1,0:T(8,128)(2,1)} %get-tuple-element.133.first_ref.refs_0_), channel_id=1, source_target_pairs={{0,2},{1,3},{2,0},{3,1},{4,6},{5,7},{6,4},{7,5},{8,10},{9,11},{10,... | collective-permute-start | bytes 3538952 | tf_op jit(solution)/shard_map/ppermute | solution.py:38
  434.9 52.2 %collective-permute-start.37 = (bf16[512,1152]{1,0:T(8,128)(2,1)}, bf16[512,1152]{1,0:T(8,128)(2,1)S(1)}, u32[]{:S(2)}, u32[]{:S(2)}) collective-permute-start(bf16[512,1152]{1,0:T(8,128)(2,1)} %get-tuple-element.119), channel_id=1, source_target_pairs={{0,1},{1,0},{2,3},{3,2},{4,5},{5,4},{6,7},{7,6},{8,9},{9,8},{10,11... | collective-permute-start | bytes 3538952 | tf_op jit(solution)/shard_map/ppermute | solution.py:34
  440.4 47.8 %collective-permute-start.41 = (bf16[512,1152]{1,0:T(8,128)(2,1)}, bf16[512,1152]{1,0:T(8,128)(2,1)}, u32[]{:S(2)}, u32[]{:S(2)}) collective-permute-start(bf16[512,1152]{1,0:T(8,128)(2,1)} %add_convert_fusion.1), channel_id=1, source_target_pairs={{0,2},{1,3},{2,0},{3,1},{4,6},{5,7},{6,4},{7,5},{8,10},{9,11},{10,... | collective-permute-start | bytes 3538952 | tf_op jit(solution)/shard_map/ppermute | solution.py:38
  507.1 35.3 %collective-permute-start.45 = (bf16[208,1728]{1,0:T(8,128)(2,1)}, bf16[208,1728]{1,0:T(8,128)(2,1)S(1)}, u32[]{:S(2)}, u32[]{:S(2)}) collective-permute-start(bf16[208,1728]{1,0:T(8,128)(2,1)} %get-tuple-element.139.refs_3_), channel_id=1, source_target_pairs={{0,8},{8,16},{16,24},{24,28},{28,20},{20,12},{12,4},{4,0},{1,9},{9... | collective-permute-start | bytes 2156552 | tf_op jit(solution)/shard_map/ppermute | solution.py:57
  508.1 34.3 %collective-permute-start.44 = (bf16[224,1728]{1,0:T(8,128)(2,1)}, bf16[224,1728]{1,0:T(8,128)(2,1)S(1)}, u32[]{:S(2)}, u32[]{:S(2)}) collective-permute-start(bf16[224,1728]{1,0:T(8,128)(2,1)} %get-tuple-element.138.refs_2_), channel_id=1, source_target_pairs={{0,4},{8,0},{16,8},{24,16},{28,24},{20,28},{12,20},{4,12},{1,5},{9... | collective-permute-start | bytes 2322440 | tf_op jit(solution)/shard_map/ppermute | solution.py:57
  563.3 55.3 %collective-permute-start.55 = (bf16[1152,512]{0,1:T(8,128)(2,1)}, bf16[1152,512]{0,1:T(8,128)(2,1)}, u32[]{:S(2)}, u32[]{:S(2)}) collective-permute-start(bf16[1152,512]{0,1:T(8,128)(2,1)} %pad_maximum_fusion), channel_id=1, source_target_pairs={{0,1},{1,0},{2,3},{3,2},{4,5},{5,4},{6,7},{7,6},{8,9},{9,8},{10,11... | collective-permute-start | bytes 3538952 | tf_op jit(solution)/shard_map/ppermute | solution.py:34
  566.3 52.2 %collective-permute-start.57 = (bf16[1152,512]{0,1:T(8,128)(2,1)}, bf16[1152,512]{0,1:T(8,128)(2,1)}, u32[]{:S(2)}, u32[]{:S(2)}) collective-permute-start(bf16[1152,512]{0,1:T(8,128)(2,1)} %fusion.4), channel_id=1, source_target_pairs={{0,2},{1,3},{2,0},{3,1},{4,6},{5,7},{6,4},{7,5},{8,10},{9,11},{10,... | collective-permute-start | bytes 3538952 | tf_op jit(solution)/shard_map/ppermute | solution.py:38
  573.8 39.1 %collective-permute-start.47 = (bf16[224,1728]{1,0:T(8,128)(2,1)}, bf16[224,1728]{1,0:T(8,128)(2,1)}, u32[]{:S(2)}, u32[]{:S(2)}) collective-permute-start(bf16[224,1728]{1,0:T(8,128)(2,1)} %get-tuple-element.144), channel_id=1, source_target_pairs={{0,4},{8,0},{16,8},{24,16},{28,24},{20,28},{12,20},{4,12},{1,5},{9... | collective-permute-start | bytes 2322440 | tf_op jit(solution)/shard_map/ppermute | solution.py:57
  574.1 34.6 %collective-permute-start.48 = (bf16[208,1728]{1,0:T(8,128)(2,1)}, bf16[208,1728]{1,0:T(8,128)(2,1)}, u32[]{:S(2)}, u32[]{:S(2)}) collective-permute-start(bf16[208,1728]{1,0:T(8,128)(2,1)} %get-tuple-element.145), channel_id=1, source_target_pairs={{0,8},{8,16},{16,24},{24,28},{28,20},{20,12},{12,4},{4,0},{1,9},{9... | collective-permute-start | bytes 2156552 | tf_op jit(solution)/shard_map/ppermute | solution.py:57
  626.8 33.3 %collective-permute-start.58 = (bf16[4,144,512]{2,1,0:T(8,128)(2,1)S(1)}, bf16[4,144,512]{2,1,0:T(8,128)(2,1)}, u32[]{:S(2)}, u32[]{:S(2)}) collective-permute-start(bf16[4,144,512]{2,1,0:T(8,128)(2,1)S(1)} %fusion.10), channel_id=1, source_target_pairs={{0,4},{4,0},{8,12},{12,8},{16,20},{20,16},{24,28},{28,24},{1,5},{5... | collective-permute-start | bytes 1769480 | tf_op jit(solution)/shard_map/ppermute | solution.py:43
  646.0 33.1 %collective-permute-start.51 = (bf16[224,1728]{1,0:T(8,128)(2,1)}, bf16[224,1728]{1,0:T(8,128)(2,1)}, u32[]{:S(2)}, u32[]{:S(2)}) collective-permute-start(bf16[224,1728]{1,0:T(8,128)(2,1)} %get-tuple-element.148), channel_id=1, source_target_pairs={{0,4},{8,0},{16,8},{24,16},{28,24},{20,28},{12,20},{4,12},{1,5},{9... | collective-permute-start | bytes 2322440 | tf_op jit(solution)/shard_map/ppermute | solution.py:57
  720.4 29.2 %collective-permute-start.75 = (bf16[224,1728]{1,0:T(8,128)(2,1)}, bf16[224,1728]{1,0:T(8,128)(2,1)S(1)}, u32[]{:S(2)}, u32[]{:S(2)}) collective-permute-start(bf16[224,1728]{1,0:T(8,128)(2,1)} %get-tuple-element.169), channel_id=1, source_target_pairs={{0,4},{8,0},{16,8},{24,16},{28,24},{20,28},{12,20},{4,12},{1,5},{9... | collective-permute-start | bytes 2322440 | tf_op jit(solution)/shard_map/ppermute | solution.py:57
  (180 other events, 2476.4 us)
Sparse Core Ops, SparseCore 0:
  109.1 100.1 all-gather.2
  552.0 119.7 reduce-scatter.1
